TPU v7x, 32 devices: a whole 2x2x4 slice. The times are simulated.
32 devices in a mesh: tm: 8 (over y, x, core), chan: 4 (over z).
Axes of the slice: x: 2, y: 2, z: 4, core: 2. Of those that a mesh axis runs over, the one named last changes fastest.
Arguments:
- latents: bfloat16 [512, 32, 512], P('chan', 'tm'), may hold values from -6 to 6
- conv_weight: bfloat16 [512, 3, 9, 512], P(None, None, None, 'chan'), may hold values from -0.0546875 to 0.0546875
- norm_gain: float32 [512], P('chan'), may hold values from 0.1 to 1.9
- norm_bias: float32 [512], P('chan'), may hold values from -3 to 3
- clip_lengths: int32 [12], replicated, may hold values from 1 to 8, 32 in all
- slab_bounds: int32 [8, 2], P('tm'), may hold values from 0 to 32, as said below
Outputs:
- decoded: bfloat16 [512, 64, 512], P('chan', 'tm')
Inputs may be any that keep to these rules, and one draw needn't show every extreme that they name: `clip_lengths`: the clips lie end to end and cover all 32 frames; the longest clip has exactly a quarter of 32 frames. `slab_bounds`: slab 0 starts at frame 0, the last slab ends at 32, each slab ends where the next starts, slab s starts within 2 frames of s * 4, so a slab holds 0 to 8 frames; some slab holds exactly 8 frames.
All inputs are finite; a program needn't handle non-finite values.
Results may differ from a plain program's by a relative error of at most 0.001.
Values may be sent and summed in bfloat16 or wider, within the bound.
No kernel may reach another device: no remote copies, remote signals or barrier semaphores. Data moves between devices by JAX's collectives and lax.ppermute only.
A program may use at most 128 MiB of HBM per device.

v0:
```python
import jax
import jax.numpy as jnp
from jax import lax
from jax.sharding import PartitionSpec as P

C = 512
GROUPS = 32
H = 16
W = 32


norm_eps = 1e-06


def padded_2(block, sides, width):
    for axis, dim in sides:
        count = lax.axis_size(axis)
        forward = [(i, i + 1) for i in range(count - 1)]
        backward = [(target, source) for source, target in forward]
        low = lax.ppermute(
            lax.slice_in_dim(block, block.shape[dim] - width, None, axis=dim), axis, forward
        )
        high = lax.ppermute(lax.slice_in_dim(block, 0, width, axis=dim), axis, backward)
        block = jnp.concatenate([low, block, high], axis=dim)
    return block


def frame_starts(clip_lengths, frames):
    clip_ends = jnp.cumsum(clip_lengths)
    starts = clip_ends - clip_lengths
    chosen = jnp.where(starts[None, :] <= frames[:, None], starts[None, :], 0)
    return jnp.max(chosen, axis=1)


def tap_sources(frames, clip_lengths):
    clip_first = frame_starts(clip_lengths, frames)
    return jnp.stack([jnp.maximum(frames - 2 + offset, clip_first) for offset in range(3)])


def columns(extended, local_index):
    channels = extended.shape[0]
    frame_count = local_index.shape[0]
    picked = jnp.take(extended, local_index, axis=1).reshape(channels, frame_count, H, W)
    padded = jnp.pad(picked, ((0, 0), (0, 0), (1, 1), (1, 1)))
    pieces = [
        padded[:, :, row_tap : row_tap + H, col_tap : col_tap + W]
        for row_tap in range(3)
        for col_tap in range(3)
    ]
    return jnp.stack(pieces).reshape(9 * channels, frame_count * H * W)


def norm_block(summed, residual, norm_gain, norm_bias):
    channels, frame_count, cell_count = summed.shape
    group_width = C // GROUPS
    grouped = summed.reshape(channels // group_width, group_width, frame_count, cell_count)
    average = jnp.mean(grouped, axis=(1, 3), keepdims=True)
    variance = jnp.mean(jnp.square(grouped - average), axis=(1, 3), keepdims=True)
    normed = ((grouped - average) * lax.rsqrt(variance + norm_eps)).reshape(
        channels, frame_count, cell_count
    )
    normed = normed * norm_gain[:, None, None] + norm_bias[:, None, None]
    return (jax.nn.silu(normed) + residual.astype(jnp.float32)).astype(jnp.bfloat16)


def shards(latents, conv_weight, norm_gain, norm_bias, clip_lengths, slab_bounds):
    channels, frame_count, cell_count = latents.shape
    out_channels = conv_weight.shape[0]
    own_rows = out_channels // lax.axis_size("chan")
    capacity = 2 * frame_count
    slab_index = lax.axis_index("tm")
    slab_first = slab_bounds[0, 0]
    slab_end = slab_bounds[0, 1]
    slot_index = jnp.arange(capacity, dtype=jnp.int32)
    occupied = slot_index < slab_end - slab_first
    wanted = jnp.where(occupied, slab_first + slot_index, slab_first)
    weights = [conv_weight[:, offset].reshape(out_channels, 9 * channels) for offset in range(3)]
    extended = padded_2(latents, (("tm", 1),), frame_count)
    anchor = (slab_index - 1) * frame_count
    sources = tap_sources(wanted, clip_lengths) - anchor
    stacks = [columns(extended, sources[offset]) for offset in range(3)]
    summed = jnp.zeros((own_rows * lax.axis_size("chan"), stacks[0].shape[1]), jnp.float32)
    for offset in range(3):
        weight_rows = weights[offset]
        summed = summed + jnp.dot(weight_rows, stacks[offset], preferred_element_type=jnp.float32)
    partial_total = lax.psum_scatter(summed, "chan", scatter_dimension=0, tiled=True)
    residual = jnp.take(extended, wanted - anchor, axis=1)
    decoded = norm_block(
        partial_total.reshape(own_rows, wanted.shape[0], cell_count), residual, norm_gain, norm_bias
    )
    return jnp.where(occupied[None, :, None], decoded, jnp.zeros_like(decoded))


def solution(mesh):
    placed = (
        P("chan", "tm", None),
        P(None, None, None, "chan"),
        P("chan"),
        P("chan"),
        P(),
        P("tm", None),
    )
    return jax.shard_map(
        shards, mesh=mesh, in_specs=placed, out_specs=P("chan", "tm", None), check_vma=False
    )
```

profile of v0, /device:TPU:3, one launch (start us, length us, event | category | flops | bytes accessed | tf_op | source)
XLA Modules:
  0.0 290.1 jit_solution(5438502585984151004)
XLA Ops:
  6.5 1.9 copy.30
  8.5 3.7 %collective-permute-start = (bf16[128,4,512]{2,0,1:T(8,128)(2,1)}, bf16[128,4,512]{2,0,1:T(8,128)(2,1)}, u32[]{:S(2)}, u32[]{:S(2)}) collective-permute-start(bf16[128,4,512]{2,0,1:T(8,128)(2,1)} %copy.30), channel_id=1, source_target_pairs={{0,4},{4,8},{8,12},{12,16},{16,20},{20,24},{24,28},{1,5},{5,9},{9,... | collective-permute-start | bytes 1572872 | tf_op jit(solution)/shard_map/ppermute | solution.py:20
  12.1 1.9 collective-permute-start.1
  14.1 1.3 fusion.62
  18.2 1.3 compare_and_fusion
  20.9 2.2 fusion.61
  23.1 1.4 copy.52
  24.6 1.4 copy.51
  26.0 1.5 copy.50
  33.3 1.6 copy.41
  38.3 11.4 %copy.43 = bf16[9,128,8,16,32]{1,0,4,3,2:T(8,128)(2,1)} copy(bf16[9,128,8,16,32]{1,4,3,2,0:T(8,128)(2,1)S(1)} %fusion.60) | data formatting | bytes 18874368 | tf_op jit(solution)/shard_map/stack | solution.py:50
  51.5 1.6 copy.37
  56.5 11.4 %copy.39 = bf16[9,128,8,16,32]{1,0,4,3,2:T(8,128)(2,1)} copy(bf16[9,128,8,16,32]{1,4,3,2,0:T(8,128)(2,1)S(1)} %fusion.44) | data formatting | bytes 18874368 | tf_op jit(solution)/shard_map/stack | solution.py:50
  69.7 1.8 copy.33
  75.0 11.4 %copy.35 = bf16[9,128,8,16,32]{1,0,4,3,2:T(8,128)(2,1)} copy(bf16[9,128,8,16,32]{1,4,3,2,0:T(8,128)(2,1)S(1)} %fusion.28) | data formatting | bytes 18874368 | tf_op jit(solution)/shard_map/stack | solution.py:50
  86.4 8.1 %fusion = f32[4096,512]{1,0:T(8,128)} fusion(bf16[512,1152]{0,1:T(8,128)(2,1)S(1)} %bitcast.215, bf16[512,8,9,128]{3,2,1,0:T(8,128)(2,1)S(1)} %bitcast.208), kind=kOutput, calls=%fused_computation.4 | convolution fusion | flops 4831838208 | bytes 19005440 | tf_op jit(solution)/shard_map/dot_general | solution.py:85
  94.5 14.0 %fusion.3 = f32[4096,512]{1,0:T(8,128)} fusion(bf16[512,1152]{0,1:T(8,128)(2,1)S(1)} %bitcast.213, bf16[512,8,9,128]{3,2,1,0:T(8,128)(2,1)} %bitcast.209), kind=kOutput, calls=%fused_computation.7 | convolution fusion | flops 4831838208 | bytes 19005440 | tf_op jit(solution)/shard_map/dot_general | solution.py:85
  108.5 17.1 %add_bitcast_fusion = f32[512,4096]{0,1:T(8,128)} fusion(f32[4096,512]{1,0:T(8,128)} %fusion, f32[4096,512]{1,0:T(8,128)} %fusion.3, bf16[512,1152]{0,1:T(8,128)(2,1)S(1)} %bitcast.214, bf16[512,8,9,128]{3,2,1,0:T(8,128)(2,1)} %bitcast.210), kind=kOutput, calls=%fused_computation.13 | convolution fusion | flops 4836032512 | bytes 35782656 | tf_op jit(solution)/shard_map/dot_general | solution.py:85
  125.7 1.6 gather_fusion.3
  127.3 144.0 %reduce-scatter.2.cloned.1.call-done = f32[128,4096]{0,1:T(8,128)} async-done(((f32[512,4096]{0,1:T(8,128)}), f32[128,4096]{0,1:T(8,128)}) %reduce-scatter.2.cloned.1.call-update) | async-done | bytes 2097168 | tf_op jit(solution)/shard_map/reduce_scatter | solution.py:86
  271.3 2.9 copy.45
  274.2 3.2 %copy.56 = f32[16,8,8,512]{3,2,1,0:T(8,128)S(1)} copy(f32[16,8,8,512]{3,1,2,0:T(8,128)} %bitcast.212) | data formatting | bytes 4194304
  278.4 1.9 copy.47
  281.7 1.5 copy.49
  (86 shorter events, 24.7 us)
Async XLA Ops:
  6.5 264.8 %reduce-scatter.2.cloned.1.call-start = ((), (), s32[]{:S(2)}) async-start(), calls=%async_computation.1 | async-start | bytes 10485760 | tf_op jit(solution)/shard_map/reduce_scatter | solution.py:86
  8.5 19.7 %collective-permute-start = (bf16[128,4,512]{2,0,1:T(8,128)(2,1)}, bf16[128,4,512]{2,0,1:T(8,128)(2,1)}, u32[]{:S(2)}, u32[]{:S(2)}) collective-permute-start(bf16[128,4,512]{2,0,1:T(8,128)(2,1)} %copy.30), channel_id=1, source_target_pairs={{0,4},{4,8},{8,12},{12,16},{16,20},{20,24},{24,28},{1,5},{5,9},{9,... | collective-permute-start | bytes 1572872 | tf_op jit(solution)/shard_map/ppermute | solution.py:20
  12.1 18.3 %collective-permute-start.1 = (bf16[128,4,512]{2,0,1:T(8,128)(2,1)}, bf16[128,4,512]{2,0,1:T(8,128)(2,1)}, u32[]{:S(2)}, u32[]{:S(2)}) collective-permute-start(bf16[128,4,512]{2,0,1:T(8,128)(2,1)} %copy.30), channel_id=1, source_target_pairs={{4,0},{8,4},{12,8},{16,12},{20,16},{24,20},{28,24},{5,1},{9,5},{13... | collective-permute-start | bytes 1572872 | tf_op jit(solution)/shard_map/ppermute | solution.py:23
  74.2 12.1 %slice-start = ((s8[16777216]{0:T(1024)(128)(4,1)}), s8[4194304]{0:T(1024)(128)(4,1)S(1)}, s32[]{:S(2)}) async-start(s8[16777216]{0:T(1024)(128)(4,1)} %bitcast.206), calls=%async_computation.2 | async-start | bytes 8388608
  74.9 11.4 %slice-start.1 = ((s8[16777216]{0:T(1024)(128)(4,1)}), s8[4194304]{0:T(1024)(128)(4,1)S(1)}, s32[]{:S(2)}) async-start(s8[16777216]{0:T(1024)(128)(4,1)} %bitcast.206), calls=%async_computation.3 | async-start | bytes 8388608
  74.9 11.4 %slice-start.2 = ((s8[16777216]{0:T(1024)(128)(4,1)}), s8[4194304]{0:T(1024)(128)(4,1)S(1)}, s32[]{:S(2)}) async-start(s8[16777216]{0:T(1024)(128)(4,1)} %bitcast.206), calls=%async_computation.4 | async-start | bytes 8388608
  74.9 11.4 %slice-start.3 = ((s8[16777216]{0:T(1024)(128)(4,1)}), s8[4194304]{0:T(1024)(128)(4,1)S(1)}, s32[]{:S(2)}) async-start(s8[16777216]{0:T(1024)(128)(4,1)} %bitcast.206), calls=%async_computation.5 | async-start | bytes 8388608
  75.0 11.4 %copy-start.3 = (bf16[512,1,9,128]{0,3,2,1:T(8,128)(2,1)S(1)}, bf16[512,1,9,128]{0,3,2,1:T(8,128)(2,1)}, u32[]{:S(2)}) copy-start(bf16[512,1,9,128]{0,3,2,1:T(8,128)(2,1)} %copy.52) | copy-start | bytes 3538948
  86.4 8.1 %copy-start.1 = (bf16[512,1,9,128]{0,3,2,1:T(8,128)(2,1)S(1)}, bf16[512,1,9,128]{0,3,2,1:T(8,128)(2,1)}, u32[]{:S(2)}) copy-start(bf16[512,1,9,128]{0,3,2,1:T(8,128)(2,1)} %copy.51) | copy-start | bytes 3538948
  94.5 14.0 %copy-start.2 = (bf16[512,1,9,128]{0,3,2,1:T(8,128)(2,1)S(1)}, bf16[512,1,9,128]{0,3,2,1:T(8,128)(2,1)}, u32[]{:S(2)}) copy-start(bf16[512,1,9,128]{0,3,2,1:T(8,128)(2,1)} %copy.50) | copy-start | bytes 3538948
  108.5 17.2 %copy-start.4 = (s32[8]{0:T(128)S(1)}, s32[8]{0:T(128)}, u32[]{:S(2)}) copy-start(s32[8]{0:T(128)} %get-tuple-element.13) | copy-start | bytes 100
  125.7 154.8 %copy-start.5 = (pred[8]{0:T(512)(128)(4,1)S(1)}, pred[8]{0:T(512)(128)(4,1)}, u32[]{:S(2)}) copy-start(pred[8]{0:T(512)(128)(4,1)} %get-tuple-element.12) | copy-start | bytes 28
  125.7 154.8 %copy-start.6 = (f32[128]{0:T(128)S(1)}, f32[128]{0:T(128)}, u32[]{:S(2)}) copy-start(f32[128]{0:T(128)} %param.11) | copy-start | bytes 1540
  125.7 154.8 %copy-start.7 = (f32[128]{0:T(128)S(1)}, f32[128]{0:T(128)}, u32[]{:S(2)}) copy-start(f32[128]{0:T(128)} %param.10) | copy-start | bytes 1540
  127.3 153.2 %copy-start = (bf16[8,128,512]{2,1,0:T(8,128)(2,1)S(1)}, bf16[8,128,512]{2,1,0:T(8,128)(2,1)}, u32[]{:S(2)}) copy-start(bf16[8,128,512]{2,1,0:T(8,128)(2,1)} %gather_fusion.3) | copy-start | bytes 3145732
Sparse Core Ops, SparseCore 0:
  125.8 145.4 reduce-scatter.1
where the time goes:
time: 292 us; the launch traced here: 290 us
  waiting for transfers between devices  144 us (49%)
  local copies, waits for them, and re-layouts  75.9 us (26%)
  matrix products  39.2 us (13%)
  between operations  15.2 us (5%)
  other arithmetic  10.1 us (3%)
  starting transfers between devices  5.59 us (2%)
    reduce_scatter x1, waiting for transfers between devices, shards(): lax.psum_scatter(summed, 'chan', scatter_dimension=0, tiled=True)  144 us
    dot_general x3, matrix products, shards(): jnp.dot(weight_rows, stacks[offset], preferred_element_type=jnp.float32)  39.2 us
    another operation x6, local copies, waits for them, and re-layouts, columns(): return jnp.stack(pieces).reshape(9 * channels, frame_count * H * W)  35.6 us
    unnamed x55, local copies, waits for them, and re-layouts  20.4 us
  transfers between devices with their start and end apart: 3, of which 1 were waited for; matrix products, arithmetic and copies ran while one was open for 6% of the time, Pallas kernels for 0%

commit v1 on v0

v1 whole, which is shorter than its diff:
```python
import functools

import jax
import jax.numpy as jnp
from jax import lax
from jax.experimental import pallas as pl
from jax.experimental.pallas import tpu as pltpu
from jax.sharding import PartitionSpec as P

C = 512
GROUPS = 32
H = 16
W = 32
CELLS = H * W
GROUP_WIDTH = C // GROUPS
PIECES = 8
TAPS = 27
LANES = 128
VMEM_BYTES = 9 * 1024 * 1024

norm_eps = 1e-06


def clip_start(clip_ref, g):
    first = jnp.int32(0)
    running = jnp.int32(0)
    for c in range(clip_ref.shape[0]):
        first = jnp.where(running <= g, jnp.maximum(first, running), first)
        running = running + clip_ref[c]
    return first


def group_sum(grouped):
    tiles = [grouped[:, :, i : i + LANES] for i in range(0, CELLS, LANES)]
    while len(tiles) > 1:
        tiles = [x + y for x, y in zip(tiles[::2], tiles[1::2])]
    folded = tiles[0][:, :8] + tiles[0][:, 8:]
    return jnp.sum(jnp.sum(folded, axis=1, keepdims=True), axis=2, keepdims=True)


def group_norm(total, gain, bias):
    own = total.shape[0]
    grouped = total.reshape(own // GROUP_WIDTH, GROUP_WIDTH, CELLS)
    scale = 1.0 / (GROUP_WIDTH * CELLS)
    centred = grouped - group_sum(grouped) * scale
    variance = group_sum(centred * centred) * scale
    normed = (centred * lax.rsqrt(variance + norm_eps)).reshape(own, CELLS)
    return normed * gain + bias


def as_column(row):
    count = row.shape[1]
    return jnp.transpose(jnp.broadcast_to(row, (count, count)))[:, :1]


def finished(total, gain, bias, residual):
    normed = group_norm(total, gain, bias)
    activated = normed / (1.0 + jnp.exp(-normed))
    return (activated + residual.astype(jnp.float32)).astype(jnp.bfloat16)


def conv_kernel(parts, halo, slots_of, groups, added, finish, ordered, *refs):
    refs = list(refs)
    clip_ref = refs.pop(0)
    frame_refs = [refs.pop(0) for _ in range(parts)]
    halo_ref = refs.pop(0) if halo else None
    weight_refs = [refs.pop(0) for _ in range(1 if slots_of is None else PIECES)]
    sum_refs = [[refs.pop(0) for _ in range(count)] for count in added]
    if finish:
        residual_ref = refs.pop(0)
        gain, bias = [as_column(refs.pop(0)[...]) for _ in range(2)]
    out_refs = [refs.pop(0) for _ in groups]
    shifted_ref = refs.pop(0)
    total_ref = refs.pop(0) if finish else None
    frame_count, shard, _ = frame_refs[0].shape
    half, own, _ = out_refs[0].shape
    piece_rows = own // PIECES
    slab = lax.axis_index("tm")
    place = slab % PIECES
    first_frame = slab * frame_count

    def piece_start(i):
        return pl.multiple_of(jnp.bitwise_xor(place, i) * piece_rows, piece_rows)

    cell = lax.broadcasted_iota(jnp.int32, (1, CELLS), 1)
    column = cell % W
    for p in range(parts):
        needed = list(range(frame_count + (2 if halo else 0)))
        if groups == ("next",):
            needed = needed[half:]
        if groups == ("head",):
            needed = needed[:half] + needed[frame_count:]
        for f in needed:
            frame = frame_refs[p][f] if f < frame_count else halo_ref[f - frame_count]
            zero = jnp.zeros_like(frame)
            shifted_ref[p, f, 0:shard, :] = jnp.where(column > 0, pltpu.roll(frame, 1, 1), zero)
            shifted_ref[p, f, shard : 2 * shard, :] = frame
            shifted_ref[p, f, 2 * shard :, :] = jnp.where(
                column < W - 1, pltpu.roll(frame, CELLS - 1, 1), zero
            )
        if not halo:
            shifted_ref[p, frame_count] = jnp.zeros_like(shifted_ref[p, frame_count])

    def weight_rows(p, i):
        if slots_of is None:
            return weight_refs[0][:, pl.ds(piece_start(i), piece_rows), :]
        return weight_refs[i][slots_of[p]]

    def convolved(j, time_taps):
        g = first_frame + j
        first = clip_start(clip_ref, g)
        inputs = []
        for p in range(parts):
            for k in time_taps:
                source = jnp.maximum(g - 2 + k, first) - first_frame
                if halo:
                    source = jnp.where(source < 0, source + frame_count + 2, source)
                else:
                    source = jnp.where(source < 0, frame_count, jnp.minimum(source, frame_count))
                inputs.append(shifted_ref[p, source])
        pieces = [[weight_rows(p, i) for i in range(PIECES)] for p in range(parts)]
        weights = []
        for a in range(3):
            for block in range(PIECES):
                row = [
                    pieces[p][block][9 * k + 3 * a + b]
                    for p in range(parts)
                    for k in time_taps
                    for b in range(3)
                ]
                weights.append(jnp.concatenate(row, axis=1))
        product = jnp.dot(
            jnp.concatenate(weights, axis=0),
            jnp.concatenate(inputs, axis=0),
            preferred_element_type=jnp.float32,
        )
        up = pltpu.roll(product[:own], W, 1)
        down = pltpu.roll(product[2 * own :], CELLS - W, 1)
        return (
            jnp.where(cell >= W, up, 0.0)
            + product[own : 2 * own]
            + jnp.where(cell < CELLS - W, down, 0.0)
        )

    def store_in_order(ref, total):
        for block in range(PIECES):
            ref[pl.ds(piece_start(block), piece_rows), :] = total[
                block * piece_rows : (block + 1) * piece_rows
            ]

    for group, out_ref, earlier in zip(groups, out_refs, sum_refs):
        if group == "next":
            for i, time_taps in enumerate(((0, 1), (0,))):
                total = convolved(frame_count + i, time_taps)
                for sum_ref in earlier:
                    total = total + sum_ref[i]
                if group in ordered:
                    store_in_order(out_ref.at[i], total)
                else:
                    out_ref[i] = total
            continue

        def one_frame(i, carry, group=group, out_ref=out_ref, earlier=earlier):
            j = i if group == "head" else i + half
            total = convolved(j, (0, 1, 2))
            for sum_ref in earlier[:1]:
                total = total + sum_ref[i]
            if group in finish:
                store_in_order(total_ref, total)
                total = total_ref[...]
                for sum_ref in earlier[1:]:
                    total = total + sum_ref[i]
                out_ref[i] = finished(total, gain, bias, residual_ref[j])
            else:
                out_ref[i] = total
            return carry

        lax.fori_loop(0, half, one_frame, 0)


def conv_parts(clip_lengths, shards_in, halo, weights, slots_of, groups, added, params, finish, ordered):
    frame_count, shard, cells = shards_in[0].shape
    own, half, parts = shard, frame_count // 2, len(shards_in)
    vectors = pl.BlockSpec(memory_space=pltpu.VMEM)
    operands = [clip_lengths, *shards_in]
    if halo is not None:
        operands.append(halo)
    operands += list(weights)
    for sums in added:
        operands += list(sums)
    if finish:
        operands += list(params)
    frames = frame_count + (1 if halo is None else 2)
    scratch = [pltpu.VMEM((parts, frames, 3 * shard, cells), jnp.bfloat16)]
    if finish:
        scratch.append(pltpu.VMEM((own, cells), jnp.float32))
    kernel = functools.partial(
        conv_kernel,
        parts,
        halo is not None,
        slots_of,
        groups,
        [len(sums) for sums in added],
        finish,
        ordered,
    )
    return pl.pallas_call(
        kernel,
        out_shape=[
            jax.ShapeDtypeStruct(
                (half, own, cells), jnp.bfloat16 if group in finish else jnp.float32
            )
            for group in groups
        ],
        in_specs=[pl.BlockSpec(memory_space=pltpu.SMEM)] + [vectors] * (len(operands) - 1),
        out_specs=[vectors] * len(groups),
        scratch_shapes=scratch,
        compiler_params=pltpu.CompilerParams(vmem_limit_bytes=VMEM_BYTES),
        cost_estimate=pl.CostEstimate(
            flops=2500000000 if groups == ("tail",) else 1024,
            bytes_accessed=1024,
            transcendentals=0,
        ),
        name="conv_parts",
    )(*operands)


def slots_kernel(bounds_ref, before_ref, head_ref, tail_ref, after_ref, out_ref, slot_ref):
    half, channels, _ = head_ref.shape
    capacity = out_ref.shape[1]
    offset = bounds_ref[0, 0] - (lax.axis_index("tm") * 2 * half - half)
    size = bounds_ref[0, 1] - bounds_ref[0, 0]
    for w in range(capacity):
        pair = (before_ref, head_ref, tail_ref, after_ref)[w // half]
        slot = w - offset

        @pl.when((slot >= 0) & (slot < size))
        def _():
            slot_ref[slot] = pair[w % half].astype(jnp.float32)

        @pl.when(w >= size)
        def _():
            slot_ref[w] = jnp.zeros_like(slot_ref[w])

    rows = 16
    for start in range(0, channels, rows):
        block = slot_ref[:, start : start + rows, :]
        out_ref[start : start + rows] = jnp.swapaxes(block, 0, 1).astype(jnp.bfloat16)


def slots(bounds, before, head, tail, after):
    half, channels, cells = head.shape
    capacity = 4 * half
    vectors = pl.BlockSpec(memory_space=pltpu.VMEM)
    return pl.pallas_call(
        slots_kernel,
        out_shape=jax.ShapeDtypeStruct((channels, capacity, cells), jnp.bfloat16),
        in_specs=[pl.BlockSpec(memory_space=pltpu.SMEM)] + [vectors] * 4,
        out_specs=vectors,
        scratch_shapes=[pltpu.VMEM((capacity, channels, cells), jnp.float32)],
        compiler_params=pltpu.CompilerParams(vmem_limit_bytes=VMEM_BYTES),
        name="slots",
    )(bounds, before, head, tail, after)


def xor_permute(array, axis, bits):
    return lax.ppermute(array, axis, [(i, i ^ bits) for i in range(lax.axis_size(axis))])


def weight_blocks(by_tap):
    _, out_channels, shard = by_tap.shape
    chan_count = lax.axis_size("chan")
    own = out_channels // chan_count
    piece_rows = own // PIECES
    piece = lax.axis_index("tm") % PIECES
    me = lax.axis_index("chan")
    pieces = [
        lax.dynamic_slice(
            by_tap,
            (0, jnp.bitwise_xor(me, s) * own + piece * piece_rows, 0),
            (TAPS, piece_rows, shard),
        )
        for s in range(1, chan_count)
    ]
    return lax.dynamic_slice(by_tap, (0, me * own, 0), (TAPS, own, shard)), pieces


def shards(latents, conv_weight, norm_gain, norm_bias, clip_lengths, slab_bounds):
    own, frame_count, cells = latents.shape
    out_channels, _, _, shard = conv_weight.shape
    tm_count = lax.axis_size("tm")
    forward = [(i, i + 1) for i in range(tm_count - 1)]
    backward = [(i + 1, i) for i in range(tm_count - 1)]

    by_tap = jnp.transpose(conv_weight, (1, 2, 0, 3)).reshape(TAPS, out_channels, shard)
    own_weights, blocks = weight_blocks(by_tap)
    blocks, latents = lax.optimization_barrier((blocks, latents))
    by_frame = jnp.transpose(latents, (1, 0, 2))
    swapped = [xor_permute(block, "chan", s) for s, block in enumerate(blocks, 1)]

    half = frame_count // 2

    def conv(shards_in, halo, given, slots_of, groups, added, params=(), finish=(), ordered=()):
        return conv_parts(
            clip_lengths, shards_in, halo, given, slots_of, groups, added, params, finish, ordered
        )

    swapped[0], by_frame = lax.optimization_barrier((swapped[0], by_frame))
    first = xor_permute(by_frame, "chan", 1)
    swapped, kept = lax.optimization_barrier((jnp.stack(swapped), by_frame))
    second = xor_permute(kept, "chan", 2)
    first, by_frame = lax.optimization_barrier((first, by_frame))
    totals = conv([by_frame], None, [own_weights], None, ("head", "tail", "next"), [[], [], []])
    same_core = [swapped] + [xor_permute(swapped, "tm", bits) for bits in range(2, PIECES, 2)]
    same_core, totals = lax.optimization_barrier((same_core, totals))
    head, tail, following = totals
    other_core = [xor_permute(piece, "tm", 1) for piece in same_core]
    weights = [piece for pair in zip(same_core, other_core) for piece in pair]
    third = xor_permute(second, "chan", 1)
    chan_count = lax.axis_size("chan")
    third_halo = lax.ppermute(
        second[half:],
        ("tm", "chan"),
        [
            (t * chan_count + (c ^ 1), (t + 1) * chan_count + c)
            for t in range(tm_count - 1)
            for c in range(chan_count)
        ],
    )
    pair, slots_of = [first, second], (0, 1)
    (following,) = conv(
        pair, None, weights, slots_of, ("next",), [[following]], ordered=("next",)
    )
    arrived = lax.ppermute(following, "tm", forward)
    both = ("head", "tail")
    head, tail = conv(pair, None, weights, slots_of, both, [[head], [tail]])
    params = (by_frame, norm_gain.reshape(1, own), norm_bias.reshape(1, own))
    (tail,) = conv([third], None, weights, (2,), ("tail",), [[tail]], params, ("tail",))
    before = lax.ppermute(tail, "tm", forward)
    arrived, tail = lax.optimization_barrier((arrived, tail))
    (head,) = conv(
        [third], third_halo, weights, (2,), ("head",), [[head, arrived]], params, ("head",)
    )
    after = lax.ppermute(head, "tm", backward)
    return slots(slab_bounds, before, head, tail, after)


def solution(mesh):
    placed = (
        P("chan", "tm", None),
        P(None, None, None, "chan"),
        P("chan"),
        P("chan"),
        P(),
        P("tm", None),
    )
    return jax.shard_map(
        shards, mesh=mesh, in_specs=placed, out_specs=P("chan", "tm", None), check_vma=False
    )
```

time: 292 us -> 75.7 us (0.26)
  waiting for transfers between devices: 144 us -> 23.7 us
  local copies, waits for them, and re-layouts: 75.9 us -> 3.45 us
  matrix products: 39.2 us -> 0 us
  Pallas kernels: 0 us -> 21.6 us
  starting transfers between devices: 5.59 us -> 26.4 us
  between operations: 15.2 us -> 0.21 us
  other arithmetic: 10.1 us -> 0.04 us
    reduce_scatter x1 -> x0, waiting for transfers between devices: 144 us -> none  [shards(): lax.psum_scatter(summed, 'chan', scatter_dimension=0, tiled=True)]
    dot_general x3 -> x0, matrix products: 39.2 us -> none  [shards(): jnp.dot(weight_rows, stacks[offset], preferred_element_type=jnp.float32)]
    another operation x7 -> x0, local copies, waits for them, and re-layouts: 37.6 us -> none  [the longest x6 35.6 us: columns(): return jnp.stack(pieces).reshape(9 * channels, frame_count * H * W)]
    ppermute x2 -> x17, waiting for transfers between devices: 0.01 us -> 23.7 us  [the longest x13 17 us: xor_permute(): lax.ppermute(array, axis, [(i, i ^ bits) for i in range(lax.axis_size(axi...]
    pallas_call x0 -> x6, Pallas kernels: none -> 21.6 us  [the longest x5 19.5 us: conv_parts(): pl.pallas_call(kernel, out_shape=[jax.ShapeDtypeStruct((half, own, cells)...]
    ppermute x2 -> x17, starting transfers between devices: 5.59 us -> 26.4 us  [the longest x13 13.1 us: xor_permute(): lax.ppermute(array, axis, [(i, i ^ bits) for i in range(lax.axis_size(axi...]
    unnamed x55 -> x8, local copies, waits for them, and re-layouts: 20.4 us -> 0.02 us
    select_n x4 -> x0, local copies, waits for them, and re-layouts: 6.56 us -> none  [the longest x3 5.01 us: columns(): jnp.take(extended, local_index, axis=1).reshape(channels, frame_count, H, W)]
  transfers between devices with their start and end apart: 3 -> 17, of which waited for: 1 -> 8; matrix products, arithmetic and copies ran while one was open for 6% -> 3% of each run, Pallas kernels for 0% -> 26%
where the time goes in v1:
time: 75.7 us; the launch traced here: 75.4 us
  starting transfers between devices  26.4 us (35%)
  waiting for transfers between devices  23.7 us (31%)
  Pallas kernels  21.6 us (29%)
  local copies, waits for them, and re-layouts  3.45 us (5%)
    pallas_call x5, Pallas kernels, conv_parts(): pl.pallas_call(kernel, out_shape=[jax.ShapeDtypeStruct((half, own, cells)...  19.5 us
    ppermute x13, waiting for transfers between devices, xor_permute(): lax.ppermute(array, axis, [(i, i ^ bits) for i in range(lax.axis_size(axi...  17 us
    ppermute x13, starting transfers between devices, xor_permute(): lax.ppermute(array, axis, [(i, i ^ bits) for i in range(lax.axis_size(axi...  13.1 us
    ppermute x1, waiting for transfers between devices, shards(): after = lax.ppermute(head, 'tm', backward)  6.65 us
    ppermute x1, starting transfers between devices, shards(): arrived = lax.ppermute(following, 'tm', forward)  4.37 us
    ppermute x1, starting transfers between devices, shards(): before = lax.ppermute(tail, 'tm', forward)  3.67 us
    ppermute x1, starting transfers between devices, shards(): lax.ppermute(second[half:], ('tm', 'chan'), [(t * chan_count + (c ^ 1), (...  3.37 us
    pallas_call x1, Pallas kernels, slots(): pl.pallas_call(slots_kernel, out_shape=jax.ShapeDtypeStruct((channels, ca...  2.11 us
  transfers between devices with their start and end apart: 17, of which 8 were waited for; matrix products, arithmetic and copies ran while one was open for 3% of the time, Pallas kernels for 26%

profile of v1, /device:TPU:3, one launch (start us, length us, event | category | flops | bytes accessed | tf_op | source)
XLA Modules:
  0.0 75.4 jit_solution(8975988686107630709)
XLA Ops:
  0.0 1.0 %constant_dynamic-slice_fusion.1 = (bf16[27,16,128]{2,1,0:T(8,128)(2,1)S(1)}, bf16[27,16,128]{2,1,0:T(8,128)(2,1)S(1)}, bf16[27,16,128]{2,1,0:T(8,128)(2,1)S(1)}) fusion(bf16[27,512,128]{2,1,0:T(8,128)(2,1)} %bitcast.20, s32[]{:T(128)S(6)} %select_n.22, s32[]{:T(128)S(6)} %select_n.21, s32[]{:T(128)S(6)} %select_n.20), kind=kLoop, calls=%fused_computation.3 | loop fusion | bytes 663564 | tf_op jit(solution)/shard_map/dynamic_slice | solution.py:278
  1.1 1.4 %collective-permute-start = (bf16[27,16,128]{2,1,0:T(8,128)(2,1)S(1)}, bf16[27,16,128]{2,1,0:T(8,128)(2,1)S(1)}, u32[]{:S(2)}, u32[]{:S(2)}) collective-permute-start(bf16[27,16,128]{2,1,0:T(8,128)(2,1)S(1)} %get-tuple-element.29), channel_id=1, source_target_pairs={{0,1},{1,0},{2,3},{3,2},{4,5},{5,4},{6,7},{7,6},{8,9},{9,8},{10,11... | collective-permute-start | bytes 331784 | tf_op jit(solution)/shard_map/ppermute | solution.py:267
  2.4 2.3 %collective-permute-start.1 = (bf16[27,16,128]{2,1,0:T(8,128)(2,1)S(1)}, bf16[27,16,128]{2,1,0:T(8,128)(2,1)S(1)}, u32[]{:S(2)}, u32[]{:S(2)}) collective-permute-start(bf16[27,16,128]{2,1,0:T(8,128)(2,1)S(1)} %get-tuple-element.32), channel_id=1, source_target_pairs={{0,2},{1,3},{2,0},{3,1},{4,6},{5,7},{6,4},{7,5},{8,10},{9,11},{10,... | collective-permute-start | bytes 331784 | tf_op jit(solution)/shard_map/ppermute | solution.py:267
  4.7 1.1 %copy.9 = bf16[128,4,512]{2,0,1:T(8,128)(2,1)S(1)} copy(bf16[128,4,512]{2,1,0:T(4,128)(2,1)} %param.6) | data formatting | bytes 1048576 | tf_op jit(solution)/shard_map/optimization_barrier | solution.py:297
  6.3 0.8 %collective-permute-done.1 = bf16[27,16,128]{2,1,0:T(8,128)(2,1)S(1)} collective-permute-done((bf16[27,16,128]{2,1,0:T(8,128)(2,1)S(1)}, bf16[27,16,128]{2,1,0:T(8,128)(2,1)S(1)}, u32[]{:S(2)}, u32[]{:S(2)}) %collective-permute-start.1) | collective-permute-done | bytes 110624 | tf_op jit(solution)/shard_map/ppermute | solution.py:267
  7.1 4.7 %collective-permute-done.2 = bf16[27,16,128]{2,1,0:T(8,128)(2,1)S(1)} collective-permute-done((bf16[27,16,128]{2,1,0:T(8,128)(2,1)S(1)}, bf16[27,16,128]{2,1,0:T(8,128)(2,1)S(1)}, u32[]{:S(2)}, u32[]{:S(2)}) %collective-permute-start.2) | collective-permute-done | bytes 110624 | tf_op jit(solution)/shard_map/ppermute | solution.py:267
  11.9 3.9 %collective-permute-start.3 = (bf16[4,128,512]{2,1,0:T(8,128)(2,1)S(1)}, bf16[4,128,512]{2,1,0:T(8,128)(2,1)S(1)}, u32[]{:S(2)}, u32[]{:S(2)}) collective-permute-start(bf16[4,128,512]{2,1,0:T(8,128)(2,1)S(1)} %bitcast.12), channel_id=1, source_target_pairs={{0,2},{1,3},{2,0},{3,1},{4,6},{5,7},{6,4},{7,5},{8,10},{9,11},{10,... | collective-permute-start | bytes 1572872 | tf_op jit(solution)/shard_map/ppermute | solution.py:267
  16.0 1.2 %collective-permute-start.6 = (bf16[3,27,16,128]{3,2,1,0:T(8,128)(2,1)S(1)}, bf16[3,27,16,128]{3,2,1,0:T(8,128)(2,1)S(1)}, u32[]{:S(2)}, u32[]{:S(2)}) collective-permute-start(bf16[3,27,16,128]{3,2,1,0:T(8,128)(2,1)S(1)} %pad_maximum_fusion.refs_3_.refs_2_), channel_id=1, source_target_pairs={{0,16},{4,20},{8,24},{12,28},{16,0},{20,4},{24,8},{28,12},{1,17},{... | collective-permute-start | bytes 995336 | tf_op jit(solution)/shard_map/ppermute | solution.py:267
  17.3 1.2 %collective-permute-start.7 = (bf16[3,27,16,128]{3,2,1,0:T(8,128)(2,1)S(1)}, bf16[3,27,16,128]{3,2,1,0:T(8,128)(2,1)S(1)}, u32[]{:S(2)}, u32[]{:S(2)}) collective-permute-start(bf16[3,27,16,128]{3,2,1,0:T(8,128)(2,1)S(1)} %pad_maximum_fusion.refs_3_.refs_2_), channel_id=1, source_target_pairs={{0,24},{4,28},{8,16},{12,20},{16,8},{20,12},{24,0},{28,4},{1,25},{... | collective-permute-start | bytes 995336 | tf_op jit(solution)/shard_map/ppermute | solution.py:267
  18.4 1.2 %constant_dynamic-slice_fusion.refs_2_ = bf16[27,128,128]{2,1,0:T(8,128)(2,1)S(1)} fusion(bf16[27,512,128]{2,1,0:T(8,128)(2,1)} %bitcast.21, s32[]{:T(128)S(6)} %select_n.23), kind=kLoop, calls=%fused_computation.2 | loop fusion | bytes 1769476 | tf_op jit(solution)/shard_map/dynamic_slice | solution.py:285
  19.6 9.4 %collective-permute-done.8.refs_1_ = bf16[4,128,512]{2,1,0:T(8,128)(2,1)S(1)} collective-permute-done((bf16[4,128,512]{2,1,0:T(8,128)(2,1)S(1)}, bf16[4,128,512]{2,1,0:T(8,128)(2,1)S(1)}, u32[]{:S(2)}, u32[]{:S(2)}) %collective-permute-start.8) | collective-permute-done | bytes 524320 | tf_op jit(solution)/shard_map/ppermute | solution.py:267
  29.0 5.0 %conv_parts.5 = (f32[2,128,512]{2,1,0:T(8,128)S(1)}, f32[2,128,512]{2,1,0:T(8,128)S(1)}, f32[2,128,512]{2,1,0:T(8,128)S(1)}) custom-call(s32[12]{0:T(128)S(1)} %copy-done, bf16[4,128,512]{2,1,0:T(8,128)(2,1)S(1)} %bitcast.13, bf16[27,128,128]{2,1,0:T(8,128)(2,1)S(1)} %constant_dynamic-slice_fusion.refs_2_), custom_call_target="tpu_custom_call" | custom-call | flops 1024 | bytes 1024 | tf_op jit(solution)/shard_map/conv_parts/pallas_call | solution.py:207
  34.1 1.9 %collective-permute-start.10 = (bf16[3,27,16,128]{3,2,1,0:T(8,128)(2,1)S(1)}, bf16[3,27,16,128]{3,2,1,0:T(8,128)(2,1)S(1)}, u32[]{:S(2)}, u32[]{:S(2)}) collective-permute-start(bf16[3,27,16,128]{3,2,1,0:T(8,128)(2,1)S(1)} %collective-permute-done.5.refs_5_.refs_4_), channel_id=1, source_target_pairs={{0,4},{4,0},{8,12},{12,8},{16,20},{20,16},{24,28},{28,24},{1,5},{5... | collective-permute-start | bytes 995336 | tf_op jit(solution)/shard_map/ppermute | solution.py:267
  36.5 1.1 %collective-permute-done.3.refs_2_ = bf16[4,128,512]{2,1,0:T(8,128)(2,1)S(1)} collective-permute-done((bf16[4,128,512]{2,1,0:T(8,128)(2,1)S(1)}, bf16[4,128,512]{2,1,0:T(8,128)(2,1)S(1)}, u32[]{:S(2)}, u32[]{:S(2)}) %collective-permute-start.3) | collective-permute-done | bytes 524320 | tf_op jit(solution)/shard_map/ppermute | solution.py:267
  38.6 2.1 %conv_parts.8 = f32[2,128,512]{2,1,0:T(8,128)S(1)} custom-call(s32[12]{0:T(128)S(1)} %copy-done, bf16[4,128,512]{2,1,0:T(8,128)(2,1)S(1)} %collective-permute-done.8.refs_1_, bf16[4,128,512]{2,1,0:T(8,128)(2,1)S(1)} %collective-permute-done.3.refs_2_, bf16[3,27,16,128]{3,2,1,0:T(8,128)(2,1)S(1)} %pad_maximum_fusion.refs_3_.refs_2_, ...), custom_call_target="tpu_custom_call" | custom-call | flops 1024 | bytes 1024 | tf_op jit(solution)/shard_map/conv_parts/pallas_call | solution.py:207
  40.8 4.4 %collective-permute-start.15 = (f32[2,128,512]{2,1,0:T(8,128)S(1)}, f32[2,128,512]{2,1,0:T(8,128)S(1)}, u32[]{:S(2)}, u32[]{:S(2)}) collective-permute-start(f32[2,128,512]{2,1,0:T(8,128)S(1)} %conv_parts.8), channel_id=1, source_target_pairs={{0,4},{4,8},{8,12},{12,16},{16,20},{20,24},{24,28},{1,5},{5,9},{9,... | collective-permute-start | bytes 1572872 | tf_op jit(solution)/shard_map/ppermute | solution.py:334
  45.2 3.4 %collective-permute-start.14 = (bf16[2,128,512]{2,1,0:T(8,128)(2,1)S(1)}, bf16[2,128,512]{2,1,0:T(8,128)(2,1)S(1)}, u32[]{:S(2)}, u32[]{:S(2)}) collective-permute-start(bf16[2,128,512]{2,1,0:T(8,128)(2,1)S(1)} %slice.4), channel_id=1, source_target_pairs={{1,4},{0,5},{3,6},{2,7},{5,8},{4,9},{7,10},{6,11},{9,12},{8,13},{1... | collective-permute-start | bytes 786440 | tf_op jit(solution)/shard_map/ppermute | solution.py:321
  48.5 6.1 %conv_parts.6 = (f32[2,128,512]{2,1,0:T(8,128)S(1)}, f32[2,128,512]{2,1,0:T(8,128)S(1)}) custom-call(s32[12]{0:T(128)S(1)} %copy-done, bf16[4,128,512]{2,1,0:T(8,128)(2,1)S(1)} %collective-permute-done.8.refs_1_, bf16[4,128,512]{2,1,0:T(8,128)(2,1)S(1)} %collective-permute-done.3.refs_2_, bf16[3,27,16,128]{3,2,1,0:T(8,128)(2,1)S(1)} %pad_maximum_fusion.refs_3_.refs_2_, ...), custom_call_target="tpu_custom_call" | custom-call | flops 1024 | bytes 1024 | tf_op jit(solution)/shard_map/conv_parts/pallas_call | solution.py:207
  54.7 3.1 %conv_parts.7.tail_ref = bf16[2,128,512]{2,1,0:T(8,128)(2,1)S(1)} custom-call(s32[12]{0:T(128)S(1)} %copy-done, bf16[4,128,512]{2,1,0:T(8,128)(2,1)S(1)} %collective-permute-done.4.refs_1_, bf16[3,27,16,128]{3,2,1,0:T(8,128)(2,1)S(1)} %pad_maximum_fusion.refs_3_.refs_2_, bf16[3,27,16,128]{3,2,1,0:T(8,128)(2,1)S(1)} %collective-permute-done.9.refs_4_.refs_3_, ...), custom_call_target="tpu_custom_call" | custom-call | flops 2500000000 | bytes 1024 | tf_op jit(solution)/shard_map/conv_parts/pallas_call | solution.py:207
  57.8 3.7 %collective-permute-start.13 = (bf16[2,128,512]{2,1,0:T(8,128)(2,1)S(1)}, bf16[2,128,512]{2,1,0:T(8,128)(2,1)S(1)}, u32[]{:S(2)}, u32[]{:S(2)}) collective-permute-start(bf16[2,128,512]{2,1,0:T(8,128)(2,1)S(1)} %conv_parts.7.tail_ref), channel_id=1, source_target_pairs={{0,4},{4,8},{8,12},{12,16},{16,20},{20,24},{24,28},{1,5},{5,9},{9,... | collective-permute-start | bytes 786440 | tf_op jit(solution)/shard_map/ppermute | solution.py:339
  61.5 3.2 %conv_parts.9.head_ref = bf16[2,128,512]{2,1,0:T(8,128)(2,1)S(1)} custom-call(s32[12]{0:T(128)S(1)} %copy-done, bf16[4,128,512]{2,1,0:T(8,128)(2,1)S(1)} %collective-permute-done.4.refs_1_, bf16[2,128,512]{2,1,0:T(8,128)(2,1)S(1)} %collective-permute-done.14.refs_2_, bf16[3,27,16,128]{3,2,1,0:T(8,128)(2,1)S(1)} %pad_maximum_fusion.refs_3_.refs_2_, ...), custom_call_target="tpu_custom_call" | custom-call | flops 1024 | bytes 1024 | tf_op jit(solution)/shard_map/conv_parts/pallas_call | solution.py:207
  64.7 1.9 %collective-permute-start.16 = (bf16[2,128,512]{2,1,0:T(8,128)(2,1)S(1)}, bf16[2,128,512]{2,1,0:T(8,128)(2,1)S(1)}, u32[]{:S(2)}, u32[]{:S(2)}) collective-permute-start(bf16[2,128,512]{2,1,0:T(8,128)(2,1)S(1)} %conv_parts.9.head_ref), channel_id=1, source_target_pairs={{4,0},{8,4},{12,8},{16,12},{20,16},{24,20},{28,24},{5,1},{9,5},{13... | collective-permute-start | bytes 786440 | tf_op jit(solution)/shard_map/ppermute | solution.py:344
  66.6 6.7 %collective-permute-done.16.after_ref = bf16[2,128,512]{2,1,0:T(8,128)(2,1)S(1)} collective-permute-done((bf16[2,128,512]{2,1,0:T(8,128)(2,1)S(1)}, bf16[2,128,512]{2,1,0:T(8,128)(2,1)S(1)}, u32[]{:S(2)}, u32[]{:S(2)}) %collective-permute-start.16) | collective-permute-done | bytes 262176 | tf_op jit(solution)/shard_map/ppermute | solution.py:344
  73.3 2.1 %slots.1 = bf16[128,8,512]{2,1,0:T(8,128)(2,1)} custom-call(s32[1,2]{1,0:T(1,128)S(1)} %copy-done.3, bf16[2,128,512]{2,1,0:T(8,128)(2,1)S(1)} %collective-permute-done.13.before_ref, bf16[2,128,512]{2,1,0:T(8,128)(2,1)S(1)} %conv_parts.9.head_ref, bf16[2,128,512]{2,1,0:T(8,128)(2,1)S(1)} %conv_parts.7.tail_ref, ...), custom_call_target="tpu_custom_call" | custom-call | tf_op jit(solution)/shard_map/slots/pallas_call | solution.py:255
  (29 shorter events, 2.4 us)
Async XLA Ops:
  0.0 29.0 %copy-start = (s32[12]{0:T(128)S(1)}, s32[12]{0:T(128)}, u32[]{:S(2)}) copy-start(s32[12]{0:T(128)} %refs_0_.9) | copy-start | bytes 148
  1.1 4.8 %collective-permute-start = (bf16[27,16,128]{2,1,0:T(8,128)(2,1)S(1)}, bf16[27,16,128]{2,1,0:T(8,128)(2,1)S(1)}, u32[]{:S(2)}, u32[]{:S(2)}) collective-permute-start(bf16[27,16,128]{2,1,0:T(8,128)(2,1)S(1)} %get-tuple-element.29), channel_id=1, source_target_pairs={{0,1},{1,0},{2,3},{3,2},{4,5},{5,4},{6,7},{7,6},{8,9},{9,8},{10,11... | collective-permute-start | bytes 331784 | tf_op jit(solution)/shard_map/ppermute | solution.py:267
  2.4 4.7 %collective-permute-start.1 = (bf16[27,16,128]{2,1,0:T(8,128)(2,1)S(1)}, bf16[27,16,128]{2,1,0:T(8,128)(2,1)S(1)}, u32[]{:S(2)}, u32[]{:S(2)}) collective-permute-start(bf16[27,16,128]{2,1,0:T(8,128)(2,1)S(1)} %get-tuple-element.32), channel_id=1, source_target_pairs={{0,2},{1,3},{2,0},{3,1},{4,6},{5,7},{6,4},{7,5},{8,10},{9,11},{10,... | collective-permute-start | bytes 331784 | tf_op jit(solution)/shard_map/ppermute | solution.py:267
  4.7 7.1 %collective-permute-start.2 = (bf16[27,16,128]{2,1,0:T(8,128)(2,1)S(1)}, bf16[27,16,128]{2,1,0:T(8,128)(2,1)S(1)}, u32[]{:S(2)}, u32[]{:S(2)}) collective-permute-start(bf16[27,16,128]{2,1,0:T(8,128)(2,1)S(1)} %get-tuple-element.33), channel_id=1, source_target_pairs={{0,3},{1,2},{2,1},{3,0},{4,7},{5,6},{6,5},{7,4},{8,11},{9,10},{10,... | collective-permute-start | bytes 331784 | tf_op jit(solution)/shard_map/ppermute | solution.py:267
  5.9 23.2 %collective-permute-start.8 = (bf16[4,128,512]{2,1,0:T(8,128)(2,1)S(1)}, bf16[4,128,512]{2,1,0:T(8,128)(2,1)S(1)}, u32[]{:S(2)}, u32[]{:S(2)}) collective-permute-start(bf16[4,128,512]{2,1,0:T(8,128)(2,1)S(1)} %bitcast.11), channel_id=1, source_target_pairs={{0,1},{1,0},{2,3},{3,2},{4,5},{5,4},{6,7},{7,6},{8,9},{9,8},{10,11... | collective-permute-start | bytes 1572872 | tf_op jit(solution)/shard_map/ppermute | solution.py:267
  11.9 25.7 %collective-permute-start.3 = (bf16[4,128,512]{2,1,0:T(8,128)(2,1)S(1)}, bf16[4,128,512]{2,1,0:T(8,128)(2,1)S(1)}, u32[]{:S(2)}, u32[]{:S(2)}) collective-permute-start(bf16[4,128,512]{2,1,0:T(8,128)(2,1)S(1)} %bitcast.12), channel_id=1, source_target_pairs={{0,2},{1,3},{2,0},{3,1},{4,6},{5,7},{6,4},{7,5},{8,10},{9,11},{10,... | collective-permute-start | bytes 1572872 | tf_op jit(solution)/shard_map/ppermute | solution.py:267
  15.8 18.3 %collective-permute-start.5 = (bf16[3,27,16,128]{3,2,1,0:T(8,128)(2,1)S(1)}, bf16[3,27,16,128]{3,2,1,0:T(8,128)(2,1)S(1)}, u32[]{:S(2)}, u32[]{:S(2)}) collective-permute-start(bf16[3,27,16,128]{3,2,1,0:T(8,128)(2,1)S(1)} %pad_maximum_fusion.refs_3_.refs_2_), channel_id=1, source_target_pairs={{0,8},{4,12},{8,0},{12,4},{16,24},{20,28},{24,16},{28,20},{1,9},{5... | collective-permute-start | bytes 995336 | tf_op jit(solution)/shard_map/ppermute | solution.py:267
  16.0 18.0 %collective-permute-start.6 = (bf16[3,27,16,128]{3,2,1,0:T(8,128)(2,1)S(1)}, bf16[3,27,16,128]{3,2,1,0:T(8,128)(2,1)S(1)}, u32[]{:S(2)}, u32[]{:S(2)}) collective-permute-start(bf16[3,27,16,128]{3,2,1,0:T(8,128)(2,1)S(1)} %pad_maximum_fusion.refs_3_.refs_2_), channel_id=1, source_target_pairs={{0,16},{4,20},{8,24},{12,28},{16,0},{20,4},{24,8},{28,12},{1,17},{... | collective-permute-start | bytes 995336 | tf_op jit(solution)/shard_map/ppermute | solution.py:267
  17.3 16.8 %collective-permute-start.7 = (bf16[3,27,16,128]{3,2,1,0:T(8,128)(2,1)S(1)}, bf16[3,27,16,128]{3,2,1,0:T(8,128)(2,1)S(1)}, u32[]{:S(2)}, u32[]{:S(2)}) collective-permute-start(bf16[3,27,16,128]{3,2,1,0:T(8,128)(2,1)S(1)} %pad_maximum_fusion.refs_3_.refs_2_), channel_id=1, source_target_pairs={{0,24},{4,28},{8,16},{12,20},{16,8},{20,12},{24,0},{28,4},{1,25},{... | collective-permute-start | bytes 995336 | tf_op jit(solution)/shard_map/ppermute | solution.py:267
  34.1 3.5 %collective-permute-start.10 = (bf16[3,27,16,128]{3,2,1,0:T(8,128)(2,1)S(1)}, bf16[3,27,16,128]{3,2,1,0:T(8,128)(2,1)S(1)}, u32[]{:S(2)}, u32[]{:S(2)}) collective-permute-start(bf16[3,27,16,128]{3,2,1,0:T(8,128)(2,1)S(1)} %collective-permute-done.5.refs_5_.refs_4_), channel_id=1, source_target_pairs={{0,4},{4,0},{8,12},{12,8},{16,20},{20,16},{24,28},{28,24},{1,5},{5... | collective-permute-start | bytes 995336 | tf_op jit(solution)/shard_map/ppermute | solution.py:267
  35.9 1.7 %collective-permute-start.11 = (bf16[3,27,16,128]{3,2,1,0:T(8,128)(2,1)S(1)}, bf16[3,27,16,128]{3,2,1,0:T(8,128)(2,1)S(1)}, u32[]{:S(2)}, u32[]{:S(2)}) collective-permute-start(bf16[3,27,16,128]{3,2,1,0:T(8,128)(2,1)S(1)} %collective-permute-done.6.refs_7_.refs_6_), channel_id=1, source_target_pairs={{0,4},{4,0},{8,12},{12,8},{16,20},{20,16},{24,28},{28,24},{1,5},{5... | collective-permute-start | bytes 995336 | tf_op jit(solution)/shard_map/ppermute | solution.py:267
  36.0 2.1 %collective-permute-start.12 = (bf16[3,27,16,128]{3,2,1,0:T(8,128)(2,1)S(1)}, bf16[3,27,16,128]{3,2,1,0:T(8,128)(2,1)S(1)}, u32[]{:S(2)}, u32[]{:S(2)}) collective-permute-start(bf16[3,27,16,128]{3,2,1,0:T(8,128)(2,1)S(1)} %collective-permute-done.7.refs_9_.refs_8_), channel_id=1, source_target_pairs={{0,4},{4,0},{8,12},{12,8},{16,20},{20,16},{24,28},{28,24},{1,5},{5... | collective-permute-start | bytes 995336 | tf_op jit(solution)/shard_map/ppermute | solution.py:267
  36.4 2.2 %collective-permute-start.9 = (bf16[3,27,16,128]{3,2,1,0:T(8,128)(2,1)S(1)}, bf16[3,27,16,128]{3,2,1,0:T(8,128)(2,1)S(1)}, u32[]{:S(2)}, u32[]{:S(2)}) collective-permute-start(bf16[3,27,16,128]{3,2,1,0:T(8,128)(2,1)S(1)} %pad_maximum_fusion.refs_3_.refs_2_), channel_id=1, source_target_pairs={{0,4},{4,0},{8,12},{12,8},{16,20},{20,16},{24,28},{28,24},{1,5},{5... | collective-permute-start | bytes 995336 | tf_op jit(solution)/shard_map/ppermute | solution.py:267
  37.6 17.1 %collective-permute-start.4 = (bf16[4,128,512]{2,1,0:T(8,128)(2,1)S(1)}, bf16[4,128,512]{2,1,0:T(8,128)(2,1)S(1)}, u32[]{:S(2)}, u32[]{:S(2)}) collective-permute-start(bf16[4,128,512]{2,1,0:T(8,128)(2,1)S(1)} %collective-permute-done.3.refs_2_), channel_id=1, source_target_pairs={{0,1},{1,0},{2,3},{3,2},{4,5},{5,4},{6,7},{7,6},{8,9},{9,8},{10,11... | collective-permute-start | bytes 1572872 | tf_op jit(solution)/shard_map/ppermute | solution.py:267
  40.7 13.9 %copy-start.1 = (f32[128]{0:T(128)S(1)}, f32[128]{0:T(128)}, u32[]{:S(2)}) copy-start(f32[128]{0:T(128)} %param.8) | copy-start | bytes 1540
  40.7 13.9 %copy-start.2 = (f32[128]{0:T(128)S(1)}, f32[128]{0:T(128)}, u32[]{:S(2)}) copy-start(f32[128]{0:T(128)} %param.9) | copy-start | bytes 1540
  40.8 20.8 %collective-permute-start.15 = (f32[2,128,512]{2,1,0:T(8,128)S(1)}, f32[2,128,512]{2,1,0:T(8,128)S(1)}, u32[]{:S(2)}, u32[]{:S(2)}) collective-permute-start(f32[2,128,512]{2,1,0:T(8,128)S(1)} %conv_parts.8), channel_id=1, source_target_pairs={{0,4},{4,8},{8,12},{12,16},{16,20},{20,24},{24,28},{1,5},{5,9},{9,... | collective-permute-start | bytes 1572872 | tf_op jit(solution)/shard_map/ppermute | solution.py:334
  45.2 16.4 %collective-permute-start.14 = (bf16[2,128,512]{2,1,0:T(8,128)(2,1)S(1)}, bf16[2,128,512]{2,1,0:T(8,128)(2,1)S(1)}, u32[]{:S(2)}, u32[]{:S(2)}) collective-permute-start(bf16[2,128,512]{2,1,0:T(8,128)(2,1)S(1)} %slice.4), channel_id=1, source_target_pairs={{1,4},{0,5},{3,6},{2,7},{5,8},{4,9},{7,10},{6,11},{9,12},{8,13},{1... | collective-permute-start | bytes 786440 | tf_op jit(solution)/shard_map/ppermute | solution.py:321
  57.8 15.5 %copy-start.3 = (s32[1,2]{1,0:T(1,128)S(1)}, s32[1,2]{1,0:T(1,128)}, u32[]{:S(2)}) copy-start(s32[1,2]{1,0:T(1,128)} %bounds_ref.1) | copy-start | bytes 28
  57.8 8.8 %collective-permute-start.13 = (bf16[2,128,512]{2,1,0:T(8,128)(2,1)S(1)}, bf16[2,128,512]{2,1,0:T(8,128)(2,1)S(1)}, u32[]{:S(2)}, u32[]{:S(2)}) collective-permute-start(bf16[2,128,512]{2,1,0:T(8,128)(2,1)S(1)} %conv_parts.7.tail_ref), channel_id=1, source_target_pairs={{0,4},{4,8},{8,12},{12,16},{16,20},{20,24},{24,28},{1,5},{5,9},{9,... | collective-permute-start | bytes 786440 | tf_op jit(solution)/shard_map/ppermute | solution.py:339
  64.7 8.6 %collective-permute-start.16 = (bf16[2,128,512]{2,1,0:T(8,128)(2,1)S(1)}, bf16[2,128,512]{2,1,0:T(8,128)(2,1)S(1)}, u32[]{:S(2)}, u32[]{:S(2)}) collective-permute-start(bf16[2,128,512]{2,1,0:T(8,128)(2,1)S(1)} %conv_parts.9.head_ref), channel_id=1, source_target_pairs={{4,0},{8,4},{12,8},{16,12},{20,16},{24,20},{28,24},{5,1},{9,5},{13... | collective-permute-start | bytes 786440 | tf_op jit(solution)/shard_map/ppermute | solution.py:344

commit v2 on v1

v2 whole, which is shorter than its diff:
```python
import functools

import jax
import jax.numpy as jnp
from jax import lax
from jax.experimental import pallas as pl
from jax.experimental.pallas import tpu as pltpu
from jax.sharding import PartitionSpec as P

C = 512
GROUPS = 32
H = 16
W = 32
CELLS = H * W
GROUP_WIDTH = C // GROUPS
PIECES = 8
TAPS = 27
LANES = 128
VMEM_BYTES = 9 * 1024 * 1024

norm_eps = 1e-06


def clip_start(clip_ref, g):
    first = jnp.int32(0)
    running = jnp.int32(0)
    for c in range(clip_ref.shape[0]):
        first = jnp.where(running <= g, jnp.maximum(first, running), first)
        running = running + clip_ref[c]
    return first


def group_sum(grouped):
    tiles = [grouped[:, :, i : i + LANES] for i in range(0, CELLS, LANES)]
    while len(tiles) > 1:
        tiles = [x + y for x, y in zip(tiles[::2], tiles[1::2])]
    folded = tiles[0][:, :8] + tiles[0][:, 8:]
    return jnp.sum(jnp.sum(folded, axis=1, keepdims=True), axis=2, keepdims=True)


def group_norm(total, gain, bias):
    own = total.shape[0]
    grouped = total.reshape(own // GROUP_WIDTH, GROUP_WIDTH, CELLS)
    scale = 1.0 / (GROUP_WIDTH * CELLS)
    centred = grouped - group_sum(grouped) * scale
    variance = group_sum(centred * centred) * scale
    normed = (centred * lax.rsqrt(variance + norm_eps)).reshape(own, CELLS)
    return normed * gain + bias


def as_column(row):
    count = row.shape[1]
    return jnp.transpose(jnp.broadcast_to(row, (count, count)))[:, :1]


def finished(total, gain, bias, residual):
    normed = group_norm(total, gain, bias)
    activated = normed / (1.0 + jnp.exp(-normed))
    return (activated + residual.astype(jnp.float32)).astype(jnp.bfloat16)


def piece_starts(piece_rows):
    place = lax.axis_index("tm") % PIECES
    return [
        pl.multiple_of(jnp.bitwise_xor(place, i) * piece_rows, piece_rows) for i in range(PIECES)
    ]


def store_in_order(ref, total):
    rows = total.shape[0] // PIECES
    for block, start in enumerate(piece_starts(rows)):
        ref[pl.ds(start, rows), :] = total[block * rows : (block + 1) * rows]


def store_shifted(ref, index, frame):
    shard = frame.shape[0]
    column = lax.broadcasted_iota(jnp.int32, (1, CELLS), 1) % W
    zero = jnp.zeros_like(frame)
    ref[(*index, pl.ds(0, shard))] = jnp.where(column > 0, pltpu.roll(frame, 1, 1), zero)
    ref[(*index, pl.ds(shard, shard))] = frame
    ref[(*index, pl.ds(2 * shard, shard))] = jnp.where(
        column < W - 1, pltpu.roll(frame, CELLS - 1, 1), zero
    )


def row_taps(pieces, inputs, time_taps):
    weights = []
    for a in range(3):
        for block in range(PIECES):
            row = [
                part[block][9 * k + 3 * a + b] for part in pieces for k in time_taps for b in range(3)
            ]
            weights.append(jnp.concatenate(row, axis=1))
    product = jnp.dot(
        jnp.concatenate(weights, axis=0),
        jnp.concatenate(inputs, axis=0),
        preferred_element_type=jnp.float32,
    )
    own = product.shape[0] // 3
    cell = lax.broadcasted_iota(jnp.int32, (1, CELLS), 1)
    up = pltpu.roll(product[:own], W, 1)
    down = pltpu.roll(product[2 * own :], CELLS - W, 1)
    return (
        jnp.where(cell >= W, up, 0.0)
        + product[own : 2 * own]
        + jnp.where(cell < CELLS - W, down, 0.0)
    )


def conv_kernel(parts, slots_of, groups, *refs):
    refs = list(refs)
    clip_ref = refs.pop(0)
    frame_refs = [refs.pop(0) for _ in range(parts)]
    weight_refs = [refs.pop(0) for _ in range(1 if slots_of is None else PIECES)]
    sum_refs = [None if slots_of is None else refs.pop(0) for _ in groups]
    out_refs = [refs.pop(0) for _ in groups]
    shifted_ref = refs.pop(0)
    frame_count, shard, _ = frame_refs[0].shape
    own = out_refs[0].shape[1]
    first_frame = lax.axis_index("tm") * frame_count
    starts = piece_starts(own // PIECES)
    for p in range(parts):
        for f in range(0 if "own" in groups else frame_count // 2, frame_count):
            store_shifted(shifted_ref, (p, f), frame_refs[p][f])
        shifted_ref[p, frame_count] = jnp.zeros_like(shifted_ref[p, frame_count])

    def weight_rows(p, i):
        if slots_of is None:
            return weight_refs[0][:, pl.ds(starts[i], own // PIECES), :]
        return weight_refs[i][slots_of[p]]

    def convolved(j, time_taps):
        g = first_frame + j
        first = clip_start(clip_ref, g)
        inputs = []
        for p in range(parts):
            for k in time_taps:
                source = jnp.maximum(g - 2 + k, first) - first_frame
                source = jnp.where(source < 0, frame_count, jnp.minimum(source, frame_count))
                inputs.append(shifted_ref[p, source])
        pieces = [[weight_rows(p, i) for i in range(PIECES)] for p in range(parts)]
        return row_taps(pieces, inputs, time_taps)

    for group, out_ref, sum_ref in zip(groups, out_refs, sum_refs):
        if group == "next":
            for i, time_taps in enumerate(((0, 1), (0,))):
                total = convolved(frame_count + i, time_taps)
                if sum_ref is not None:
                    total = total + sum_ref[i]
                if groups == ("next",):
                    store_in_order(out_ref.at[i], total)
                else:
                    out_ref[i] = total
            continue

        def one_frame(j, carry, out_ref=out_ref, sum_ref=sum_ref):
            total = convolved(j, (0, 1, 2))
            out_ref[j] = total if sum_ref is None else total + sum_ref[j]
            return carry

        lax.fori_loop(0, frame_count, one_frame, 0)


def conv_parts(clip_lengths, shards_in, weights, slots_of, groups, sums=()):
    frame_count, shard, cells = shards_in[0].shape
    own, parts = shard, len(shards_in)
    vectors = pl.BlockSpec(memory_space=pltpu.VMEM)
    operands = [clip_lengths, *shards_in, *weights, *sums]
    frames = {"own": frame_count, "next": frame_count // 2}
    return pl.pallas_call(
        functools.partial(conv_kernel, parts, slots_of, groups),
        out_shape=[
            jax.ShapeDtypeStruct((frames[group], own, cells), jnp.float32) for group in groups
        ],
        in_specs=[pl.BlockSpec(memory_space=pltpu.SMEM)] + [vectors] * (len(operands) - 1),
        out_specs=[vectors] * len(groups),
        scratch_shapes=[pltpu.VMEM((parts, frame_count + 1, 3 * shard, cells), jnp.bfloat16)],
        compiler_params=pltpu.CompilerParams(vmem_limit_bytes=VMEM_BYTES),
        cost_estimate=pl.CostEstimate(flops=1024, bytes_accessed=1024, transcendentals=0),
        name="conv_parts",
    )(*operands)


def shift_kernel(frames_ref, out_ref):
    for f in range(frames_ref.shape[0]):
        store_shifted(out_ref, (f,), frames_ref[f])


def shifted_frames(frames):
    count, shard, cells = frames.shape
    return pl.pallas_call(
        shift_kernel,
        out_shape=jax.ShapeDtypeStruct((count, 3 * shard, cells), jnp.bfloat16),
        in_specs=[pl.BlockSpec(memory_space=pltpu.VMEM)],
        out_specs=pl.BlockSpec(memory_space=pltpu.VMEM),
        compiler_params=pltpu.CompilerParams(vmem_limit_bytes=VMEM_BYTES),
        cost_estimate=pl.CostEstimate(flops=1500000000, bytes_accessed=1024, transcendentals=0),
        name="shifted_frames",
    )(frames)


def last_kernel(slot, far, *refs):
    refs = list(refs)
    clip_ref, shifted_ref, halo_ref = refs[:3]
    weight_refs = refs[3 : 3 + PIECES]
    sum_ref, arrived_ref, residual_ref, gain_ref, bias_ref = refs[3 + PIECES : 8 + PIECES]
    out_ref, earlier_ref, total_ref = refs[8 + PIECES :]
    frame_count = shifted_ref.shape[0]
    half = frame_count // 2
    slab = lax.axis_index("tm")
    first_frame = slab * frame_count
    tail = (slab % 2 == 1) if far else (slab % 2 == 0)
    gain, bias = as_column(gain_ref[...]), as_column(bias_ref[...])

    @pl.when(jnp.logical_not(tail))
    def _():
        for f in range(half):
            store_shifted(earlier_ref, (f,), halo_ref[f])

    @pl.when(tail)
    def _():
        for f in range(half):
            earlier_ref[f] = jnp.zeros_like(earlier_ref[f])

    def one_frame(i, carry):
        j = jnp.where(tail, i + half, i)
        g = first_frame + j
        first = clip_start(clip_ref, g)
        inputs = []
        for k in range(3):
            source = jnp.maximum(g - 2 + k, first) - first_frame
            inputs.append(
                jnp.where(
                    source < 0,
                    earlier_ref[jnp.clip(source + 2, 0, half - 1)],
                    shifted_ref[jnp.maximum(source, 0)],
                )
            )
        pieces = [[ref[min(slot, ref.shape[0] - 1)] for ref in weight_refs]]
        total = row_taps(pieces, inputs, (0, 1, 2)) + sum_ref[j]
        store_in_order(total_ref, total)
        total = total_ref[...] + jnp.where(tail, 0.0, arrived_ref[i])
        out_ref[i] = finished(total, gain, bias, residual_ref[j])
        return carry

    lax.fori_loop(0, half, one_frame, 0)


def last_part(clip_lengths, far, slot, *operands):
    shifted, halo = operands[:2]
    half, shard, cells = halo.shape
    vectors = pl.BlockSpec(memory_space=pltpu.VMEM)
    return pl.pallas_call(
        functools.partial(last_kernel, slot, far),
        out_shape=jax.ShapeDtypeStruct((half, shard, cells), jnp.bfloat16),
        in_specs=[pl.BlockSpec(memory_space=pltpu.SMEM)] + [vectors] * len(operands),
        out_specs=vectors,
        scratch_shapes=[
            pltpu.VMEM((half, 3 * shard, cells), jnp.bfloat16),
            pltpu.VMEM((shard, cells), jnp.float32),
        ],
        compiler_params=pltpu.CompilerParams(vmem_limit_bytes=VMEM_BYTES),
        cost_estimate=pl.CostEstimate(flops=1024 if far else 1024, bytes_accessed=1024, transcendentals=0),
        name="last_part",
    )(clip_lengths, *operands)


def slot_of(bounds_ref, frame_count, position):
    first = lax.axis_index("tm") * frame_count - frame_count // 2
    return position + first - bounds_ref[0, 0], bounds_ref[0, 1] - bounds_ref[0, 0]


def near_position(place, half):
    odd = lax.axis_index("tm") % 2 == 1
    return jnp.where(odd, place * half, (3 - place) * half)


def window_kernel(bounds_ref, near_ref, far_ref, far_in_ref, out_ref):
    half = near_ref.shape[0]
    capacity = out_ref.shape[0]
    for place, pair in enumerate((near_ref, far_ref, far_in_ref), 1):
        for i in range(half):
            slot, size = slot_of(bounds_ref, 2 * half, near_position(place, half) + i)

            @pl.when((slot >= 0) & (slot < size))
            def _():
                out_ref[slot] = pair[i].astype(jnp.float32)

    for slot in range(capacity):

        @pl.when(slot >= size)
        def _():
            out_ref[slot] = jnp.zeros_like(out_ref[slot])


def slots_kernel(bounds_ref, window_ref, near_in_ref, out_ref):
    capacity, channels, _ = window_ref.shape
    half = near_in_ref.shape[0]
    position = near_position(0, half)
    slot, size = slot_of(bounds_ref, 2 * half, position)
    rows = 16
    for start in range(0, channels, rows):
        frames = [window_ref[w, start : start + rows, :] for w in range(capacity)]
        for i in range(half):
            frame = near_in_ref[i, start : start + rows, :].astype(jnp.float32)
            for w in range(capacity):
                frames[w] = jnp.where((slot + i == w) & (w < size), frame, frames[w])
        block = jnp.stack(frames)
        out_ref[start : start + rows] = jnp.swapaxes(block, 0, 1).astype(jnp.bfloat16)


def slots(bounds, near_in, near, far, far_in):
    half, channels, cells = near.shape
    capacity = 4 * half
    scalars = pl.BlockSpec(memory_space=pltpu.SMEM)
    vectors = pl.BlockSpec(memory_space=pltpu.VMEM)
    window = pl.pallas_call(
        window_kernel,
        out_shape=jax.ShapeDtypeStruct((capacity, channels, cells), jnp.float32),
        in_specs=[scalars] + [vectors] * 3,
        out_specs=vectors,
        compiler_params=pltpu.CompilerParams(vmem_limit_bytes=VMEM_BYTES),
        cost_estimate=pl.CostEstimate(flops=1000000000, bytes_accessed=1024, transcendentals=0),
        name="window",
    )(bounds, near, far, far_in)
    return pl.pallas_call(
        slots_kernel,
        out_shape=jax.ShapeDtypeStruct((channels, capacity, cells), jnp.bfloat16),
        in_specs=[scalars] + [vectors] * 2,
        out_specs=vectors,
        compiler_params=pltpu.CompilerParams(vmem_limit_bytes=VMEM_BYTES),
        name="slots",
    )(bounds, window, near_in)


def xor_permute(array, axis, bits):
    return lax.ppermute(array, axis, [(i, i ^ bits) for i in range(lax.axis_size(axis))])


def weight_blocks(by_tap):
    _, out_channels, shard = by_tap.shape
    chan_count = lax.axis_size("chan")
    own = out_channels // chan_count
    piece_rows = own // PIECES
    piece = lax.axis_index("tm") % PIECES
    me = lax.axis_index("chan")
    pieces = [
        lax.dynamic_slice(
            by_tap,
            (0, jnp.bitwise_xor(me, s) * own + piece * piece_rows, 0),
            (TAPS, piece_rows, shard),
        )
        for s in range(1, chan_count)
    ]
    return lax.dynamic_slice(by_tap, (0, me * own, 0), (TAPS, own, shard)), pieces


def shards(latents, conv_weight, norm_gain, norm_bias, clip_lengths, slab_bounds):
    own, frame_count, cells = latents.shape
    out_channels, _, _, shard = conv_weight.shape
    tm_count = lax.axis_size("tm")

    by_tap = jnp.transpose(conv_weight, (1, 2, 0, 3)).reshape(TAPS, out_channels, shard)
    own_weights, blocks = weight_blocks(by_tap)
    blocks, latents = lax.optimization_barrier((blocks, latents))
    by_frame = jnp.transpose(latents, (1, 0, 2))
    swapped = [xor_permute(block, "chan", s) for s, block in enumerate(blocks, 1)]

    half = frame_count // 2
    swapped[0], by_frame = lax.optimization_barrier((swapped[0], by_frame))
    first = xor_permute(by_frame, "chan", 1)
    swapped, kept = lax.optimization_barrier((jnp.stack(swapped), by_frame))
    second = xor_permute(kept, "chan", 2)
    total, following = conv_parts(clip_lengths, [by_frame], [own_weights], None, ("own", "next"))
    same_core = [swapped] + [xor_permute(swapped, "tm", bits) for bits in range(2, PIECES, 2)]
    same_core, total, first = lax.optimization_barrier((same_core, total, first))
    other_core = [xor_permute(piece, "tm", 1) for piece in same_core]
    weights = [piece for pair in zip(same_core, other_core) for piece in pair]
    third = xor_permute(second, "chan", 1)
    chan_count = lax.axis_size("chan")
    third_halo = lax.ppermute(
        second[half:],
        ("tm", "chan"),
        [
            (t * chan_count + (c ^ 1), (t + 1) * chan_count + c)
            for t in range(tm_count - 1)
            for c in range(chan_count)
        ],
    )
    pair, slots_of = [first, second], (0, 1)
    (following,) = conv_parts(clip_lengths, pair, weights, slots_of, ("next",), [following])
    arrived = lax.ppermute(following, "tm", [(i, i + 1) for i in range(tm_count - 1)])
    (total,) = conv_parts(clip_lengths, pair, weights, slots_of, ("own",), [total])
    operands = [shifted_frames(third), third_halo, *weights, total]
    params = (by_frame, norm_gain.reshape(1, own), norm_bias.reshape(1, own))

    def swapped_pairs(start):
        pairs = range(start, tm_count - 1, 2)
        return [(i, i + 1) for i in pairs] + [(i + 1, i) for i in pairs]

    far = last_part(clip_lengths, True, 2, *operands, arrived, *params)
    far_in = lax.ppermute(far, "tm", swapped_pairs(1))
    arrived, far = lax.optimization_barrier((arrived, far))
    near = last_part(clip_lengths, False, 2, *operands, arrived, *params)
    near_in = lax.ppermute(near, "tm", swapped_pairs(0))
    return slots(slab_bounds, near_in, near, far, far_in)


def solution(mesh):
    placed = (
        P("chan", "tm", None),
        P(None, None, None, "chan"),
        P("chan"),
        P("chan"),
        P(),
        P("tm", None),
    )
    return jax.shard_map(
        shards, mesh=mesh, in_specs=placed, out_specs=P("chan", "tm", None), check_vma=False
    )
```

time: 75.7 us -> 73.9 us (0.976)
  waiting for transfers between devices: 23.7 us -> 20.5 us
  Pallas kernels: 21.6 us -> 22.6 us
    ppermute x3, waiting for transfers between devices: 6.66 us -> 3.57 us  [the longest x1 3.57 us: shards(): far_in = lax.ppermute(far, 'tm', swapped_pairs(1))]
    ppermute x13, waiting for transfers between devices: 17 us -> 15.1 us  [xor_permute(): lax.ppermute(array, axis, [(i, i ^ bits) for i in range(lax.axis_size(axi...]
    ppermute x1, waiting for transfers between devices: 0.01 us -> 1.82 us  [shards(): lax.ppermute(second[half:], ('tm', 'chan'), [(t * chan_count + (c ^ 1), (...]
    ppermute x3, starting transfers between devices: 9.96 us -> 8.75 us  [the longest x1 5.36 us: shards(): lax.ppermute(following, 'tm', [(i, i + 1) for i in range(tm_count - 1)])]
    pallas_call x5 -> x7, Pallas kernels: 19.5 us -> 20.6 us  [the longest x3 13.2 us: conv_parts(): pl.pallas_call(functools.partial(conv_kernel, parts, slots_of, groups), o...]
    ppermute x13, starting transfers between devices: 13.1 us -> 14 us  [xor_permute(): lax.ppermute(array, axis, [(i, i ^ bits) for i in range(lax.axis_size(axi...]
  transfers between devices with their start and end apart: 17 -> 17, of which waited for: 8 -> 6; matrix products, arithmetic and copies ran while one was open for 3% -> 3% of each run, Pallas kernels for 26% -> 24%
where the time goes in v2:
time: 73.9 us; the launch traced here: 72.9 us
  starting transfers between devices  26.1 us (35%)
  Pallas kernels  22.6 us (31%)
  waiting for transfers between devices  20.5 us (28%)
  local copies, waits for them, and re-layouts  3.45 us (5%)
    ppermute x13, waiting for transfers between devices, xor_permute(): lax.ppermute(array, axis, [(i, i ^ bits) for i in range(lax.axis_size(axi...  15.1 us
    ppermute x13, starting transfers between devices, xor_permute(): lax.ppermute(array, axis, [(i, i ^ bits) for i in range(lax.axis_size(axi...  14 us
    pallas_call x3, Pallas kernels, conv_parts(): pl.pallas_call(functools.partial(conv_kernel, parts, slots_of, groups), o...  13.2 us
    pallas_call x2, Pallas kernels, last_part(): pl.pallas_call(functools.partial(last_kernel, slot, far), out_shape=jax.S...  6.24 us
    ppermute x1, starting transfers between devices, shards(): lax.ppermute(following, 'tm', [(i, i + 1) for i in range(tm_count - 1)])  5.36 us
    ppermute x1, waiting for transfers between devices, shards(): far_in = lax.ppermute(far, 'tm', swapped_pairs(1))  3.57 us
    ppermute x1, starting transfers between devices, shards(): lax.ppermute(second[half:], ('tm', 'chan'), [(t * chan_count + (c ^ 1), (...  3.37 us
    ppermute x1, starting transfers between devices, shards(): far_in = lax.ppermute(far, 'tm', swapped_pairs(1))  3.31 us
  transfers between devices with their start and end apart: 17, of which 6 were waited for; matrix products, arithmetic and copies ran while one was open for 3% of the time, Pallas kernels for 24%

profile of v2, /device:TPU:3, one launch (start us, length us, event | category | flops | bytes accessed | tf_op | source)
XLA Modules:
  0.0 72.9 jit_solution(1491057117693025337)
XLA Ops:
  0.0 1.0 %constant_dynamic-slice_fusion.1 = (bf16[27,16,128]{2,1,0:T(8,128)(2,1)S(1)}, bf16[27,16,128]{2,1,0:T(8,128)(2,1)S(1)}, bf16[27,16,128]{2,1,0:T(8,128)(2,1)S(1)}) fusion(bf16[27,512,128]{2,1,0:T(8,128)(2,1)} %bitcast.20, s32[]{:T(128)S(6)} %select_n.22, s32[]{:T(128)S(6)} %select_n.21, s32[]{:T(128)S(6)} %select_n.20), kind=kLoop, calls=%fused_computation.3 | loop fusion | bytes 663564 | tf_op jit(solution)/shard_map/dynamic_slice | solution.py:348
  1.1 1.4 %collective-permute-start = (bf16[27,16,128]{2,1,0:T(8,128)(2,1)S(1)}, bf16[27,16,128]{2,1,0:T(8,128)(2,1)S(1)}, u32[]{:S(2)}, u32[]{:S(2)}) collective-permute-start(bf16[27,16,128]{2,1,0:T(8,128)(2,1)S(1)} %get-tuple-element.23), channel_id=1, source_target_pairs={{0,1},{1,0},{2,3},{3,2},{4,5},{5,4},{6,7},{7,6},{8,9},{9,8},{10,11... | collective-permute-start | bytes 331784 | tf_op jit(solution)/shard_map/ppermute | solution.py:337
  2.4 2.3 %collective-permute-start.1 = (bf16[27,16,128]{2,1,0:T(8,128)(2,1)S(1)}, bf16[27,16,128]{2,1,0:T(8,128)(2,1)S(1)}, u32[]{:S(2)}, u32[]{:S(2)}) collective-permute-start(bf16[27,16,128]{2,1,0:T(8,128)(2,1)S(1)} %get-tuple-element.26), channel_id=1, source_target_pairs={{0,2},{1,3},{2,0},{3,1},{4,6},{5,7},{6,4},{7,5},{8,10},{9,11},{10,... | collective-permute-start | bytes 331784 | tf_op jit(solution)/shard_map/ppermute | solution.py:337
  4.7 1.1 %copy.9 = bf16[128,4,512]{2,0,1:T(8,128)(2,1)S(1)} copy(bf16[128,4,512]{2,1,0:T(4,128)(2,1)} %param.6) | data formatting | bytes 1048576 | tf_op jit(solution)/shard_map/optimization_barrier | solution.py:365
  6.3 0.8 %collective-permute-done.1 = bf16[27,16,128]{2,1,0:T(8,128)(2,1)S(1)} collective-permute-done((bf16[27,16,128]{2,1,0:T(8,128)(2,1)S(1)}, bf16[27,16,128]{2,1,0:T(8,128)(2,1)S(1)}, u32[]{:S(2)}, u32[]{:S(2)}) %collective-permute-start.1) | collective-permute-done | bytes 110624 | tf_op jit(solution)/shard_map/ppermute | solution.py:337
  7.1 4.7 %collective-permute-done.2 = bf16[27,16,128]{2,1,0:T(8,128)(2,1)S(1)} collective-permute-done((bf16[27,16,128]{2,1,0:T(8,128)(2,1)S(1)}, bf16[27,16,128]{2,1,0:T(8,128)(2,1)S(1)}, u32[]{:S(2)}, u32[]{:S(2)}) %collective-permute-start.2) | collective-permute-done | bytes 110624 | tf_op jit(solution)/shard_map/ppermute | solution.py:337
  11.9 3.9 %collective-permute-start.3 = (bf16[4,128,512]{2,1,0:T(8,128)(2,1)S(1)}, bf16[4,128,512]{2,1,0:T(8,128)(2,1)S(1)}, u32[]{:S(2)}, u32[]{:S(2)}) collective-permute-start(bf16[4,128,512]{2,1,0:T(8,128)(2,1)S(1)} %bitcast.12), channel_id=1, source_target_pairs={{0,2},{1,3},{2,0},{3,1},{4,6},{5,7},{6,4},{7,5},{8,10},{9,11},{10,... | collective-permute-start | bytes 1572872 | tf_op jit(solution)/shard_map/ppermute | solution.py:337
  16.0 1.2 %collective-permute-start.7 = (bf16[3,27,16,128]{3,2,1,0:T(8,128)(2,1)S(1)}, bf16[3,27,16,128]{3,2,1,0:T(8,128)(2,1)S(1)}, u32[]{:S(2)}, u32[]{:S(2)}) collective-permute-start(bf16[3,27,16,128]{3,2,1,0:T(8,128)(2,1)S(1)} %pad_maximum_fusion.refs_3_), channel_id=1, source_target_pairs={{0,16},{4,20},{8,24},{12,28},{16,0},{20,4},{24,8},{28,12},{1,17},{... | collective-permute-start | bytes 995336 | tf_op jit(solution)/shard_map/ppermute | solution.py:337
  17.3 1.2 %collective-permute-start.8 = (bf16[3,27,16,128]{3,2,1,0:T(8,128)(2,1)S(1)}, bf16[3,27,16,128]{3,2,1,0:T(8,128)(2,1)S(1)}, u32[]{:S(2)}, u32[]{:S(2)}) collective-permute-start(bf16[3,27,16,128]{3,2,1,0:T(8,128)(2,1)S(1)} %pad_maximum_fusion.refs_3_), channel_id=1, source_target_pairs={{0,24},{4,28},{8,16},{12,20},{16,8},{20,12},{24,0},{28,4},{1,25},{... | collective-permute-start | bytes 995336 | tf_op jit(solution)/shard_map/ppermute | solution.py:337
  18.4 1.2 %constant_dynamic-slice_fusion.refs_2_ = bf16[27,128,128]{2,1,0:T(8,128)(2,1)S(1)} fusion(bf16[27,512,128]{2,1,0:T(8,128)(2,1)} %bitcast.21, s32[]{:T(128)S(6)} %select_n.23), kind=kLoop, calls=%fused_computation.2 | loop fusion | bytes 1769476 | tf_op jit(solution)/shard_map/dynamic_slice | solution.py:355
  19.7 5.0 %conv_parts.3 = (f32[4,128,512]{2,1,0:T(8,128)S(1)}, f32[2,128,512]{2,1,0:T(8,128)S(1)}) custom-call(s32[12]{0:T(128)S(1)} %copy-done, bf16[4,128,512]{2,1,0:T(8,128)(2,1)S(1)} %bitcast.13, bf16[27,128,128]{2,1,0:T(8,128)(2,1)S(1)} %constant_dynamic-slice_fusion.refs_2_), custom_call_target="tpu_custom_call" | custom-call | flops 1024 | bytes 1024 | tf_op jit(solution)/shard_map/conv_parts/pallas_call | solution.py:170
  24.7 6.6 %collective-permute-done.8.refs_9_ = bf16[3,27,16,128]{3,2,1,0:T(8,128)(2,1)S(1)} collective-permute-done((bf16[3,27,16,128]{3,2,1,0:T(8,128)(2,1)S(1)}, bf16[3,27,16,128]{3,2,1,0:T(8,128)(2,1)S(1)}, u32[]{:S(2)}, u32[]{:S(2)}) %collective-permute-start.8) | collective-permute-done | bytes 331808 | tf_op jit(solution)/shard_map/ppermute | solution.py:337
  31.3 2.8 %collective-permute-start.10 = (bf16[3,27,16,128]{3,2,1,0:T(8,128)(2,1)S(1)}, bf16[3,27,16,128]{3,2,1,0:T(8,128)(2,1)S(1)}, u32[]{:S(2)}, u32[]{:S(2)}) collective-permute-start(bf16[3,27,16,128]{3,2,1,0:T(8,128)(2,1)S(1)} %pad_maximum_fusion.refs_3_), channel_id=1, source_target_pairs={{0,4},{4,0},{8,12},{12,8},{16,20},{20,16},{24,28},{28,24},{1,5},{5... | collective-permute-start | bytes 995336 | tf_op jit(solution)/shard_map/ppermute | solution.py:337
  34.6 3.0 %collective-permute-done.3.refs_2_ = bf16[4,128,512]{2,1,0:T(8,128)(2,1)S(1)} collective-permute-done((bf16[4,128,512]{2,1,0:T(8,128)(2,1)S(1)}, bf16[4,128,512]{2,1,0:T(8,128)(2,1)S(1)}, u32[]{:S(2)}, u32[]{:S(2)}) %collective-permute-start.3) | collective-permute-done | bytes 524320 | tf_op jit(solution)/shard_map/ppermute | solution.py:337
  37.6 2.1 %conv_parts.5 = f32[2,128,512]{2,1,0:T(8,128)S(1)} custom-call(s32[12]{0:T(128)S(1)} %copy-done, bf16[4,128,512]{2,1,0:T(8,128)(2,1)S(1)} %collective-permute-done.9.refs_1_, bf16[4,128,512]{2,1,0:T(8,128)(2,1)S(1)} %collective-permute-done.3.refs_2_, bf16[3,27,16,128]{3,2,1,0:T(8,128)(2,1)S(1)} %pad_maximum_fusion.refs_3_, ...), custom_call_target="tpu_custom_call" | custom-call | flops 1024 | bytes 1024 | tf_op jit(solution)/shard_map/conv_parts/pallas_call | solution.py:170
  39.7 5.4 %collective-permute-start.14 = (f32[2,128,512]{2,1,0:T(8,128)S(1)}, f32[2,128,512]{2,1,0:T(8,128)S(1)}, u32[]{:S(2)}, u32[]{:S(2)}) collective-permute-start(f32[2,128,512]{2,1,0:T(8,128)S(1)} %conv_parts.5), channel_id=1, source_target_pairs={{0,4},{4,8},{8,12},{12,16},{16,20},{20,24},{24,28},{1,5},{5,9},{9,... | collective-permute-start | bytes 1572872 | tf_op jit(solution)/shard_map/ppermute | solution.py:392
  45.1 3.4 %collective-permute-start.5 = (bf16[2,128,512]{2,1,0:T(8,128)(2,1)S(1)}, bf16[2,128,512]{2,1,0:T(8,128)(2,1)S(1)}, u32[]{:S(2)}, u32[]{:S(2)}) collective-permute-start(bf16[2,128,512]{2,1,0:T(8,128)(2,1)S(1)} %slice.4), channel_id=1, source_target_pairs={{1,4},{0,5},{3,6},{2,7},{5,8},{4,9},{7,10},{6,11},{9,12},{8,13},{1... | collective-permute-start | bytes 786440 | tf_op jit(solution)/shard_map/ppermute | solution.py:381
  48.5 6.1 %conv_parts.4.refs_11_ = f32[4,128,512]{2,1,0:T(8,128)S(1)} custom-call(s32[12]{0:T(128)S(1)} %copy-done, bf16[4,128,512]{2,1,0:T(8,128)(2,1)S(1)} %collective-permute-done.9.refs_1_, bf16[4,128,512]{2,1,0:T(8,128)(2,1)S(1)} %collective-permute-done.3.refs_2_, bf16[3,27,16,128]{3,2,1,0:T(8,128)(2,1)S(1)} %pad_maximum_fusion.refs_3_, ...), custom_call_target="tpu_custom_call" | custom-call | flops 1024 | bytes 1024 | tf_op jit(solution)/shard_map/conv_parts/pallas_call | solution.py:170
  55.0 1.8 %collective-permute-done.5.refs_2_ = bf16[2,128,512]{2,1,0:T(8,128)(2,1)S(1)} collective-permute-done((bf16[2,128,512]{2,1,0:T(8,128)(2,1)S(1)}, bf16[2,128,512]{2,1,0:T(8,128)(2,1)S(1)}, u32[]{:S(2)}, u32[]{:S(2)}) %collective-permute-start.5) | collective-permute-done | bytes 262176 | tf_op jit(solution)/shard_map/ppermute | solution.py:381
  56.8 3.0 %last_part.2.far_ref = bf16[2,128,512]{2,1,0:T(8,128)(2,1)S(1)} custom-call(s32[12]{0:T(128)S(1)} %copy-done, bf16[4,384,512]{2,1,0:T(8,128)(2,1)S(1)} %shifted_frames.1.refs_1_, bf16[2,128,512]{2,1,0:T(8,128)(2,1)S(1)} %collective-permute-done.5.refs_2_, bf16[3,27,16,128]{3,2,1,0:T(8,128)(2,1)S(1)} %pad_maximum_fusion.refs_3_, ...), custom_call_target="tpu_custom_call" | custom-call | flops 1024 | bytes 1024 | tf_op jit(solution)/shard_map/last_part/pallas_call | solution.py:253
  59.9 3.3 %collective-permute-start.15 = (bf16[2,128,512]{2,1,0:T(8,128)(2,1)S(1)}, bf16[2,128,512]{2,1,0:T(8,128)(2,1)S(1)}, u32[]{:S(2)}, u32[]{:S(2)}) collective-permute-start(bf16[2,128,512]{2,1,0:T(8,128)(2,1)S(1)} %last_part.2.far_ref), channel_id=1, source_target_pairs={{4,8},{12,16},{20,24},{8,4},{16,12},{24,20},{5,9},{13,17},{21,25},... | collective-permute-start | bytes 786440 | tf_op jit(solution)/shard_map/ppermute | solution.py:402
  63.2 3.2 %last_part.3.near_ref = bf16[2,128,512]{2,1,0:T(8,128)(2,1)S(1)} custom-call(s32[12]{0:T(128)S(1)} %copy-done, bf16[4,384,512]{2,1,0:T(8,128)(2,1)S(1)} %shifted_frames.1.refs_1_, bf16[2,128,512]{2,1,0:T(8,128)(2,1)S(1)} %collective-permute-done.5.refs_2_, bf16[3,27,16,128]{3,2,1,0:T(8,128)(2,1)S(1)} %pad_maximum_fusion.refs_3_, ...), custom_call_target="tpu_custom_call" | custom-call | flops 1024 | bytes 1024 | tf_op jit(solution)/shard_map/last_part/pallas_call | solution.py:253
  66.5 3.6 %collective-permute-done.15.far_in_ref = bf16[2,128,512]{2,1,0:T(8,128)(2,1)S(1)} collective-permute-done((bf16[2,128,512]{2,1,0:T(8,128)(2,1)S(1)}, bf16[2,128,512]{2,1,0:T(8,128)(2,1)S(1)}, u32[]{:S(2)}, u32[]{:S(2)}) %collective-permute-start.15) | collective-permute-done | bytes 262176 | tf_op jit(solution)/shard_map/ppermute | solution.py:402
  70.9 2.1 %slots.1 = bf16[128,8,512]{2,1,0:T(8,128)(2,1)} custom-call(s32[1,2]{1,0:T(1,128)S(1)} %copy-done.3, f32[8,128,512]{2,1,0:T(8,128)S(1)} %window.1.window_ref, bf16[2,128,512]{2,1,0:T(8,128)(2,1)S(1)} %collective-permute-done.16.near_in_ref), custom_call_target="tpu_custom_call" | custom-call | tf_op jit(solution)/shard_map/slots/pallas_call | solution.py:326
  (31 shorter events, 2.5 us)
Async XLA Ops:
  0.0 19.6 %copy-start = (s32[12]{0:T(128)S(1)}, s32[12]{0:T(128)}, u32[]{:S(2)}) copy-start(s32[12]{0:T(128)} %refs_0_.9) | copy-start | bytes 148
  1.1 4.8 %collective-permute-start = (bf16[27,16,128]{2,1,0:T(8,128)(2,1)S(1)}, bf16[27,16,128]{2,1,0:T(8,128)(2,1)S(1)}, u32[]{:S(2)}, u32[]{:S(2)}) collective-permute-start(bf16[27,16,128]{2,1,0:T(8,128)(2,1)S(1)} %get-tuple-element.23), channel_id=1, source_target_pairs={{0,1},{1,0},{2,3},{3,2},{4,5},{5,4},{6,7},{7,6},{8,9},{9,8},{10,11... | collective-permute-start | bytes 331784 | tf_op jit(solution)/shard_map/ppermute | solution.py:337
  2.4 4.7 %collective-permute-start.1 = (bf16[27,16,128]{2,1,0:T(8,128)(2,1)S(1)}, bf16[27,16,128]{2,1,0:T(8,128)(2,1)S(1)}, u32[]{:S(2)}, u32[]{:S(2)}) collective-permute-start(bf16[27,16,128]{2,1,0:T(8,128)(2,1)S(1)} %get-tuple-element.26), channel_id=1, source_target_pairs={{0,2},{1,3},{2,0},{3,1},{4,6},{5,7},{6,4},{7,5},{8,10},{9,11},{10,... | collective-permute-start | bytes 331784 | tf_op jit(solution)/shard_map/ppermute | solution.py:337
  4.7 7.1 %collective-permute-start.2 = (bf16[27,16,128]{2,1,0:T(8,128)(2,1)S(1)}, bf16[27,16,128]{2,1,0:T(8,128)(2,1)S(1)}, u32[]{:S(2)}, u32[]{:S(2)}) collective-permute-start(bf16[27,16,128]{2,1,0:T(8,128)(2,1)S(1)} %get-tuple-element.27), channel_id=1, source_target_pairs={{0,3},{1,2},{2,1},{3,0},{4,7},{5,6},{6,5},{7,4},{8,11},{9,10},{10,... | collective-permute-start | bytes 331784 | tf_op jit(solution)/shard_map/ppermute | solution.py:337
  5.9 25.4 %collective-permute-start.9 = (bf16[4,128,512]{2,1,0:T(8,128)(2,1)S(1)}, bf16[4,128,512]{2,1,0:T(8,128)(2,1)S(1)}, u32[]{:S(2)}, u32[]{:S(2)}) collective-permute-start(bf16[4,128,512]{2,1,0:T(8,128)(2,1)S(1)} %bitcast.11), channel_id=1, source_target_pairs={{0,1},{1,0},{2,3},{3,2},{4,5},{5,4},{6,7},{7,6},{8,9},{9,8},{10,11... | collective-permute-start | bytes 1572872 | tf_op jit(solution)/shard_map/ppermute | solution.py:337
  11.9 25.7 %collective-permute-start.3 = (bf16[4,128,512]{2,1,0:T(8,128)(2,1)S(1)}, bf16[4,128,512]{2,1,0:T(8,128)(2,1)S(1)}, u32[]{:S(2)}, u32[]{:S(2)}) collective-permute-start(bf16[4,128,512]{2,1,0:T(8,128)(2,1)S(1)} %bitcast.12), channel_id=1, source_target_pairs={{0,2},{1,3},{2,0},{3,1},{4,6},{5,7},{6,4},{7,5},{8,10},{9,11},{10,... | collective-permute-start | bytes 1572872 | tf_op jit(solution)/shard_map/ppermute | solution.py:337
  15.8 8.9 %collective-permute-start.6 = (bf16[3,27,16,128]{3,2,1,0:T(8,128)(2,1)S(1)}, bf16[3,27,16,128]{3,2,1,0:T(8,128)(2,1)S(1)}, u32[]{:S(2)}, u32[]{:S(2)}) collective-permute-start(bf16[3,27,16,128]{3,2,1,0:T(8,128)(2,1)S(1)} %pad_maximum_fusion.refs_3_), channel_id=1, source_target_pairs={{0,8},{4,12},{8,0},{12,4},{16,24},{20,28},{24,16},{28,20},{1,9},{5... | collective-permute-start | bytes 995336 | tf_op jit(solution)/shard_map/ppermute | solution.py:337
  16.0 8.6 %collective-permute-start.7 = (bf16[3,27,16,128]{3,2,1,0:T(8,128)(2,1)S(1)}, bf16[3,27,16,128]{3,2,1,0:T(8,128)(2,1)S(1)}, u32[]{:S(2)}, u32[]{:S(2)}) collective-permute-start(bf16[3,27,16,128]{3,2,1,0:T(8,128)(2,1)S(1)} %pad_maximum_fusion.refs_3_), channel_id=1, source_target_pairs={{0,16},{4,20},{8,24},{12,28},{16,0},{20,4},{24,8},{28,12},{1,17},{... | collective-permute-start | bytes 995336 | tf_op jit(solution)/shard_map/ppermute | solution.py:337
  17.3 14.0 %collective-permute-start.8 = (bf16[3,27,16,128]{3,2,1,0:T(8,128)(2,1)S(1)}, bf16[3,27,16,128]{3,2,1,0:T(8,128)(2,1)S(1)}, u32[]{:S(2)}, u32[]{:S(2)}) collective-permute-start(bf16[3,27,16,128]{3,2,1,0:T(8,128)(2,1)S(1)} %pad_maximum_fusion.refs_3_), channel_id=1, source_target_pairs={{0,24},{4,28},{8,16},{12,20},{16,8},{20,12},{24,0},{28,4},{1,25},{... | collective-permute-start | bytes 995336 | tf_op jit(solution)/shard_map/ppermute | solution.py:337
  31.3 6.3 %collective-permute-start.10 = (bf16[3,27,16,128]{3,2,1,0:T(8,128)(2,1)S(1)}, bf16[3,27,16,128]{3,2,1,0:T(8,128)(2,1)S(1)}, u32[]{:S(2)}, u32[]{:S(2)}) collective-permute-start(bf16[3,27,16,128]{3,2,1,0:T(8,128)(2,1)S(1)} %pad_maximum_fusion.refs_3_), channel_id=1, source_target_pairs={{0,4},{4,0},{8,12},{12,8},{16,20},{20,16},{24,28},{28,24},{1,5},{5... | collective-permute-start | bytes 995336 | tf_op jit(solution)/shard_map/ppermute | solution.py:337
  34.0 3.5 %collective-permute-start.11 = (bf16[3,27,16,128]{3,2,1,0:T(8,128)(2,1)S(1)}, bf16[3,27,16,128]{3,2,1,0:T(8,128)(2,1)S(1)}, u32[]{:S(2)}, u32[]{:S(2)}) collective-permute-start(bf16[3,27,16,128]{3,2,1,0:T(8,128)(2,1)S(1)} %collective-permute-done.6.refs_5_), channel_id=1, source_target_pairs={{0,4},{4,0},{8,12},{12,8},{16,20},{20,16},{24,28},{28,24},{1,5},{5... | collective-permute-start | bytes 995336 | tf_op jit(solution)/shard_map/ppermute | solution.py:337
  34.1 3.5 %collective-permute-start.12 = (bf16[3,27,16,128]{3,2,1,0:T(8,128)(2,1)S(1)}, bf16[3,27,16,128]{3,2,1,0:T(8,128)(2,1)S(1)}, u32[]{:S(2)}, u32[]{:S(2)}) collective-permute-start(bf16[3,27,16,128]{3,2,1,0:T(8,128)(2,1)S(1)} %collective-permute-done.7.refs_7_), channel_id=1, source_target_pairs={{0,4},{4,0},{8,12},{12,8},{16,20},{20,16},{24,28},{28,24},{1,5},{5... | collective-permute-start | bytes 995336 | tf_op jit(solution)/shard_map/ppermute | solution.py:337
  34.6 3.0 %collective-permute-start.13 = (bf16[3,27,16,128]{3,2,1,0:T(8,128)(2,1)S(1)}, bf16[3,27,16,128]{3,2,1,0:T(8,128)(2,1)S(1)}, u32[]{:S(2)}, u32[]{:S(2)}) collective-permute-start(bf16[3,27,16,128]{3,2,1,0:T(8,128)(2,1)S(1)} %collective-permute-done.8.refs_9_), channel_id=1, source_target_pairs={{0,4},{4,0},{8,12},{12,8},{16,20},{20,16},{24,28},{28,24},{1,5},{5... | collective-permute-start | bytes 995336 | tf_op jit(solution)/shard_map/ppermute | solution.py:337
  37.6 17.1 %collective-permute-start.4 = (bf16[4,128,512]{2,1,0:T(8,128)(2,1)S(1)}, bf16[4,128,512]{2,1,0:T(8,128)(2,1)S(1)}, u32[]{:S(2)}, u32[]{:S(2)}) collective-permute-start(bf16[4,128,512]{2,1,0:T(8,128)(2,1)S(1)} %collective-permute-done.3.refs_2_), channel_id=1, source_target_pairs={{0,1},{1,0},{2,3},{3,2},{4,5},{5,4},{6,7},{7,6},{8,9},{9,8},{10,11... | collective-permute-start | bytes 1572872 | tf_op jit(solution)/shard_map/ppermute | solution.py:337
  39.7 17.1 %collective-permute-start.14 = (f32[2,128,512]{2,1,0:T(8,128)S(1)}, f32[2,128,512]{2,1,0:T(8,128)S(1)}, u32[]{:S(2)}, u32[]{:S(2)}) collective-permute-start(f32[2,128,512]{2,1,0:T(8,128)S(1)} %conv_parts.5), channel_id=1, source_target_pairs={{0,4},{4,8},{8,12},{12,16},{16,20},{20,24},{24,28},{1,5},{5,9},{9,... | collective-permute-start | bytes 1572872 | tf_op jit(solution)/shard_map/ppermute | solution.py:392
  45.1 11.7 %collective-permute-start.5 = (bf16[2,128,512]{2,1,0:T(8,128)(2,1)S(1)}, bf16[2,128,512]{2,1,0:T(8,128)(2,1)S(1)}, u32[]{:S(2)}, u32[]{:S(2)}) collective-permute-start(bf16[2,128,512]{2,1,0:T(8,128)(2,1)S(1)} %slice.4), channel_id=1, source_target_pairs={{1,4},{0,5},{3,6},{2,7},{5,8},{4,9},{7,10},{6,11},{9,12},{8,13},{1... | collective-permute-start | bytes 786440 | tf_op jit(solution)/shard_map/ppermute | solution.py:381
  54.6 2.2 %copy-start.1 = (f32[128]{0:T(128)S(1)}, f32[128]{0:T(128)}, u32[]{:S(2)}) copy-start(f32[128]{0:T(128)} %param.8) | copy-start | bytes 1540
  54.6 2.2 %copy-start.2 = (f32[128]{0:T(128)S(1)}, f32[128]{0:T(128)}, u32[]{:S(2)}) copy-start(f32[128]{0:T(128)} %param.9) | copy-start | bytes 1540
  59.9 10.2 %copy-start.3 = (s32[1,2]{1,0:T(1,128)S(1)}, s32[1,2]{1,0:T(1,128)}, u32[]{:S(2)}) copy-start(s32[1,2]{1,0:T(1,128)} %bounds_ref.3) | copy-start | bytes 28
  59.9 10.2 %collective-permute-start.15 = (bf16[2,128,512]{2,1,0:T(8,128)(2,1)S(1)}, bf16[2,128,512]{2,1,0:T(8,128)(2,1)S(1)}, u32[]{:S(2)}, u32[]{:S(2)}) collective-permute-start(bf16[2,128,512]{2,1,0:T(8,128)(2,1)S(1)} %last_part.2.far_ref), channel_id=1, source_target_pairs={{4,8},{12,16},{20,24},{8,4},{16,12},{24,20},{5,9},{13,17},{21,25},... | collective-permute-start | bytes 786440 | tf_op jit(solution)/shard_map/ppermute | solution.py:402
  66.4 4.4 %collective-permute-start.16 = (bf16[2,128,512]{2,1,0:T(8,128)(2,1)S(1)}, bf16[2,128,512]{2,1,0:T(8,128)(2,1)S(1)}, u32[]{:S(2)}, u32[]{:S(2)}) collective-permute-start(bf16[2,128,512]{2,1,0:T(8,128)(2,1)S(1)} %last_part.3.near_ref), channel_id=1, source_target_pairs={{0,4},{8,12},{16,20},{24,28},{4,0},{12,8},{20,16},{28,24},{1,5},{9... | collective-permute-start | bytes 786440 | tf_op jit(solution)/shard_map/ppermute | solution.py:405

commit v3 on v2

--- a/solution.py
+++ b/solution.py
@@ -153,12 +153,9 @@
                     out_ref[i] = total
             continue
 
-        def one_frame(j, carry, out_ref=out_ref, sum_ref=sum_ref):
+        for j in range(frame_count):
             total = convolved(j, (0, 1, 2))
             out_ref[j] = total if sum_ref is None else total + sum_ref[j]
-            return carry
-
-        lax.fori_loop(0, frame_count, one_frame, 0)
 
 
 def conv_parts(clip_lengths, shards_in, weights, slots_of, groups, sums=()):
@@ -181,74 +178,56 @@
     )(*operands)
 
 
-def shift_kernel(frames_ref, out_ref):
-    for f in range(frames_ref.shape[0]):
+def shift_kernel(frames_ref, halo_ref, out_ref):
+    count = frames_ref.shape[0]
+    for f in range(count):
         store_shifted(out_ref, (f,), frames_ref[f])
-
-
-def shifted_frames(frames):
+    for f in range(halo_ref.shape[0]):
+        store_shifted(out_ref, (count + f,), halo_ref[f])
+
+
+def shifted_frames(frames, halo):
     count, shard, cells = frames.shape
     return pl.pallas_call(
         shift_kernel,
-        out_shape=jax.ShapeDtypeStruct((count, 3 * shard, cells), jnp.bfloat16),
-        in_specs=[pl.BlockSpec(memory_space=pltpu.VMEM)],
+        out_shape=jax.ShapeDtypeStruct((count + halo.shape[0], 3 * shard, cells), jnp.bfloat16),
+        in_specs=[pl.BlockSpec(memory_space=pltpu.VMEM)] * 2,
         out_specs=pl.BlockSpec(memory_space=pltpu.VMEM),
         compiler_params=pltpu.CompilerParams(vmem_limit_bytes=VMEM_BYTES),
         cost_estimate=pl.CostEstimate(flops=1500000000, bytes_accessed=1024, transcendentals=0),
         name="shifted_frames",
-    )(frames)
+    )(frames, halo)
 
 
 def last_kernel(slot, far, *refs):
     refs = list(refs)
-    clip_ref, shifted_ref, halo_ref = refs[:3]
-    weight_refs = refs[3 : 3 + PIECES]
-    sum_ref, arrived_ref, residual_ref, gain_ref, bias_ref = refs[3 + PIECES : 8 + PIECES]
-    out_ref, earlier_ref, total_ref = refs[8 + PIECES :]
-    frame_count = shifted_ref.shape[0]
-    half = frame_count // 2
+    clip_ref, shifted_ref = refs[:2]
+    weight_refs = refs[2 : 2 + PIECES]
+    sum_ref, arrived_ref, residual_ref, gain_ref, bias_ref = refs[2 + PIECES : 7 + PIECES]
+    out_ref, total_ref = refs[7 + PIECES :]
+    frame_count, half = residual_ref.shape[0], arrived_ref.shape[0]
     slab = lax.axis_index("tm")
     first_frame = slab * frame_count
     tail = (slab % 2 == 1) if far else (slab % 2 == 0)
     gain, bias = as_column(gain_ref[...]), as_column(bias_ref[...])
 
-    @pl.when(jnp.logical_not(tail))
-    def _():
-        for f in range(half):
-            store_shifted(earlier_ref, (f,), halo_ref[f])
-
-    @pl.when(tail)
-    def _():
-        for f in range(half):
-            earlier_ref[f] = jnp.zeros_like(earlier_ref[f])
-
-    def one_frame(i, carry):
+    for i in range(half):
         j = jnp.where(tail, i + half, i)
         g = first_frame + j
         first = clip_start(clip_ref, g)
         inputs = []
         for k in range(3):
             source = jnp.maximum(g - 2 + k, first) - first_frame
-            inputs.append(
-                jnp.where(
-                    source < 0,
-                    earlier_ref[jnp.clip(source + 2, 0, half - 1)],
-                    shifted_ref[jnp.maximum(source, 0)],
-                )
-            )
+            inputs.append(shifted_ref[jnp.where(source < 0, source + frame_count + half, source)])
         pieces = [[ref[min(slot, ref.shape[0] - 1)] for ref in weight_refs]]
         total = row_taps(pieces, inputs, (0, 1, 2)) + sum_ref[j]
-        store_in_order(total_ref, total)
-        total = total_ref[...] + jnp.where(tail, 0.0, arrived_ref[i])
+        store_in_order(total_ref.at[i], total)
+        total = total_ref[i] + jnp.where(tail, 0.0, arrived_ref[i])
         out_ref[i] = finished(total, gain, bias, residual_ref[j])
-        return carry
-
-    lax.fori_loop(0, half, one_frame, 0)
 
 
 def last_part(clip_lengths, far, slot, *operands):
-    shifted, halo = operands[:2]
-    half, shard, cells = halo.shape
+    half, shard, cells = operands[2 + PIECES].shape
     vectors = pl.BlockSpec(memory_space=pltpu.VMEM)
     return pl.pallas_call(
         functools.partial(last_kernel, slot, far),
@@ -256,8 +235,7 @@
         in_specs=[pl.BlockSpec(memory_space=pltpu.SMEM)] + [vectors] * len(operands),
         out_specs=vectors,
         scratch_shapes=[
-            pltpu.VMEM((half, 3 * shard, cells), jnp.bfloat16),
-            pltpu.VMEM((shard, cells), jnp.float32),
+            pltpu.VMEM((half, shard, cells), jnp.float32),
         ],
         compiler_params=pltpu.CompilerParams(vmem_limit_bytes=VMEM_BYTES),
         cost_estimate=pl.CostEstimate(flops=1024 if far else 1024, bytes_accessed=1024, transcendentals=0),
@@ -391,7 +369,7 @@
     (following,) = conv_parts(clip_lengths, pair, weights, slots_of, ("next",), [following])
     arrived = lax.ppermute(following, "tm", [(i, i + 1) for i in range(tm_count - 1)])
     (total,) = conv_parts(clip_lengths, pair, weights, slots_of, ("own",), [total])
-    operands = [shifted_frames(third), third_halo, *weights, total]
+    operands = [shifted_frames(third, third_halo), *weights, total]
     params = (by_frame, norm_gain.reshape(1, own), norm_bias.reshape(1, own))
 
     def swapped_pairs(start):

time: 73.9 us -> 73.8 us (level)
  waiting for transfers between devices: 20.5 us -> 26.1 us
  Pallas kernels: 22.6 us -> 19 us
  starting transfers between devices: 26.1 us -> 23.7 us
    ppermute x13, waiting for transfers between devices: 15.1 us -> 18.5 us  [xor_permute(): lax.ppermute(array, axis, [(i, i ^ bits) for i in range(lax.axis_size(axi...]
    ppermute x13, starting transfers between devices: 14 us -> 11.8 us  [xor_permute(): lax.ppermute(array, axis, [(i, i ^ bits) for i in range(lax.axis_size(axi...]
    pallas_call x3, Pallas kernels: 13.2 us -> 11.1 us  [conv_parts(): pl.pallas_call(functools.partial(conv_kernel, parts, slots_of, groups), o...]
    pallas_call x2, Pallas kernels: 6.24 us -> 4.52 us  [last_part(): pl.pallas_call(functools.partial(last_kernel, slot, far), out_shape=jax.S...]
    ppermute x1, waiting for transfers between devices: 1.82 us -> 3.07 us  [shards(): lax.ppermute(second[half:], ('tm', 'chan'), [(t * chan_count + (c ^ 1), (...]
    ppermute x1, waiting for transfers between devices: 3.57 us -> 4.51 us  [shards(): far_in = lax.ppermute(far, 'tm', swapped_pairs(1))]
  transfers between devices with their start and end apart: 17 -> 17, of which waited for: 6 -> 7; matrix products, arithmetic and copies ran while one was open for 3% -> 3% of each run, Pallas kernels for 24% -> 20%
where the time goes in v3:
time: 73.8 us; the launch traced here: 72.5 us
  waiting for transfers between devices  26.1 us (35%)
  starting transfers between devices  23.7 us (32%)
  Pallas kernels  19 us (26%)
  local copies, waits for them, and re-layouts  3.45 us (5%)
    ppermute x13, waiting for transfers between devices, xor_permute(): lax.ppermute(array, axis, [(i, i ^ bits) for i in range(lax.axis_size(axi...  18.5 us
    ppermute x13, starting transfers between devices, xor_permute(): lax.ppermute(array, axis, [(i, i ^ bits) for i in range(lax.axis_size(axi...  11.8 us
    pallas_call x3, Pallas kernels, conv_parts(): pl.pallas_call(functools.partial(conv_kernel, parts, slots_of, groups), o...  11.1 us
    ppermute x1, starting transfers between devices, shards(): lax.ppermute(following, 'tm', [(i, i + 1) for i in range(tm_count - 1)])  5.36 us
    pallas_call x2, Pallas kernels, last_part(): pl.pallas_call(functools.partial(last_kernel, slot, far), out_shape=jax.S...  4.52 us
    ppermute x1, waiting for transfers between devices, shards(): far_in = lax.ppermute(far, 'tm', swapped_pairs(1))  4.51 us
    ppermute x1, starting transfers between devices, shards(): lax.ppermute(second[half:], ('tm', 'chan'), [(t * chan_count + (c ^ 1), (...  3.37 us
    ppermute x1, starting transfers between devices, shards(): far_in = lax.ppermute(far, 'tm', swapped_pairs(1))  3.16 us
  transfers between devices with their start and end apart: 17, of which 7 were waited for; matrix products, arithmetic and copies ran while one was open for 3% of the time, Pallas kernels for 20%

profile of v3, /device:TPU:3, one launch (start us, length us, event | category | flops | bytes accessed | tf_op | source)
XLA Modules:
  0.0 72.5 jit_solution(7043315800378422401)
XLA Ops:
  0.0 1.0 %constant_dynamic-slice_fusion.1 = (bf16[27,16,128]{2,1,0:T(8,128)(2,1)S(1)}, bf16[27,16,128]{2,1,0:T(8,128)(2,1)S(1)}, bf16[27,16,128]{2,1,0:T(8,128)(2,1)S(1)}) fusion(bf16[27,512,128]{2,1,0:T(8,128)(2,1)} %bitcast.20, s32[]{:T(128)S(6)} %select_n.22, s32[]{:T(128)S(6)} %select_n.21, s32[]{:T(128)S(6)} %select_n.20), kind=kLoop, calls=%fused_computation.3 | loop fusion | bytes 663564 | tf_op jit(solution)/shard_map/dynamic_slice | solution.py:326
  1.1 1.4 %collective-permute-start = (bf16[27,16,128]{2,1,0:T(8,128)(2,1)S(1)}, bf16[27,16,128]{2,1,0:T(8,128)(2,1)S(1)}, u32[]{:S(2)}, u32[]{:S(2)}) collective-permute-start(bf16[27,16,128]{2,1,0:T(8,128)(2,1)S(1)} %get-tuple-element.23), channel_id=1, source_target_pairs={{0,1},{1,0},{2,3},{3,2},{4,5},{5,4},{6,7},{7,6},{8,9},{9,8},{10,11... | collective-permute-start | bytes 331784 | tf_op jit(solution)/shard_map/ppermute | solution.py:315
  2.4 2.3 %collective-permute-start.1 = (bf16[27,16,128]{2,1,0:T(8,128)(2,1)S(1)}, bf16[27,16,128]{2,1,0:T(8,128)(2,1)S(1)}, u32[]{:S(2)}, u32[]{:S(2)}) collective-permute-start(bf16[27,16,128]{2,1,0:T(8,128)(2,1)S(1)} %get-tuple-element.26), channel_id=1, source_target_pairs={{0,2},{1,3},{2,0},{3,1},{4,6},{5,7},{6,4},{7,5},{8,10},{9,11},{10,... | collective-permute-start | bytes 331784 | tf_op jit(solution)/shard_map/ppermute | solution.py:315
  4.7 1.1 %copy.9 = bf16[128,4,512]{2,0,1:T(8,128)(2,1)S(1)} copy(bf16[128,4,512]{2,1,0:T(4,128)(2,1)} %param.6) | data formatting | bytes 1048576 | tf_op jit(solution)/shard_map/optimization_barrier | solution.py:343
  6.3 0.8 %collective-permute-done.1 = bf16[27,16,128]{2,1,0:T(8,128)(2,1)S(1)} collective-permute-done((bf16[27,16,128]{2,1,0:T(8,128)(2,1)S(1)}, bf16[27,16,128]{2,1,0:T(8,128)(2,1)S(1)}, u32[]{:S(2)}, u32[]{:S(2)}) %collective-permute-start.1) | collective-permute-done | bytes 110624 | tf_op jit(solution)/shard_map/ppermute | solution.py:315
  7.1 4.7 %collective-permute-done.2 = bf16[27,16,128]{2,1,0:T(8,128)(2,1)S(1)} collective-permute-done((bf16[27,16,128]{2,1,0:T(8,128)(2,1)S(1)}, bf16[27,16,128]{2,1,0:T(8,128)(2,1)S(1)}, u32[]{:S(2)}, u32[]{:S(2)}) %collective-permute-start.2) | collective-permute-done | bytes 110624 | tf_op jit(solution)/shard_map/ppermute | solution.py:315
  11.9 3.9 %collective-permute-start.3 = (bf16[4,128,512]{2,1,0:T(8,128)(2,1)S(1)}, bf16[4,128,512]{2,1,0:T(8,128)(2,1)S(1)}, u32[]{:S(2)}, u32[]{:S(2)}) collective-permute-start(bf16[4,128,512]{2,1,0:T(8,128)(2,1)S(1)} %bitcast.12), channel_id=1, source_target_pairs={{0,2},{1,3},{2,0},{3,1},{4,6},{5,7},{6,4},{7,5},{8,10},{9,11},{10,... | collective-permute-start | bytes 1572872 | tf_op jit(solution)/shard_map/ppermute | solution.py:315
  15.8 1.2 %collective-permute-start.8 = (bf16[3,27,16,128]{3,2,1,0:T(8,128)(2,1)S(1)}, bf16[3,27,16,128]{3,2,1,0:T(8,128)(2,1)S(1)}, u32[]{:S(2)}, u32[]{:S(2)}) collective-permute-start(bf16[3,27,16,128]{3,2,1,0:T(8,128)(2,1)S(1)} %pad_maximum_fusion.refs_3_.refs_2_), channel_id=1, source_target_pairs={{0,24},{4,28},{8,16},{12,20},{16,8},{20,12},{24,0},{28,4},{1,25},{... | collective-permute-start | bytes 995336 | tf_op jit(solution)/shard_map/ppermute | solution.py:315
  17.2 1.2 %collective-permute-start.6 = (bf16[3,27,16,128]{3,2,1,0:T(8,128)(2,1)S(1)}, bf16[3,27,16,128]{3,2,1,0:T(8,128)(2,1)S(1)}, u32[]{:S(2)}, u32[]{:S(2)}) collective-permute-start(bf16[3,27,16,128]{3,2,1,0:T(8,128)(2,1)S(1)} %pad_maximum_fusion.refs_3_.refs_2_), channel_id=1, source_target_pairs={{0,8},{4,12},{8,0},{12,4},{16,24},{20,28},{24,16},{28,20},{1,9},{5... | collective-permute-start | bytes 995336 | tf_op jit(solution)/shard_map/ppermute | solution.py:315
  18.4 1.2 %constant_dynamic-slice_fusion.refs_2_ = bf16[27,128,128]{2,1,0:T(8,128)(2,1)S(1)} fusion(bf16[27,512,128]{2,1,0:T(8,128)(2,1)} %bitcast.21, s32[]{:T(128)S(6)} %select_n.23), kind=kLoop, calls=%fused_computation.2 | loop fusion | bytes 1769476 | tf_op jit(solution)/shard_map/dynamic_slice | solution.py:333
  19.7 3.8 %conv_parts.3 = (f32[4,128,512]{2,1,0:T(8,128)S(1)}, f32[2,128,512]{2,1,0:T(8,128)S(1)}) custom-call(s32[12]{0:T(128)S(1)} %copy-done, bf16[4,128,512]{2,1,0:T(8,128)(2,1)S(1)} %bitcast.13, bf16[27,128,128]{2,1,0:T(8,128)(2,1)S(1)} %constant_dynamic-slice_fusion.refs_2_), custom_call_target="tpu_custom_call" | custom-call | flops 1024 | bytes 1024 | tf_op jit(solution)/shard_map/conv_parts/pallas_call | solution.py:167
  24.2 9.3 %collective-permute-done.7.refs_7_.refs_6_ = bf16[3,27,16,128]{3,2,1,0:T(8,128)(2,1)S(1)} collective-permute-done((bf16[3,27,16,128]{3,2,1,0:T(8,128)(2,1)S(1)}, bf16[3,27,16,128]{3,2,1,0:T(8,128)(2,1)S(1)}, u32[]{:S(2)}, u32[]{:S(2)}) %collective-permute-start.7) | collective-permute-done | bytes 331808 | tf_op jit(solution)/shard_map/ppermute | solution.py:315
  34.6 2.9 %collective-permute-done.3.refs_2_ = bf16[4,128,512]{2,1,0:T(8,128)(2,1)S(1)} collective-permute-done((bf16[4,128,512]{2,1,0:T(8,128)(2,1)S(1)}, bf16[4,128,512]{2,1,0:T(8,128)(2,1)S(1)}, u32[]{:S(2)}, u32[]{:S(2)}) %collective-permute-start.3) | collective-permute-done | bytes 524320 | tf_op jit(solution)/shard_map/ppermute | solution.py:315
  37.6 2.1 %conv_parts.5 = f32[2,128,512]{2,1,0:T(8,128)S(1)} custom-call(s32[12]{0:T(128)S(1)} %copy-done, bf16[4,128,512]{2,1,0:T(8,128)(2,1)S(1)} %collective-permute-done.9.refs_1_, bf16[4,128,512]{2,1,0:T(8,128)(2,1)S(1)} %collective-permute-done.3.refs_2_, bf16[3,27,16,128]{3,2,1,0:T(8,128)(2,1)S(1)} %pad_maximum_fusion.refs_3_.refs_2_, ...), custom_call_target="tpu_custom_call" | custom-call | flops 1024 | bytes 1024 | tf_op jit(solution)/shard_map/conv_parts/pallas_call | solution.py:167
  39.7 5.4 %collective-permute-start.14 = (f32[2,128,512]{2,1,0:T(8,128)S(1)}, f32[2,128,512]{2,1,0:T(8,128)S(1)}, u32[]{:S(2)}, u32[]{:S(2)}) collective-permute-start(f32[2,128,512]{2,1,0:T(8,128)S(1)} %conv_parts.5), channel_id=1, source_target_pairs={{0,4},{4,8},{8,12},{12,16},{16,20},{20,24},{24,28},{1,5},{5,9},{9,... | collective-permute-start | bytes 1572872 | tf_op jit(solution)/shard_map/ppermute | solution.py:370
  45.1 3.4 %collective-permute-start.5 = (bf16[2,128,512]{2,1,0:T(8,128)(2,1)S(1)}, bf16[2,128,512]{2,1,0:T(8,128)(2,1)S(1)}, u32[]{:S(2)}, u32[]{:S(2)}) collective-permute-start(bf16[2,128,512]{2,1,0:T(8,128)(2,1)S(1)} %slice.4), channel_id=1, source_target_pairs={{1,4},{0,5},{3,6},{2,7},{5,8},{4,9},{7,10},{6,11},{9,12},{8,13},{1... | collective-permute-start | bytes 786440 | tf_op jit(solution)/shard_map/ppermute | solution.py:359
  48.5 5.2 %conv_parts.4.refs_10_ = f32[4,128,512]{2,1,0:T(8,128)S(1)} custom-call(s32[12]{0:T(128)S(1)} %copy-done, bf16[4,128,512]{2,1,0:T(8,128)(2,1)S(1)} %collective-permute-done.9.refs_1_, bf16[4,128,512]{2,1,0:T(8,128)(2,1)S(1)} %collective-permute-done.3.refs_2_, bf16[3,27,16,128]{3,2,1,0:T(8,128)(2,1)S(1)} %pad_maximum_fusion.refs_3_.refs_2_, ...), custom_call_target="tpu_custom_call" | custom-call | flops 1024 | bytes 1024 | tf_op jit(solution)/shard_map/conv_parts/pallas_call | solution.py:167
  53.8 3.1 %collective-permute-done.5.halo_ref = bf16[2,128,512]{2,1,0:T(8,128)(2,1)S(1)} collective-permute-done((bf16[2,128,512]{2,1,0:T(8,128)(2,1)S(1)}, bf16[2,128,512]{2,1,0:T(8,128)(2,1)S(1)}, u32[]{:S(2)}, u32[]{:S(2)}) %collective-permute-start.5) | collective-permute-done | bytes 262176 | tf_op jit(solution)/shard_map/ppermute | solution.py:359
  57.4 2.2 %last_part.2.far_ref = bf16[2,128,512]{2,1,0:T(8,128)(2,1)S(1)} custom-call(s32[12]{0:T(128)S(1)} %copy-done, bf16[6,384,512]{2,1,0:T(8,128)(2,1)S(1)} %shifted_frames.1.refs_1_, bf16[3,27,16,128]{3,2,1,0:T(8,128)(2,1)S(1)} %pad_maximum_fusion.refs_3_.refs_2_, bf16[3,27,16,128]{3,2,1,0:T(8,128)(2,1)S(1)} %collective-permute-done.10.refs_4_.refs_3_, ...), custom_call_target="tpu_custom_call" | custom-call | flops 1024 | bytes 1024 | tf_op jit(solution)/shard_map/last_part/pallas_call | solution.py:232
  59.6 3.2 %collective-permute-start.15 = (bf16[2,128,512]{2,1,0:T(8,128)(2,1)S(1)}, bf16[2,128,512]{2,1,0:T(8,128)(2,1)S(1)}, u32[]{:S(2)}, u32[]{:S(2)}) collective-permute-start(bf16[2,128,512]{2,1,0:T(8,128)(2,1)S(1)} %last_part.2.far_ref), channel_id=1, source_target_pairs={{4,8},{12,16},{20,24},{8,4},{16,12},{24,20},{5,9},{13,17},{21,25},... | collective-permute-start | bytes 786440 | tf_op jit(solution)/shard_map/ppermute | solution.py:380
  62.8 2.3 %last_part.3.near_ref = bf16[2,128,512]{2,1,0:T(8,128)(2,1)S(1)} custom-call(s32[12]{0:T(128)S(1)} %copy-done, bf16[6,384,512]{2,1,0:T(8,128)(2,1)S(1)} %shifted_frames.1.refs_1_, bf16[3,27,16,128]{3,2,1,0:T(8,128)(2,1)S(1)} %pad_maximum_fusion.refs_3_.refs_2_, bf16[3,27,16,128]{3,2,1,0:T(8,128)(2,1)S(1)} %collective-permute-done.10.refs_4_.refs_3_, ...), custom_call_target="tpu_custom_call" | custom-call | flops 1024 | bytes 1024 | tf_op jit(solution)/shard_map/last_part/pallas_call | solution.py:232
  65.1 4.5 %collective-permute-done.15.far_in_ref = bf16[2,128,512]{2,1,0:T(8,128)(2,1)S(1)} collective-permute-done((bf16[2,128,512]{2,1,0:T(8,128)(2,1)S(1)}, bf16[2,128,512]{2,1,0:T(8,128)(2,1)S(1)}, u32[]{:S(2)}, u32[]{:S(2)}) %collective-permute-start.15) | collective-permute-done | bytes 262176 | tf_op jit(solution)/shard_map/ppermute | solution.py:380
  69.7 0.7 %window.1.window_ref = f32[8,128,512]{2,1,0:T(8,128)S(1)} custom-call(s32[1,2]{1,0:T(1,128)S(1)} %copy-done.3, bf16[2,128,512]{2,1,0:T(8,128)(2,1)S(1)} %last_part.3.near_ref, bf16[2,128,512]{2,1,0:T(8,128)(2,1)S(1)} %last_part.2.far_ref, bf16[2,128,512]{2,1,0:T(8,128)(2,1)S(1)} %collective-permute-done.15.far_in_ref), custom_call_target="tpu_custom_call" | custom-call | flops 1000000000 | bytes 1024 | tf_op jit(solution)/shard_map/window/pallas_call | solution.py:295
  70.4 2.1 %slots.1 = bf16[128,8,512]{2,1,0:T(8,128)(2,1)} custom-call(s32[1,2]{1,0:T(1,128)S(1)} %copy-done.3, f32[8,128,512]{2,1,0:T(8,128)S(1)} %window.1.window_ref, bf16[2,128,512]{2,1,0:T(8,128)(2,1)S(1)} %collective-permute-done.16.near_in_ref), custom_call_target="tpu_custom_call" | custom-call | tf_op jit(solution)/shard_map/slots/pallas_call | solution.py:304
  (31 shorter events, 3.2 us)
Async XLA Ops:
  0.0 19.6 %copy-start = (s32[12]{0:T(128)S(1)}, s32[12]{0:T(128)}, u32[]{:S(2)}) copy-start(s32[12]{0:T(128)} %refs_0_.9) | copy-start | bytes 148
  1.1 4.8 %collective-permute-start = (bf16[27,16,128]{2,1,0:T(8,128)(2,1)S(1)}, bf16[27,16,128]{2,1,0:T(8,128)(2,1)S(1)}, u32[]{:S(2)}, u32[]{:S(2)}) collective-permute-start(bf16[27,16,128]{2,1,0:T(8,128)(2,1)S(1)} %get-tuple-element.23), channel_id=1, source_target_pairs={{0,1},{1,0},{2,3},{3,2},{4,5},{5,4},{6,7},{7,6},{8,9},{9,8},{10,11... | collective-permute-start | bytes 331784 | tf_op jit(solution)/shard_map/ppermute | solution.py:315
  2.4 4.7 %collective-permute-start.1 = (bf16[27,16,128]{2,1,0:T(8,128)(2,1)S(1)}, bf16[27,16,128]{2,1,0:T(8,128)(2,1)S(1)}, u32[]{:S(2)}, u32[]{:S(2)}) collective-permute-start(bf16[27,16,128]{2,1,0:T(8,128)(2,1)S(1)} %get-tuple-element.26), channel_id=1, source_target_pairs={{0,2},{1,3},{2,0},{3,1},{4,6},{5,7},{6,4},{7,5},{8,10},{9,11},{10,... | collective-permute-start | bytes 331784 | tf_op jit(solution)/shard_map/ppermute | solution.py:315
  4.7 7.1 %collective-permute-start.2 = (bf16[27,16,128]{2,1,0:T(8,128)(2,1)S(1)}, bf16[27,16,128]{2,1,0:T(8,128)(2,1)S(1)}, u32[]{:S(2)}, u32[]{:S(2)}) collective-permute-start(bf16[27,16,128]{2,1,0:T(8,128)(2,1)S(1)} %get-tuple-element.27), channel_id=1, source_target_pairs={{0,3},{1,2},{2,1},{3,0},{4,7},{5,6},{6,5},{7,4},{8,11},{9,10},{10,... | collective-permute-start | bytes 331784 | tf_op jit(solution)/shard_map/ppermute | solution.py:315
  5.9 27.6 %collective-permute-start.9 = (bf16[4,128,512]{2,1,0:T(8,128)(2,1)S(1)}, bf16[4,128,512]{2,1,0:T(8,128)(2,1)S(1)}, u32[]{:S(2)}, u32[]{:S(2)}) collective-permute-start(bf16[4,128,512]{2,1,0:T(8,128)(2,1)S(1)} %bitcast.11), channel_id=1, source_target_pairs={{0,1},{1,0},{2,3},{3,2},{4,5},{5,4},{6,7},{7,6},{8,9},{9,8},{10,11... | collective-permute-start | bytes 1572872 | tf_op jit(solution)/shard_map/ppermute | solution.py:315
  11.9 25.7 %collective-permute-start.3 = (bf16[4,128,512]{2,1,0:T(8,128)(2,1)S(1)}, bf16[4,128,512]{2,1,0:T(8,128)(2,1)S(1)}, u32[]{:S(2)}, u32[]{:S(2)}) collective-permute-start(bf16[4,128,512]{2,1,0:T(8,128)(2,1)S(1)} %bitcast.12), channel_id=1, source_target_pairs={{0,2},{1,3},{2,0},{3,1},{4,6},{5,7},{6,4},{7,5},{8,10},{9,11},{10,... | collective-permute-start | bytes 1572872 | tf_op jit(solution)/shard_map/ppermute | solution.py:315
  15.8 8.4 %collective-permute-start.8 = (bf16[3,27,16,128]{3,2,1,0:T(8,128)(2,1)S(1)}, bf16[3,27,16,128]{3,2,1,0:T(8,128)(2,1)S(1)}, u32[]{:S(2)}, u32[]{:S(2)}) collective-permute-start(bf16[3,27,16,128]{3,2,1,0:T(8,128)(2,1)S(1)} %pad_maximum_fusion.refs_3_.refs_2_), channel_id=1, source_target_pairs={{0,24},{4,28},{8,16},{12,20},{16,8},{20,12},{24,0},{28,4},{1,25},{... | collective-permute-start | bytes 995336 | tf_op jit(solution)/shard_map/ppermute | solution.py:315
  17.0 16.5 %collective-permute-start.7 = (bf16[3,27,16,128]{3,2,1,0:T(8,128)(2,1)S(1)}, bf16[3,27,16,128]{3,2,1,0:T(8,128)(2,1)S(1)}, u32[]{:S(2)}, u32[]{:S(2)}) collective-permute-start(bf16[3,27,16,128]{3,2,1,0:T(8,128)(2,1)S(1)} %pad_maximum_fusion.refs_3_.refs_2_), channel_id=1, source_target_pairs={{0,16},{4,20},{8,24},{12,28},{16,0},{20,4},{24,8},{28,12},{1,17},{... | collective-permute-start | bytes 995336 | tf_op jit(solution)/shard_map/ppermute | solution.py:315
  17.2 16.3 %collective-permute-start.6 = (bf16[3,27,16,128]{3,2,1,0:T(8,128)(2,1)S(1)}, bf16[3,27,16,128]{3,2,1,0:T(8,128)(2,1)S(1)}, u32[]{:S(2)}, u32[]{:S(2)}) collective-permute-start(bf16[3,27,16,128]{3,2,1,0:T(8,128)(2,1)S(1)} %pad_maximum_fusion.refs_3_.refs_2_), channel_id=1, source_target_pairs={{0,8},{4,12},{8,0},{12,4},{16,24},{20,28},{24,16},{28,20},{1,9},{5... | collective-permute-start | bytes 995336 | tf_op jit(solution)/shard_map/ppermute | solution.py:315
  33.5 4.1 %collective-permute-start.10 = (bf16[3,27,16,128]{3,2,1,0:T(8,128)(2,1)S(1)}, bf16[3,27,16,128]{3,2,1,0:T(8,128)(2,1)S(1)}, u32[]{:S(2)}, u32[]{:S(2)}) collective-permute-start(bf16[3,27,16,128]{3,2,1,0:T(8,128)(2,1)S(1)} %pad_maximum_fusion.refs_3_.refs_2_), channel_id=1, source_target_pairs={{0,4},{4,0},{8,12},{12,8},{16,20},{20,16},{24,28},{28,24},{1,5},{5... | collective-permute-start | bytes 995336 | tf_op jit(solution)/shard_map/ppermute | solution.py:315
  34.1 3.5 %collective-permute-start.11 = (bf16[3,27,16,128]{3,2,1,0:T(8,128)(2,1)S(1)}, bf16[3,27,16,128]{3,2,1,0:T(8,128)(2,1)S(1)}, u32[]{:S(2)}, u32[]{:S(2)}) collective-permute-start(bf16[3,27,16,128]{3,2,1,0:T(8,128)(2,1)S(1)} %collective-permute-done.6.refs_5_.refs_4_), channel_id=1, source_target_pairs={{0,4},{4,0},{8,12},{12,8},{16,20},{20,16},{24,28},{28,24},{1,5},{5... | collective-permute-start | bytes 995336 | tf_op jit(solution)/shard_map/ppermute | solution.py:315
  34.1 3.5 %collective-permute-start.12 = (bf16[3,27,16,128]{3,2,1,0:T(8,128)(2,1)S(1)}, bf16[3,27,16,128]{3,2,1,0:T(8,128)(2,1)S(1)}, u32[]{:S(2)}, u32[]{:S(2)}) collective-permute-start(bf16[3,27,16,128]{3,2,1,0:T(8,128)(2,1)S(1)} %collective-permute-done.7.refs_7_.refs_6_), channel_id=1, source_target_pairs={{0,4},{4,0},{8,12},{12,8},{16,20},{20,16},{24,28},{28,24},{1,5},{5... | collective-permute-start | bytes 995336 | tf_op jit(solution)/shard_map/ppermute | solution.py:315
  34.6 3.0 %collective-permute-start.13 = (bf16[3,27,16,128]{3,2,1,0:T(8,128)(2,1)S(1)}, bf16[3,27,16,128]{3,2,1,0:T(8,128)(2,1)S(1)}, u32[]{:S(2)}, u32[]{:S(2)}) collective-permute-start(bf16[3,27,16,128]{3,2,1,0:T(8,128)(2,1)S(1)} %collective-permute-done.8.refs_9_.refs_8_), channel_id=1, source_target_pairs={{0,4},{4,0},{8,12},{12,8},{16,20},{20,16},{24,28},{28,24},{1,5},{5... | collective-permute-start | bytes 995336 | tf_op jit(solution)/shard_map/ppermute | solution.py:315
  37.6 19.3 %collective-permute-start.4 = (bf16[4,128,512]{2,1,0:T(8,128)(2,1)S(1)}, bf16[4,128,512]{2,1,0:T(8,128)(2,1)S(1)}, u32[]{:S(2)}, u32[]{:S(2)}) collective-permute-start(bf16[4,128,512]{2,1,0:T(8,128)(2,1)S(1)} %collective-permute-done.3.refs_2_), channel_id=1, source_target_pairs={{0,1},{1,0},{2,3},{3,2},{4,5},{5,4},{6,7},{7,6},{8,9},{9,8},{10,11... | collective-permute-start | bytes 1572872 | tf_op jit(solution)/shard_map/ppermute | solution.py:315
  39.7 17.6 %collective-permute-start.14 = (f32[2,128,512]{2,1,0:T(8,128)S(1)}, f32[2,128,512]{2,1,0:T(8,128)S(1)}, u32[]{:S(2)}, u32[]{:S(2)}) collective-permute-start(f32[2,128,512]{2,1,0:T(8,128)S(1)} %conv_parts.5), channel_id=1, source_target_pairs={{0,4},{4,8},{8,12},{12,16},{16,20},{20,24},{24,28},{1,5},{5,9},{9,... | collective-permute-start | bytes 1572872 | tf_op jit(solution)/shard_map/ppermute | solution.py:370
  45.1 11.7 %collective-permute-start.5 = (bf16[2,128,512]{2,1,0:T(8,128)(2,1)S(1)}, bf16[2,128,512]{2,1,0:T(8,128)(2,1)S(1)}, u32[]{:S(2)}, u32[]{:S(2)}) collective-permute-start(bf16[2,128,512]{2,1,0:T(8,128)(2,1)S(1)} %slice.4), channel_id=1, source_target_pairs={{1,4},{0,5},{3,6},{2,7},{5,8},{4,9},{7,10},{6,11},{9,12},{8,13},{1... | collective-permute-start | bytes 786440 | tf_op jit(solution)/shard_map/ppermute | solution.py:359
  53.7 3.6 %copy-start.1 = (f32[128]{0:T(128)S(1)}, f32[128]{0:T(128)}, u32[]{:S(2)}) copy-start(f32[128]{0:T(128)} %param.8) | copy-start | bytes 1540
  53.8 3.6 %copy-start.2 = (f32[128]{0:T(128)S(1)}, f32[128]{0:T(128)}, u32[]{:S(2)}) copy-start(f32[128]{0:T(128)} %param.9) | copy-start | bytes 1540
  59.6 10.0 %copy-start.3 = (s32[1,2]{1,0:T(1,128)S(1)}, s32[1,2]{1,0:T(1,128)}, u32[]{:S(2)}) copy-start(s32[1,2]{1,0:T(1,128)} %bounds_ref.3) | copy-start | bytes 28
  59.6 10.0 %collective-permute-start.15 = (bf16[2,128,512]{2,1,0:T(8,128)(2,1)S(1)}, bf16[2,128,512]{2,1,0:T(8,128)(2,1)S(1)}, u32[]{:S(2)}, u32[]{:S(2)}) collective-permute-start(bf16[2,128,512]{2,1,0:T(8,128)(2,1)S(1)} %last_part.2.far_ref), channel_id=1, source_target_pairs={{4,8},{12,16},{20,24},{8,4},{16,12},{24,20},{5,9},{13,17},{21,25},... | collective-permute-start | bytes 786440 | tf_op jit(solution)/shard_map/ppermute | solution.py:380
  65.1 5.3 %collective-permute-start.16 = (bf16[2,128,512]{2,1,0:T(8,128)(2,1)S(1)}, bf16[2,128,512]{2,1,0:T(8,128)(2,1)S(1)}, u32[]{:S(2)}, u32[]{:S(2)}) collective-permute-start(bf16[2,128,512]{2,1,0:T(8,128)(2,1)S(1)} %last_part.3.near_ref), channel_id=1, source_target_pairs={{0,4},{8,12},{16,20},{24,28},{4,0},{12,8},{20,16},{28,24},{1,5},{9... | collective-permute-start | bytes 786440 | tf_op jit(solution)/shard_map/ppermute | solution.py:383

commit v4 on v3

--- a/solution.py
+++ b/solution.py
@@ -178,25 +178,25 @@
     )(*operands)
 
 
-def shift_kernel(frames_ref, halo_ref, out_ref):
-    count = frames_ref.shape[0]
-    for f in range(count):
-        store_shifted(out_ref, (f,), frames_ref[f])
-    for f in range(halo_ref.shape[0]):
-        store_shifted(out_ref, (count + f,), halo_ref[f])
-
-
-def shifted_frames(frames, halo):
-    count, shard, cells = frames.shape
+def shift_kernel(*refs):
+    *pair_refs, out_ref = refs
+    half = pair_refs[0].shape[0]
+    for i, pair_ref in enumerate(pair_refs):
+        for f in range(half):
+            store_shifted(out_ref, (i * half + f,), pair_ref[f])
+
+
+def shifted_frames(*pairs):
+    half, shard, cells = pairs[0].shape
     return pl.pallas_call(
         shift_kernel,
-        out_shape=jax.ShapeDtypeStruct((count + halo.shape[0], 3 * shard, cells), jnp.bfloat16),
-        in_specs=[pl.BlockSpec(memory_space=pltpu.VMEM)] * 2,
+        out_shape=jax.ShapeDtypeStruct((len(pairs) * half, 3 * shard, cells), jnp.bfloat16),
+        in_specs=[pl.BlockSpec(memory_space=pltpu.VMEM)] * len(pairs),
         out_specs=pl.BlockSpec(memory_space=pltpu.VMEM),
         compiler_params=pltpu.CompilerParams(vmem_limit_bytes=VMEM_BYTES),
         cost_estimate=pl.CostEstimate(flops=1500000000, bytes_accessed=1024, transcendentals=0),
         name="shifted_frames",
-    )(frames, halo)
+    )(*pairs)
 
 
 def last_kernel(slot, far, *refs):
@@ -354,22 +354,15 @@
     same_core, total, first = lax.optimization_barrier((same_core, total, first))
     other_core = [xor_permute(piece, "tm", 1) for piece in same_core]
     weights = [piece for pair in zip(same_core, other_core) for piece in pair]
-    third = xor_permute(second, "chan", 1)
-    chan_count = lax.axis_size("chan")
-    third_halo = lax.ppermute(
-        second[half:],
-        ("tm", "chan"),
-        [
-            (t * chan_count + (c ^ 1), (t + 1) * chan_count + c)
-            for t in range(tm_count - 1)
-            for c in range(chan_count)
-        ],
-    )
+    third_tail = xor_permute(second[half:], "chan", 1)
+    third_tail, second_head = lax.optimization_barrier((third_tail, second[:half]))
+    third_head = xor_permute(second_head, "chan", 1)
     pair, slots_of = [first, second], (0, 1)
     (following,) = conv_parts(clip_lengths, pair, weights, slots_of, ("next",), [following])
     arrived = lax.ppermute(following, "tm", [(i, i + 1) for i in range(tm_count - 1)])
+    halo = lax.ppermute(third_tail, "tm", [(i, i + 1) for i in range(tm_count - 1)])
     (total,) = conv_parts(clip_lengths, pair, weights, slots_of, ("own",), [total])
-    operands = [shifted_frames(third, third_halo), *weights, total]
+    operands = [shifted_frames(third_head, third_tail, halo), *weights, total]
     params = (by_frame, norm_gain.reshape(1, own), norm_bias.reshape(1, own))
 
     def swapped_pairs(start):

time: 73.8 us -> 72.6 us (0.984)
  waiting for transfers between devices: 26.1 us -> 23 us
  starting transfers between devices: 23.7 us -> 26.1 us
    ppermute x1, waiting for transfers between devices: 3.07 us -> 0.01 us  [shards(): lax.ppermute(third_tail, 'tm', [(i, i + 1) for i in range(tm_count - 1)])]
    ppermute x13 -> x14, starting transfers between devices: 11.8 us -> 13.6 us  [xor_permute(): lax.ppermute(array, axis, [(i, i ^ bits) for i in range(lax.axis_size(axi...]
    ppermute x1, starting transfers between devices: 3.16 us -> 4.42 us  [shards(): far_in = lax.ppermute(far, 'tm', swapped_pairs(1))]
    ppermute x13 -> x14, waiting for transfers between devices: 18.5 us -> 18.5 us  [xor_permute(): lax.ppermute(array, axis, [(i, i ^ bits) for i in range(lax.axis_size(axi...]
  transfers between devices with their start and end apart: 17 -> 18, of which waited for: 7 -> 6; matrix products, arithmetic and copies ran while one was open for 3% -> 3% of each run, Pallas kernels for 20% -> 20%
where the time goes in v4:
time: 72.6 us; the launch traced here: 71.9 us
  starting transfers between devices  26.1 us (36%)
  waiting for transfers between devices  23 us (32%)
  Pallas kernels  18.9 us (26%)
  local copies, waits for them, and re-layouts  3.58 us (5%)
    ppermute x14, waiting for transfers between devices, xor_permute(): lax.ppermute(array, axis, [(i, i ^ bits) for i in range(lax.axis_size(axi...  18.5 us
    ppermute x14, starting transfers between devices, xor_permute(): lax.ppermute(array, axis, [(i, i ^ bits) for i in range(lax.axis_size(axi...  13.6 us
    pallas_call x3, Pallas kernels, conv_parts(): pl.pallas_call(functools.partial(conv_kernel, parts, slots_of, groups), o...  11.1 us
    ppermute x1, starting transfers between devices, shards(): lax.ppermute(following, 'tm', [(i, i + 1) for i in range(tm_count - 1)])  5.36 us
    pallas_call x2, Pallas kernels, last_part(): pl.pallas_call(functools.partial(last_kernel, slot, far), out_shape=jax.S...  4.51 us
    ppermute x1, waiting for transfers between devices, shards(): far_in = lax.ppermute(far, 'tm', swapped_pairs(1))  4.5 us
    ppermute x1, starting transfers between devices, shards(): far_in = lax.ppermute(far, 'tm', swapped_pairs(1))  4.42 us
    ppermute x1, starting transfers between devices, shards(): lax.ppermute(third_tail, 'tm', [(i, i + 1) for i in range(tm_count - 1)])  2.64 us
  transfers between devices with their start and end apart: 18, of which 6 were waited for; matrix products, arithmetic and copies ran while one was open for 3% of the time, Pallas kernels for 20%

profile of v4, /device:TPU:3, one launch (start us, length us, event | category | flops | bytes accessed | tf_op | source)
XLA Modules:
  0.0 71.9 jit_solution(5095108050267138756)
XLA Ops:
  0.0 1.0 %constant_dynamic-slice_fusion.1 = (bf16[27,16,128]{2,1,0:T(8,128)(2,1)S(1)}, bf16[27,16,128]{2,1,0:T(8,128)(2,1)S(1)}, bf16[27,16,128]{2,1,0:T(8,128)(2,1)S(1)}) fusion(bf16[27,512,128]{2,1,0:T(8,128)(2,1)} %bitcast.20, s32[]{:T(128)S(6)} %select_n.22, s32[]{:T(128)S(6)} %select_n.21, s32[]{:T(128)S(6)} %select_n.20), kind=kLoop, calls=%fused_computation.3 | loop fusion | bytes 663564 | tf_op jit(solution)/shard_map/dynamic_slice | solution.py:326
  1.1 1.4 %collective-permute-start = (bf16[27,16,128]{2,1,0:T(8,128)(2,1)S(1)}, bf16[27,16,128]{2,1,0:T(8,128)(2,1)S(1)}, u32[]{:S(2)}, u32[]{:S(2)}) collective-permute-start(bf16[27,16,128]{2,1,0:T(8,128)(2,1)S(1)} %get-tuple-element.25), channel_id=1, source_target_pairs={{0,1},{1,0},{2,3},{3,2},{4,5},{5,4},{6,7},{7,6},{8,9},{9,8},{10,11... | collective-permute-start | bytes 331784 | tf_op jit(solution)/shard_map/ppermute | solution.py:315
  2.4 2.3 %collective-permute-start.1 = (bf16[27,16,128]{2,1,0:T(8,128)(2,1)S(1)}, bf16[27,16,128]{2,1,0:T(8,128)(2,1)S(1)}, u32[]{:S(2)}, u32[]{:S(2)}) collective-permute-start(bf16[27,16,128]{2,1,0:T(8,128)(2,1)S(1)} %get-tuple-element.28), channel_id=1, source_target_pairs={{0,2},{1,3},{2,0},{3,1},{4,6},{5,7},{6,4},{7,5},{8,10},{9,11},{10,... | collective-permute-start | bytes 331784 | tf_op jit(solution)/shard_map/ppermute | solution.py:315
  4.7 1.1 %copy.9 = bf16[128,4,512]{2,0,1:T(8,128)(2,1)S(1)} copy(bf16[128,4,512]{2,1,0:T(4,128)(2,1)} %param.6) | data formatting | bytes 1048576 | tf_op jit(solution)/shard_map/optimization_barrier | solution.py:343
  6.3 0.8 %collective-permute-done.1 = bf16[27,16,128]{2,1,0:T(8,128)(2,1)S(1)} collective-permute-done((bf16[27,16,128]{2,1,0:T(8,128)(2,1)S(1)}, bf16[27,16,128]{2,1,0:T(8,128)(2,1)S(1)}, u32[]{:S(2)}, u32[]{:S(2)}) %collective-permute-start.1) | collective-permute-done | bytes 110624 | tf_op jit(solution)/shard_map/ppermute | solution.py:315
  7.1 4.7 %collective-permute-done.2 = bf16[27,16,128]{2,1,0:T(8,128)(2,1)S(1)} collective-permute-done((bf16[27,16,128]{2,1,0:T(8,128)(2,1)S(1)}, bf16[27,16,128]{2,1,0:T(8,128)(2,1)S(1)}, u32[]{:S(2)}, u32[]{:S(2)}) %collective-permute-start.2) | collective-permute-done | bytes 110624 | tf_op jit(solution)/shard_map/ppermute | solution.py:315
  11.9 3.9 %collective-permute-start.3 = (bf16[4,128,512]{2,1,0:T(8,128)(2,1)S(1)}, bf16[4,128,512]{2,1,0:T(8,128)(2,1)S(1)}, u32[]{:S(2)}, u32[]{:S(2)}) collective-permute-start(bf16[4,128,512]{2,1,0:T(8,128)(2,1)S(1)} %bitcast.12), channel_id=1, source_target_pairs={{0,2},{1,3},{2,0},{3,1},{4,6},{5,7},{6,4},{7,5},{8,10},{9,11},{10,... | collective-permute-start | bytes 1572872 | tf_op jit(solution)/shard_map/ppermute | solution.py:315
  15.8 1.2 %collective-permute-start.9 = (bf16[3,27,16,128]{3,2,1,0:T(8,128)(2,1)S(1)}, bf16[3,27,16,128]{3,2,1,0:T(8,128)(2,1)S(1)}, u32[]{:S(2)}, u32[]{:S(2)}) collective-permute-start(bf16[3,27,16,128]{3,2,1,0:T(8,128)(2,1)S(1)} %pad_maximum_fusion.refs_3_.refs_2_), channel_id=1, source_target_pairs={{0,24},{4,28},{8,16},{12,20},{16,8},{20,12},{24,0},{28,4},{1,25},{... | collective-permute-start | bytes 995336 | tf_op jit(solution)/shard_map/ppermute | solution.py:315
  17.2 1.2 %collective-permute-start.7 = (bf16[3,27,16,128]{3,2,1,0:T(8,128)(2,1)S(1)}, bf16[3,27,16,128]{3,2,1,0:T(8,128)(2,1)S(1)}, u32[]{:S(2)}, u32[]{:S(2)}) collective-permute-start(bf16[3,27,16,128]{3,2,1,0:T(8,128)(2,1)S(1)} %pad_maximum_fusion.refs_3_.refs_2_), channel_id=1, source_target_pairs={{0,8},{4,12},{8,0},{12,4},{16,24},{20,28},{24,16},{28,20},{1,9},{5... | collective-permute-start | bytes 995336 | tf_op jit(solution)/shard_map/ppermute | solution.py:315
  18.4 1.2 %constant_dynamic-slice_fusion.refs_2_ = bf16[27,128,128]{2,1,0:T(8,128)(2,1)S(1)} fusion(bf16[27,512,128]{2,1,0:T(8,128)(2,1)} %bitcast.21, s32[]{:T(128)S(6)} %select_n.23), kind=kLoop, calls=%fused_computation.2 | loop fusion | bytes 1769476 | tf_op jit(solution)/shard_map/dynamic_slice | solution.py:333
  19.7 3.8 %conv_parts.3 = (f32[4,128,512]{2,1,0:T(8,128)S(1)}, f32[2,128,512]{2,1,0:T(8,128)S(1)}) custom-call(s32[12]{0:T(128)S(1)} %copy-done, bf16[4,128,512]{2,1,0:T(8,128)(2,1)S(1)} %bitcast.13, bf16[27,128,128]{2,1,0:T(8,128)(2,1)S(1)} %constant_dynamic-slice_fusion.refs_2_), custom_call_target="tpu_custom_call" | custom-call | flops 1024 | bytes 1024 | tf_op jit(solution)/shard_map/conv_parts/pallas_call | solution.py:167
  23.4 0.7 %collective-permute-done.9.refs_9_.refs_8_ = bf16[3,27,16,128]{3,2,1,0:T(8,128)(2,1)S(1)} collective-permute-done((bf16[3,27,16,128]{3,2,1,0:T(8,128)(2,1)S(1)}, bf16[3,27,16,128]{3,2,1,0:T(8,128)(2,1)S(1)}, u32[]{:S(2)}, u32[]{:S(2)}) %collective-permute-start.9) | collective-permute-done | bytes 331808 | tf_op jit(solution)/shard_map/ppermute | solution.py:315
  24.2 9.3 %collective-permute-done.8.refs_7_.refs_6_ = bf16[3,27,16,128]{3,2,1,0:T(8,128)(2,1)S(1)} collective-permute-done((bf16[3,27,16,128]{3,2,1,0:T(8,128)(2,1)S(1)}, bf16[3,27,16,128]{3,2,1,0:T(8,128)(2,1)S(1)}, u32[]{:S(2)}, u32[]{:S(2)}) %collective-permute-start.8) | collective-permute-done | bytes 331808 | tf_op jit(solution)/shard_map/ppermute | solution.py:315
  34.6 2.9 %collective-permute-done.3.refs_2_ = bf16[4,128,512]{2,1,0:T(8,128)(2,1)S(1)} collective-permute-done((bf16[4,128,512]{2,1,0:T(8,128)(2,1)S(1)}, bf16[4,128,512]{2,1,0:T(8,128)(2,1)S(1)}, u32[]{:S(2)}, u32[]{:S(2)}) %collective-permute-start.3) | collective-permute-done | bytes 524320 | tf_op jit(solution)/shard_map/ppermute | solution.py:315
  37.7 2.1 %conv_parts.5 = f32[2,128,512]{2,1,0:T(8,128)S(1)} custom-call(s32[12]{0:T(128)S(1)} %copy-done, bf16[4,128,512]{2,1,0:T(8,128)(2,1)S(1)} %collective-permute-done.10.refs_1_, bf16[4,128,512]{2,1,0:T(8,128)(2,1)S(1)} %collective-permute-done.3.refs_2_, bf16[3,27,16,128]{3,2,1,0:T(8,128)(2,1)S(1)} %pad_maximum_fusion.refs_3_.refs_2_, ...), custom_call_target="tpu_custom_call" | custom-call | flops 1024 | bytes 1024 | tf_op jit(solution)/shard_map/conv_parts/pallas_call | solution.py:167
  39.9 5.4 %collective-permute-start.15 = (f32[2,128,512]{2,1,0:T(8,128)S(1)}, f32[2,128,512]{2,1,0:T(8,128)S(1)}, u32[]{:S(2)}, u32[]{:S(2)}) collective-permute-start(f32[2,128,512]{2,1,0:T(8,128)S(1)} %conv_parts.5), channel_id=1, source_target_pairs={{0,4},{4,8},{8,12},{12,16},{16,20},{20,24},{24,28},{1,5},{5,9},{9,... | collective-permute-start | bytes 1572872 | tf_op jit(solution)/shard_map/ppermute | solution.py:362
  45.2 1.8 %collective-permute-start.5 = (bf16[2,128,512]{2,1,0:T(8,128)(2,1)S(1)}, bf16[2,128,512]{2,1,0:T(8,128)(2,1)S(1)}, u32[]{:S(2)}, u32[]{:S(2)}) collective-permute-start(bf16[2,128,512]{2,1,0:T(8,128)(2,1)S(1)} %get-tuple-element.32), channel_id=1, source_target_pairs={{0,1},{1,0},{2,3},{3,2},{4,5},{5,4},{6,7},{7,6},{8,9},{9,8},{10,11... | collective-permute-start | bytes 786440 | tf_op jit(solution)/shard_map/ppermute | solution.py:315
  47.0 2.6 %collective-permute-start.6 = (bf16[2,128,512]{2,1,0:T(8,128)(2,1)S(1)}, bf16[2,128,512]{2,1,0:T(8,128)(2,1)S(1)}, u32[]{:S(2)}, u32[]{:S(2)}) collective-permute-start(bf16[2,128,512]{2,1,0:T(8,128)(2,1)S(1)} %collective-permute-done.4.refs_1_), channel_id=1, source_target_pairs={{0,4},{4,8},{8,12},{12,16},{16,20},{20,24},{24,28},{1,5},{5,9},{9,... | collective-permute-start | bytes 786440 | tf_op jit(solution)/shard_map/ppermute | solution.py:363
  49.7 5.2 %conv_parts.4.refs_10_ = f32[4,128,512]{2,1,0:T(8,128)S(1)} custom-call(s32[12]{0:T(128)S(1)} %copy-done, bf16[4,128,512]{2,1,0:T(8,128)(2,1)S(1)} %collective-permute-done.10.refs_1_, bf16[4,128,512]{2,1,0:T(8,128)(2,1)S(1)} %collective-permute-done.3.refs_2_, bf16[3,27,16,128]{3,2,1,0:T(8,128)(2,1)S(1)} %pad_maximum_fusion.refs_3_.refs_2_, ...), custom_call_target="tpu_custom_call" | custom-call | flops 1024 | bytes 1024 | tf_op jit(solution)/shard_map/conv_parts/pallas_call | solution.py:167
  55.6 2.2 %last_part.2.far_ref = bf16[2,128,512]{2,1,0:T(8,128)(2,1)S(1)} custom-call(s32[12]{0:T(128)S(1)} %copy-done, bf16[6,384,512]{2,1,0:T(8,128)(2,1)S(1)} %shifted_frames.1.refs_1_, bf16[3,27,16,128]{3,2,1,0:T(8,128)(2,1)S(1)} %pad_maximum_fusion.refs_3_.refs_2_, bf16[3,27,16,128]{3,2,1,0:T(8,128)(2,1)S(1)} %collective-permute-done.11.refs_4_.refs_3_, ...), custom_call_target="tpu_custom_call" | custom-call | flops 1024 | bytes 1024 | tf_op jit(solution)/shard_map/last_part/pallas_call | solution.py:232
  57.8 4.4 %collective-permute-start.16 = (bf16[2,128,512]{2,1,0:T(8,128)(2,1)S(1)}, bf16[2,128,512]{2,1,0:T(8,128)(2,1)S(1)}, u32[]{:S(2)}, u32[]{:S(2)}) collective-permute-start(bf16[2,128,512]{2,1,0:T(8,128)(2,1)S(1)} %last_part.2.far_ref), channel_id=1, source_target_pairs={{4,8},{12,16},{20,24},{8,4},{16,12},{24,20},{5,9},{13,17},{21,25},... | collective-permute-start | bytes 786440 | tf_op jit(solution)/shard_map/ppermute | solution.py:373
  62.3 2.3 %last_part.3.near_ref = bf16[2,128,512]{2,1,0:T(8,128)(2,1)S(1)} custom-call(s32[12]{0:T(128)S(1)} %copy-done, bf16[6,384,512]{2,1,0:T(8,128)(2,1)S(1)} %shifted_frames.1.refs_1_, bf16[3,27,16,128]{3,2,1,0:T(8,128)(2,1)S(1)} %pad_maximum_fusion.refs_3_.refs_2_, bf16[3,27,16,128]{3,2,1,0:T(8,128)(2,1)S(1)} %collective-permute-done.11.refs_4_.refs_3_, ...), custom_call_target="tpu_custom_call" | custom-call | flops 1024 | bytes 1024 | tf_op jit(solution)/shard_map/last_part/pallas_call | solution.py:232
  64.6 4.5 %collective-permute-done.16.far_in_ref = bf16[2,128,512]{2,1,0:T(8,128)(2,1)S(1)} collective-permute-done((bf16[2,128,512]{2,1,0:T(8,128)(2,1)S(1)}, bf16[2,128,512]{2,1,0:T(8,128)(2,1)S(1)}, u32[]{:S(2)}, u32[]{:S(2)}) %collective-permute-start.16) | collective-permute-done | bytes 262176 | tf_op jit(solution)/shard_map/ppermute | solution.py:373
  69.9 2.1 %slots.1 = bf16[128,8,512]{2,1,0:T(8,128)(2,1)} custom-call(s32[1,2]{1,0:T(1,128)S(1)} %copy-done.3, f32[8,128,512]{2,1,0:T(8,128)S(1)} %window.1.window_ref, bf16[2,128,512]{2,1,0:T(8,128)(2,1)S(1)} %collective-permute-done.17.near_in_ref), custom_call_target="tpu_custom_call" | custom-call | tf_op jit(solution)/shard_map/slots/pallas_call | solution.py:304
  (33 shorter events, 3.4 us)
Async XLA Ops:
  0.0 19.6 %copy-start = (s32[12]{0:T(128)S(1)}, s32[12]{0:T(128)}, u32[]{:S(2)}) copy-start(s32[12]{0:T(128)} %refs_0_.9) | copy-start | bytes 148
  1.1 4.8 %collective-permute-start = (bf16[27,16,128]{2,1,0:T(8,128)(2,1)S(1)}, bf16[27,16,128]{2,1,0:T(8,128)(2,1)S(1)}, u32[]{:S(2)}, u32[]{:S(2)}) collective-permute-start(bf16[27,16,128]{2,1,0:T(8,128)(2,1)S(1)} %get-tuple-element.25), channel_id=1, source_target_pairs={{0,1},{1,0},{2,3},{3,2},{4,5},{5,4},{6,7},{7,6},{8,9},{9,8},{10,11... | collective-permute-start | bytes 331784 | tf_op jit(solution)/shard_map/ppermute | solution.py:315
  2.4 4.7 %collective-permute-start.1 = (bf16[27,16,128]{2,1,0:T(8,128)(2,1)S(1)}, bf16[27,16,128]{2,1,0:T(8,128)(2,1)S(1)}, u32[]{:S(2)}, u32[]{:S(2)}) collective-permute-start(bf16[27,16,128]{2,1,0:T(8,128)(2,1)S(1)} %get-tuple-element.28), channel_id=1, source_target_pairs={{0,2},{1,3},{2,0},{3,1},{4,6},{5,7},{6,4},{7,5},{8,10},{9,11},{10,... | collective-permute-start | bytes 331784 | tf_op jit(solution)/shard_map/ppermute | solution.py:315
  4.7 7.1 %collective-permute-start.2 = (bf16[27,16,128]{2,1,0:T(8,128)(2,1)S(1)}, bf16[27,16,128]{2,1,0:T(8,128)(2,1)S(1)}, u32[]{:S(2)}, u32[]{:S(2)}) collective-permute-start(bf16[27,16,128]{2,1,0:T(8,128)(2,1)S(1)} %get-tuple-element.29), channel_id=1, source_target_pairs={{0,3},{1,2},{2,1},{3,0},{4,7},{5,6},{6,5},{7,4},{8,11},{9,10},{10,... | collective-permute-start | bytes 331784 | tf_op jit(solution)/shard_map/ppermute | solution.py:315
  5.9 27.6 %collective-permute-start.10 = (bf16[4,128,512]{2,1,0:T(8,128)(2,1)S(1)}, bf16[4,128,512]{2,1,0:T(8,128)(2,1)S(1)}, u32[]{:S(2)}, u32[]{:S(2)}) collective-permute-start(bf16[4,128,512]{2,1,0:T(8,128)(2,1)S(1)} %bitcast.11), channel_id=1, source_target_pairs={{0,1},{1,0},{2,3},{3,2},{4,5},{5,4},{6,7},{7,6},{8,9},{9,8},{10,11... | collective-permute-start | bytes 1572872 | tf_op jit(solution)/shard_map/ppermute | solution.py:315
  11.9 25.7 %collective-permute-start.3 = (bf16[4,128,512]{2,1,0:T(8,128)(2,1)S(1)}, bf16[4,128,512]{2,1,0:T(8,128)(2,1)S(1)}, u32[]{:S(2)}, u32[]{:S(2)}) collective-permute-start(bf16[4,128,512]{2,1,0:T(8,128)(2,1)S(1)} %bitcast.12), channel_id=1, source_target_pairs={{0,2},{1,3},{2,0},{3,1},{4,6},{5,7},{6,4},{7,5},{8,10},{9,11},{10,... | collective-permute-start | bytes 1572872 | tf_op jit(solution)/shard_map/ppermute | solution.py:315
  15.8 8.4 %collective-permute-start.9 = (bf16[3,27,16,128]{3,2,1,0:T(8,128)(2,1)S(1)}, bf16[3,27,16,128]{3,2,1,0:T(8,128)(2,1)S(1)}, u32[]{:S(2)}, u32[]{:S(2)}) collective-permute-start(bf16[3,27,16,128]{3,2,1,0:T(8,128)(2,1)S(1)} %pad_maximum_fusion.refs_3_.refs_2_), channel_id=1, source_target_pairs={{0,24},{4,28},{8,16},{12,20},{16,8},{20,12},{24,0},{28,4},{1,25},{... | collective-permute-start | bytes 995336 | tf_op jit(solution)/shard_map/ppermute | solution.py:315
  17.0 16.5 %collective-permute-start.8 = (bf16[3,27,16,128]{3,2,1,0:T(8,128)(2,1)S(1)}, bf16[3,27,16,128]{3,2,1,0:T(8,128)(2,1)S(1)}, u32[]{:S(2)}, u32[]{:S(2)}) collective-permute-start(bf16[3,27,16,128]{3,2,1,0:T(8,128)(2,1)S(1)} %pad_maximum_fusion.refs_3_.refs_2_), channel_id=1, source_target_pairs={{0,16},{4,20},{8,24},{12,28},{16,0},{20,4},{24,8},{28,12},{1,17},{... | collective-permute-start | bytes 995336 | tf_op jit(solution)/shard_map/ppermute | solution.py:315
  17.2 16.3 %collective-permute-start.7 = (bf16[3,27,16,128]{3,2,1,0:T(8,128)(2,1)S(1)}, bf16[3,27,16,128]{3,2,1,0:T(8,128)(2,1)S(1)}, u32[]{:S(2)}, u32[]{:S(2)}) collective-permute-start(bf16[3,27,16,128]{3,2,1,0:T(8,128)(2,1)S(1)} %pad_maximum_fusion.refs_3_.refs_2_), channel_id=1, source_target_pairs={{0,8},{4,12},{8,0},{12,4},{16,24},{20,28},{24,16},{28,20},{1,9},{5... | collective-permute-start | bytes 995336 | tf_op jit(solution)/shard_map/ppermute | solution.py:315
  33.5 4.2 %collective-permute-start.11 = (bf16[3,27,16,128]{3,2,1,0:T(8,128)(2,1)S(1)}, bf16[3,27,16,128]{3,2,1,0:T(8,128)(2,1)S(1)}, u32[]{:S(2)}, u32[]{:S(2)}) collective-permute-start(bf16[3,27,16,128]{3,2,1,0:T(8,128)(2,1)S(1)} %pad_maximum_fusion.refs_3_.refs_2_), channel_id=1, source_target_pairs={{0,4},{4,0},{8,12},{12,8},{16,20},{20,16},{24,28},{28,24},{1,5},{5... | collective-permute-start | bytes 995336 | tf_op jit(solution)/shard_map/ppermute | solution.py:315
  34.1 3.6 %collective-permute-start.12 = (bf16[3,27,16,128]{3,2,1,0:T(8,128)(2,1)S(1)}, bf16[3,27,16,128]{3,2,1,0:T(8,128)(2,1)S(1)}, u32[]{:S(2)}, u32[]{:S(2)}) collective-permute-start(bf16[3,27,16,128]{3,2,1,0:T(8,128)(2,1)S(1)} %collective-permute-done.7.refs_5_.refs_4_), channel_id=1, source_target_pairs={{0,4},{4,0},{8,12},{12,8},{16,20},{20,16},{24,28},{28,24},{1,5},{5... | collective-permute-start | bytes 995336 | tf_op jit(solution)/shard_map/ppermute | solution.py:315
  34.1 3.6 %collective-permute-start.13 = (bf16[3,27,16,128]{3,2,1,0:T(8,128)(2,1)S(1)}, bf16[3,27,16,128]{3,2,1,0:T(8,128)(2,1)S(1)}, u32[]{:S(2)}, u32[]{:S(2)}) collective-permute-start(bf16[3,27,16,128]{3,2,1,0:T(8,128)(2,1)S(1)} %collective-permute-done.8.refs_7_.refs_6_), channel_id=1, source_target_pairs={{0,4},{4,0},{8,12},{12,8},{16,20},{20,16},{24,28},{28,24},{1,5},{5... | collective-permute-start | bytes 995336 | tf_op jit(solution)/shard_map/ppermute | solution.py:315
  34.6 3.1 %collective-permute-start.14 = (bf16[3,27,16,128]{3,2,1,0:T(8,128)(2,1)S(1)}, bf16[3,27,16,128]{3,2,1,0:T(8,128)(2,1)S(1)}, u32[]{:S(2)}, u32[]{:S(2)}) collective-permute-start(bf16[3,27,16,128]{3,2,1,0:T(8,128)(2,1)S(1)} %collective-permute-done.9.refs_9_.refs_8_), channel_id=1, source_target_pairs={{0,4},{4,0},{8,12},{12,8},{16,20},{20,16},{24,28},{28,24},{1,5},{5... | collective-permute-start | bytes 995336 | tf_op jit(solution)/shard_map/ppermute | solution.py:315
  37.6 7.6 %collective-permute-start.4 = (bf16[2,128,512]{2,1,0:T(8,128)(2,1)S(1)}, bf16[2,128,512]{2,1,0:T(8,128)(2,1)S(1)}, u32[]{:S(2)}, u32[]{:S(2)}) collective-permute-start(bf16[2,128,512]{2,1,0:T(8,128)(2,1)S(1)} %get-tuple-element.49), channel_id=1, source_target_pairs={{0,1},{1,0},{2,3},{3,2},{4,5},{5,4},{6,7},{7,6},{8,9},{9,8},{10,11... | collective-permute-start | bytes 786440 | tf_op jit(solution)/shard_map/ppermute | solution.py:315
  39.9 15.6 %collective-permute-start.15 = (f32[2,128,512]{2,1,0:T(8,128)S(1)}, f32[2,128,512]{2,1,0:T(8,128)S(1)}, u32[]{:S(2)}, u32[]{:S(2)}) collective-permute-start(f32[2,128,512]{2,1,0:T(8,128)S(1)} %conv_parts.5), channel_id=1, source_target_pairs={{0,4},{4,8},{8,12},{12,16},{16,20},{20,24},{24,28},{1,5},{5,9},{9,... | collective-permute-start | bytes 1572872 | tf_op jit(solution)/shard_map/ppermute | solution.py:362
  45.2 9.7 %collective-permute-start.5 = (bf16[2,128,512]{2,1,0:T(8,128)(2,1)S(1)}, bf16[2,128,512]{2,1,0:T(8,128)(2,1)S(1)}, u32[]{:S(2)}, u32[]{:S(2)}) collective-permute-start(bf16[2,128,512]{2,1,0:T(8,128)(2,1)S(1)} %get-tuple-element.32), channel_id=1, source_target_pairs={{0,1},{1,0},{2,3},{3,2},{4,5},{5,4},{6,7},{7,6},{8,9},{9,8},{10,11... | collective-permute-start | bytes 786440 | tf_op jit(solution)/shard_map/ppermute | solution.py:315
  47.0 7.9 %collective-permute-start.6 = (bf16[2,128,512]{2,1,0:T(8,128)(2,1)S(1)}, bf16[2,128,512]{2,1,0:T(8,128)(2,1)S(1)}, u32[]{:S(2)}, u32[]{:S(2)}) collective-permute-start(bf16[2,128,512]{2,1,0:T(8,128)(2,1)S(1)} %collective-permute-done.4.refs_1_), channel_id=1, source_target_pairs={{0,4},{4,8},{8,12},{12,16},{16,20},{20,24},{24,28},{1,5},{5,9},{9,... | collective-permute-start | bytes 786440 | tf_op jit(solution)/shard_map/ppermute | solution.py:363
  54.9 0.7 copy-start.1
  54.9 0.7 copy-start.2
  57.8 11.3 %copy-start.3 = (s32[1,2]{1,0:T(1,128)S(1)}, s32[1,2]{1,0:T(1,128)}, u32[]{:S(2)}) copy-start(s32[1,2]{1,0:T(1,128)} %bounds_ref.3) | copy-start | bytes 28
  57.8 11.3 %collective-permute-start.16 = (bf16[2,128,512]{2,1,0:T(8,128)(2,1)S(1)}, bf16[2,128,512]{2,1,0:T(8,128)(2,1)S(1)}, u32[]{:S(2)}, u32[]{:S(2)}) collective-permute-start(bf16[2,128,512]{2,1,0:T(8,128)(2,1)S(1)} %last_part.2.far_ref), channel_id=1, source_target_pairs={{4,8},{12,16},{20,24},{8,4},{16,12},{24,20},{5,9},{13,17},{21,25},... | collective-permute-start | bytes 786440 | tf_op jit(solution)/shard_map/ppermute | solution.py:373
  64.5 5.3 %collective-permute-start.17 = (bf16[2,128,512]{2,1,0:T(8,128)(2,1)S(1)}, bf16[2,128,512]{2,1,0:T(8,128)(2,1)S(1)}, u32[]{:S(2)}, u32[]{:S(2)}) collective-permute-start(bf16[2,128,512]{2,1,0:T(8,128)(2,1)S(1)} %last_part.3.near_ref), channel_id=1, source_target_pairs={{0,4},{8,12},{16,20},{24,28},{4,0},{12,8},{20,16},{28,24},{1,5},{9... | collective-permute-start | bytes 786440 | tf_op jit(solution)/shard_map/ppermute | solution.py:376

commit v5 on v4

--- a/solution.py
+++ b/solution.py
@@ -16,6 +16,7 @@
 PIECES = 8
 TAPS = 27
 LANES = 128
+STAGE = 32
 VMEM_BYTES = 9 * 1024 * 1024
 
 norm_eps = 1e-06
@@ -271,12 +272,13 @@
             out_ref[slot] = jnp.zeros_like(out_ref[slot])
 
 
-def slots_kernel(bounds_ref, window_ref, near_in_ref, out_ref):
+def slots_kernel(bounds_ref, window_ref, near_in_ref, out_ref, staged_ref, sent_sem):
     capacity, channels, _ = window_ref.shape
     half = near_in_ref.shape[0]
     position = near_position(0, half)
     slot, size = slot_of(bounds_ref, 2 * half, position)
     rows = 16
+    copies = []
     for start in range(0, channels, rows):
         frames = [window_ref[w, start : start + rows, :] for w in range(capacity)]
         for i in range(half):
@@ -284,7 +286,17 @@
             for w in range(capacity):
                 frames[w] = jnp.where((slot + i == w) & (w < size), frame, frames[w])
         block = jnp.stack(frames)
-        out_ref[start : start + rows] = jnp.swapaxes(block, 0, 1).astype(jnp.bfloat16)
+        staged_ref[start : start + rows] = jnp.swapaxes(block, 0, 1).astype(jnp.bfloat16)
+        if (start + rows) % STAGE == 0:
+            part = pl.ds(start + rows - STAGE, STAGE)
+            copies.append(
+                pltpu.make_async_copy(
+                    staged_ref.at[part], out_ref.at[part], sent_sem.at[start // STAGE]
+                )
+            )
+            copies[-1].start()
+    for copy in copies:
+        copy.wait()
 
 
 def slots(bounds, near_in, near, far, far_in):
@@ -305,7 +317,11 @@
         slots_kernel,
         out_shape=jax.ShapeDtypeStruct((channels, capacity, cells), jnp.bfloat16),
         in_specs=[scalars] + [vectors] * 2,
-        out_specs=vectors,
+        out_specs=pl.BlockSpec(memory_space=pl.ANY),
+        scratch_shapes=[
+            pltpu.VMEM((channels, capacity, cells), jnp.bfloat16),
+            pltpu.SemaphoreType.DMA((channels // STAGE,)),
+        ],
         compiler_params=pltpu.CompilerParams(vmem_limit_bytes=VMEM_BYTES),
         name="slots",
     )(bounds, window, near_in)

time: 72.6 us -> 72.4 us (level)
  no operation moved by 1% of the time
where the time goes in v5:
time: 72.4 us; the launch traced here: 71.7 us
  starting transfers between devices  26.1 us (36%)
  waiting for transfers between devices  23 us (32%)
  Pallas kernels  18.7 us (26%)
  local copies, waits for them, and re-layouts  3.58 us (5%)
    ppermute x14, waiting for transfers between devices, xor_permute(): lax.ppermute(array, axis, [(i, i ^ bits) for i in range(lax.axis_size(axi...  18.5 us
    ppermute x14, starting transfers between devices, xor_permute(): lax.ppermute(array, axis, [(i, i ^ bits) for i in range(lax.axis_size(axi...  13.6 us
    pallas_call x3, Pallas kernels, conv_parts(): pl.pallas_call(functools.partial(conv_kernel, parts, slots_of, groups), o...  11.1 us
    ppermute x1, starting transfers between devices, shards(): lax.ppermute(following, 'tm', [(i, i + 1) for i in range(tm_count - 1)])  5.36 us
    pallas_call x2, Pallas kernels, last_part(): pl.pallas_call(functools.partial(last_kernel, slot, far), out_shape=jax.S...  4.51 us
    ppermute x1, waiting for transfers between devices, shards(): far_in = lax.ppermute(far, 'tm', swapped_pairs(1))  4.5 us
    ppermute x1, starting transfers between devices, shards(): far_in = lax.ppermute(far, 'tm', swapped_pairs(1))  4.42 us
    ppermute x1, starting transfers between devices, shards(): lax.ppermute(third_tail, 'tm', [(i, i + 1) for i in range(tm_count - 1)])  2.64 us
  transfers between devices with their start and end apart: 18, of which 6 were waited for; matrix products, arithmetic and copies ran while one was open for 3% of the time, Pallas kernels for 20%

profile of v5, /device:TPU:3, one launch (start us, length us, event | category | flops | bytes accessed | tf_op | source)
XLA Modules:
  0.0 71.7 jit_solution(14377243752470919646)
XLA Ops:
  0.0 1.0 %constant_dynamic-slice_fusion.1 = (bf16[27,16,128]{2,1,0:T(8,128)(2,1)S(1)}, bf16[27,16,128]{2,1,0:T(8,128)(2,1)S(1)}, bf16[27,16,128]{2,1,0:T(8,128)(2,1)S(1)}) fusion(bf16[27,512,128]{2,1,0:T(8,128)(2,1)} %bitcast.20, s32[]{:T(128)S(6)} %select_n.22, s32[]{:T(128)S(6)} %select_n.21, s32[]{:T(128)S(6)} %select_n.20), kind=kLoop, calls=%fused_computation.3 | loop fusion | bytes 663564 | tf_op jit(solution)/shard_map/dynamic_slice | solution.py:342
  1.1 1.4 %collective-permute-start = (bf16[27,16,128]{2,1,0:T(8,128)(2,1)S(1)}, bf16[27,16,128]{2,1,0:T(8,128)(2,1)S(1)}, u32[]{:S(2)}, u32[]{:S(2)}) collective-permute-start(bf16[27,16,128]{2,1,0:T(8,128)(2,1)S(1)} %get-tuple-element.25), channel_id=1, source_target_pairs={{0,1},{1,0},{2,3},{3,2},{4,5},{5,4},{6,7},{7,6},{8,9},{9,8},{10,11... | collective-permute-start | bytes 331784 | tf_op jit(solution)/shard_map/ppermute | solution.py:331
  2.4 2.3 %collective-permute-start.1 = (bf16[27,16,128]{2,1,0:T(8,128)(2,1)S(1)}, bf16[27,16,128]{2,1,0:T(8,128)(2,1)S(1)}, u32[]{:S(2)}, u32[]{:S(2)}) collective-permute-start(bf16[27,16,128]{2,1,0:T(8,128)(2,1)S(1)} %get-tuple-element.28), channel_id=1, source_target_pairs={{0,2},{1,3},{2,0},{3,1},{4,6},{5,7},{6,4},{7,5},{8,10},{9,11},{10,... | collective-permute-start | bytes 331784 | tf_op jit(solution)/shard_map/ppermute | solution.py:331
  4.7 1.1 %copy.9 = bf16[128,4,512]{2,0,1:T(8,128)(2,1)S(1)} copy(bf16[128,4,512]{2,1,0:T(4,128)(2,1)} %param.6) | data formatting | bytes 1048576 | tf_op jit(solution)/shard_map/optimization_barrier | solution.py:359
  6.3 0.8 %collective-permute-done.1 = bf16[27,16,128]{2,1,0:T(8,128)(2,1)S(1)} collective-permute-done((bf16[27,16,128]{2,1,0:T(8,128)(2,1)S(1)}, bf16[27,16,128]{2,1,0:T(8,128)(2,1)S(1)}, u32[]{:S(2)}, u32[]{:S(2)}) %collective-permute-start.1) | collective-permute-done | bytes 110624 | tf_op jit(solution)/shard_map/ppermute | solution.py:331
  7.1 4.7 %collective-permute-done.2 = bf16[27,16,128]{2,1,0:T(8,128)(2,1)S(1)} collective-permute-done((bf16[27,16,128]{2,1,0:T(8,128)(2,1)S(1)}, bf16[27,16,128]{2,1,0:T(8,128)(2,1)S(1)}, u32[]{:S(2)}, u32[]{:S(2)}) %collective-permute-start.2) | collective-permute-done | bytes 110624 | tf_op jit(solution)/shard_map/ppermute | solution.py:331
  11.9 3.9 %collective-permute-start.3 = (bf16[4,128,512]{2,1,0:T(8,128)(2,1)S(1)}, bf16[4,128,512]{2,1,0:T(8,128)(2,1)S(1)}, u32[]{:S(2)}, u32[]{:S(2)}) collective-permute-start(bf16[4,128,512]{2,1,0:T(8,128)(2,1)S(1)} %bitcast.12), channel_id=1, source_target_pairs={{0,2},{1,3},{2,0},{3,1},{4,6},{5,7},{6,4},{7,5},{8,10},{9,11},{10,... | collective-permute-start | bytes 1572872 | tf_op jit(solution)/shard_map/ppermute | solution.py:331
  15.8 1.2 %collective-permute-start.9 = (bf16[3,27,16,128]{3,2,1,0:T(8,128)(2,1)S(1)}, bf16[3,27,16,128]{3,2,1,0:T(8,128)(2,1)S(1)}, u32[]{:S(2)}, u32[]{:S(2)}) collective-permute-start(bf16[3,27,16,128]{3,2,1,0:T(8,128)(2,1)S(1)} %pad_maximum_fusion.refs_3_.refs_2_), channel_id=1, source_target_pairs={{0,24},{4,28},{8,16},{12,20},{16,8},{20,12},{24,0},{28,4},{1,25},{... | collective-permute-start | bytes 995336 | tf_op jit(solution)/shard_map/ppermute | solution.py:331
  17.2 1.2 %collective-permute-start.7 = (bf16[3,27,16,128]{3,2,1,0:T(8,128)(2,1)S(1)}, bf16[3,27,16,128]{3,2,1,0:T(8,128)(2,1)S(1)}, u32[]{:S(2)}, u32[]{:S(2)}) collective-permute-start(bf16[3,27,16,128]{3,2,1,0:T(8,128)(2,1)S(1)} %pad_maximum_fusion.refs_3_.refs_2_), channel_id=1, source_target_pairs={{0,8},{4,12},{8,0},{12,4},{16,24},{20,28},{24,16},{28,20},{1,9},{5... | collective-permute-start | bytes 995336 | tf_op jit(solution)/shard_map/ppermute | solution.py:331
  18.4 1.2 %constant_dynamic-slice_fusion.refs_2_ = bf16[27,128,128]{2,1,0:T(8,128)(2,1)S(1)} fusion(bf16[27,512,128]{2,1,0:T(8,128)(2,1)} %bitcast.21, s32[]{:T(128)S(6)} %select_n.23), kind=kLoop, calls=%fused_computation.2 | loop fusion | bytes 1769476 | tf_op jit(solution)/shard_map/dynamic_slice | solution.py:349
  19.7 3.8 %conv_parts.3 = (f32[4,128,512]{2,1,0:T(8,128)S(1)}, f32[2,128,512]{2,1,0:T(8,128)S(1)}) custom-call(s32[12]{0:T(128)S(1)} %copy-done, bf16[4,128,512]{2,1,0:T(8,128)(2,1)S(1)} %bitcast.13, bf16[27,128,128]{2,1,0:T(8,128)(2,1)S(1)} %constant_dynamic-slice_fusion.refs_2_), custom_call_target="tpu_custom_call" | custom-call | flops 1024 | bytes 1024 | tf_op jit(solution)/shard_map/conv_parts/pallas_call | solution.py:168
  24.2 9.3 %collective-permute-done.8.refs_7_.refs_6_ = bf16[3,27,16,128]{3,2,1,0:T(8,128)(2,1)S(1)} collective-permute-done((bf16[3,27,16,128]{3,2,1,0:T(8,128)(2,1)S(1)}, bf16[3,27,16,128]{3,2,1,0:T(8,128)(2,1)S(1)}, u32[]{:S(2)}, u32[]{:S(2)}) %collective-permute-start.8) | collective-permute-done | bytes 331808 | tf_op jit(solution)/shard_map/ppermute | solution.py:331
  34.6 2.9 %collective-permute-done.3.refs_2_ = bf16[4,128,512]{2,1,0:T(8,128)(2,1)S(1)} collective-permute-done((bf16[4,128,512]{2,1,0:T(8,128)(2,1)S(1)}, bf16[4,128,512]{2,1,0:T(8,128)(2,1)S(1)}, u32[]{:S(2)}, u32[]{:S(2)}) %collective-permute-start.3) | collective-permute-done | bytes 524320 | tf_op jit(solution)/shard_map/ppermute | solution.py:331
  37.7 2.1 %conv_parts.5 = f32[2,128,512]{2,1,0:T(8,128)S(1)} custom-call(s32[12]{0:T(128)S(1)} %copy-done, bf16[4,128,512]{2,1,0:T(8,128)(2,1)S(1)} %collective-permute-done.10.refs_1_, bf16[4,128,512]{2,1,0:T(8,128)(2,1)S(1)} %collective-permute-done.3.refs_2_, bf16[3,27,16,128]{3,2,1,0:T(8,128)(2,1)S(1)} %pad_maximum_fusion.refs_3_.refs_2_, ...), custom_call_target="tpu_custom_call" | custom-call | flops 1024 | bytes 1024 | tf_op jit(solution)/shard_map/conv_parts/pallas_call | solution.py:168
  39.9 5.4 %collective-permute-start.15 = (f32[2,128,512]{2,1,0:T(8,128)S(1)}, f32[2,128,512]{2,1,0:T(8,128)S(1)}, u32[]{:S(2)}, u32[]{:S(2)}) collective-permute-start(f32[2,128,512]{2,1,0:T(8,128)S(1)} %conv_parts.5), channel_id=1, source_target_pairs={{0,4},{4,8},{8,12},{12,16},{16,20},{20,24},{24,28},{1,5},{5,9},{9,... | collective-permute-start | bytes 1572872 | tf_op jit(solution)/shard_map/ppermute | solution.py:378
  45.2 1.8 %collective-permute-start.5 = (bf16[2,128,512]{2,1,0:T(8,128)(2,1)S(1)}, bf16[2,128,512]{2,1,0:T(8,128)(2,1)S(1)}, u32[]{:S(2)}, u32[]{:S(2)}) collective-permute-start(bf16[2,128,512]{2,1,0:T(8,128)(2,1)S(1)} %get-tuple-element.32), channel_id=1, source_target_pairs={{0,1},{1,0},{2,3},{3,2},{4,5},{5,4},{6,7},{7,6},{8,9},{9,8},{10,11... | collective-permute-start | bytes 786440 | tf_op jit(solution)/shard_map/ppermute | solution.py:331
  47.0 2.6 %collective-permute-start.6 = (bf16[2,128,512]{2,1,0:T(8,128)(2,1)S(1)}, bf16[2,128,512]{2,1,0:T(8,128)(2,1)S(1)}, u32[]{:S(2)}, u32[]{:S(2)}) collective-permute-start(bf16[2,128,512]{2,1,0:T(8,128)(2,1)S(1)} %collective-permute-done.4.refs_1_), channel_id=1, source_target_pairs={{0,4},{4,8},{8,12},{12,16},{16,20},{20,24},{24,28},{1,5},{5,9},{9,... | collective-permute-start | bytes 786440 | tf_op jit(solution)/shard_map/ppermute | solution.py:379
  49.7 5.2 %conv_parts.4.refs_10_ = f32[4,128,512]{2,1,0:T(8,128)S(1)} custom-call(s32[12]{0:T(128)S(1)} %copy-done, bf16[4,128,512]{2,1,0:T(8,128)(2,1)S(1)} %collective-permute-done.10.refs_1_, bf16[4,128,512]{2,1,0:T(8,128)(2,1)S(1)} %collective-permute-done.3.refs_2_, bf16[3,27,16,128]{3,2,1,0:T(8,128)(2,1)S(1)} %pad_maximum_fusion.refs_3_.refs_2_, ...), custom_call_target="tpu_custom_call" | custom-call | flops 1024 | bytes 1024 | tf_op jit(solution)/shard_map/conv_parts/pallas_call | solution.py:168
  55.6 2.2 %last_part.2.far_ref = bf16[2,128,512]{2,1,0:T(8,128)(2,1)S(1)} custom-call(s32[12]{0:T(128)S(1)} %copy-done, bf16[6,384,512]{2,1,0:T(8,128)(2,1)S(1)} %shifted_frames.1.refs_1_, bf16[3,27,16,128]{3,2,1,0:T(8,128)(2,1)S(1)} %pad_maximum_fusion.refs_3_.refs_2_, bf16[3,27,16,128]{3,2,1,0:T(8,128)(2,1)S(1)} %collective-permute-done.11.refs_4_.refs_3_, ...), custom_call_target="tpu_custom_call" | custom-call | flops 1024 | bytes 1024 | tf_op jit(solution)/shard_map/last_part/pallas_call | solution.py:233
  57.8 4.4 %collective-permute-start.16 = (bf16[2,128,512]{2,1,0:T(8,128)(2,1)S(1)}, bf16[2,128,512]{2,1,0:T(8,128)(2,1)S(1)}, u32[]{:S(2)}, u32[]{:S(2)}) collective-permute-start(bf16[2,128,512]{2,1,0:T(8,128)(2,1)S(1)} %last_part.2.far_ref), channel_id=1, source_target_pairs={{4,8},{12,16},{20,24},{8,4},{16,12},{24,20},{5,9},{13,17},{21,25},... | collective-permute-start | bytes 786440 | tf_op jit(solution)/shard_map/ppermute | solution.py:389
  62.3 2.3 %last_part.3.near_ref = bf16[2,128,512]{2,1,0:T(8,128)(2,1)S(1)} custom-call(s32[12]{0:T(128)S(1)} %copy-done, bf16[6,384,512]{2,1,0:T(8,128)(2,1)S(1)} %shifted_frames.1.refs_1_, bf16[3,27,16,128]{3,2,1,0:T(8,128)(2,1)S(1)} %pad_maximum_fusion.refs_3_.refs_2_, bf16[3,27,16,128]{3,2,1,0:T(8,128)(2,1)S(1)} %collective-permute-done.11.refs_4_.refs_3_, ...), custom_call_target="tpu_custom_call" | custom-call | flops 1024 | bytes 1024 | tf_op jit(solution)/shard_map/last_part/pallas_call | solution.py:233
  64.6 4.5 %collective-permute-done.16.far_in_ref = bf16[2,128,512]{2,1,0:T(8,128)(2,1)S(1)} collective-permute-done((bf16[2,128,512]{2,1,0:T(8,128)(2,1)S(1)}, bf16[2,128,512]{2,1,0:T(8,128)(2,1)S(1)}, u32[]{:S(2)}, u32[]{:S(2)}) %collective-permute-start.16) | collective-permute-done | bytes 262176 | tf_op jit(solution)/shard_map/ppermute | solution.py:389
  69.1 0.8 %window.1.window_ref = f32[8,128,512]{2,1,0:T(8,128)S(1)} custom-call(s32[1,2]{1,0:T(1,128)S(1)} %copy-done.3, bf16[2,128,512]{2,1,0:T(8,128)(2,1)S(1)} %last_part.3.near_ref, bf16[2,128,512]{2,1,0:T(8,128)(2,1)S(1)} %last_part.2.far_ref, bf16[2,128,512]{2,1,0:T(8,128)(2,1)S(1)} %collective-permute-done.16.far_in_ref), custom_call_target="tpu_custom_call" | custom-call | flops 1000000000 | bytes 1024 | tf_op jit(solution)/shard_map/window/pallas_call | solution.py:307
  69.9 1.8 %slots.1 = bf16[128,8,512]{2,1,0:T(8,128)(2,1)} custom-call(s32[1,2]{1,0:T(1,128)S(1)} %copy-done.3, f32[8,128,512]{2,1,0:T(8,128)S(1)} %window.1.window_ref, bf16[2,128,512]{2,1,0:T(8,128)(2,1)S(1)} %collective-permute-done.17.near_in_ref), custom_call_target="tpu_custom_call" | custom-call | tf_op jit(solution)/shard_map/slots/pallas_call | solution.py:316
  (33 shorter events, 3.4 us)
Async XLA Ops:
  0.0 19.6 %copy-start = (s32[12]{0:T(128)S(1)}, s32[12]{0:T(128)}, u32[]{:S(2)}) copy-start(s32[12]{0:T(128)} %refs_0_.9) | copy-start | bytes 148
  1.1 4.8 %collective-permute-start = (bf16[27,16,128]{2,1,0:T(8,128)(2,1)S(1)}, bf16[27,16,128]{2,1,0:T(8,128)(2,1)S(1)}, u32[]{:S(2)}, u32[]{:S(2)}) collective-permute-start(bf16[27,16,128]{2,1,0:T(8,128)(2,1)S(1)} %get-tuple-element.25), channel_id=1, source_target_pairs={{0,1},{1,0},{2,3},{3,2},{4,5},{5,4},{6,7},{7,6},{8,9},{9,8},{10,11... | collective-permute-start | bytes 331784 | tf_op jit(solution)/shard_map/ppermute | solution.py:331
  2.4 4.7 %collective-permute-start.1 = (bf16[27,16,128]{2,1,0:T(8,128)(2,1)S(1)}, bf16[27,16,128]{2,1,0:T(8,128)(2,1)S(1)}, u32[]{:S(2)}, u32[]{:S(2)}) collective-permute-start(bf16[27,16,128]{2,1,0:T(8,128)(2,1)S(1)} %get-tuple-element.28), channel_id=1, source_target_pairs={{0,2},{1,3},{2,0},{3,1},{4,6},{5,7},{6,4},{7,5},{8,10},{9,11},{10,... | collective-permute-start | bytes 331784 | tf_op jit(solution)/shard_map/ppermute | solution.py:331
  4.7 7.1 %collective-permute-start.2 = (bf16[27,16,128]{2,1,0:T(8,128)(2,1)S(1)}, bf16[27,16,128]{2,1,0:T(8,128)(2,1)S(1)}, u32[]{:S(2)}, u32[]{:S(2)}) collective-permute-start(bf16[27,16,128]{2,1,0:T(8,128)(2,1)S(1)} %get-tuple-element.29), channel_id=1, source_target_pairs={{0,3},{1,2},{2,1},{3,0},{4,7},{5,6},{6,5},{7,4},{8,11},{9,10},{10,... | collective-permute-start | bytes 331784 | tf_op jit(solution)/shard_map/ppermute | solution.py:331
  5.9 27.6 %collective-permute-start.10 = (bf16[4,128,512]{2,1,0:T(8,128)(2,1)S(1)}, bf16[4,128,512]{2,1,0:T(8,128)(2,1)S(1)}, u32[]{:S(2)}, u32[]{:S(2)}) collective-permute-start(bf16[4,128,512]{2,1,0:T(8,128)(2,1)S(1)} %bitcast.11), channel_id=1, source_target_pairs={{0,1},{1,0},{2,3},{3,2},{4,5},{5,4},{6,7},{7,6},{8,9},{9,8},{10,11... | collective-permute-start | bytes 1572872 | tf_op jit(solution)/shard_map/ppermute | solution.py:331
  11.9 25.7 %collective-permute-start.3 = (bf16[4,128,512]{2,1,0:T(8,128)(2,1)S(1)}, bf16[4,128,512]{2,1,0:T(8,128)(2,1)S(1)}, u32[]{:S(2)}, u32[]{:S(2)}) collective-permute-start(bf16[4,128,512]{2,1,0:T(8,128)(2,1)S(1)} %bitcast.12), channel_id=1, source_target_pairs={{0,2},{1,3},{2,0},{3,1},{4,6},{5,7},{6,4},{7,5},{8,10},{9,11},{10,... | collective-permute-start | bytes 1572872 | tf_op jit(solution)/shard_map/ppermute | solution.py:331
  15.8 8.4 %collective-permute-start.9 = (bf16[3,27,16,128]{3,2,1,0:T(8,128)(2,1)S(1)}, bf16[3,27,16,128]{3,2,1,0:T(8,128)(2,1)S(1)}, u32[]{:S(2)}, u32[]{:S(2)}) collective-permute-start(bf16[3,27,16,128]{3,2,1,0:T(8,128)(2,1)S(1)} %pad_maximum_fusion.refs_3_.refs_2_), channel_id=1, source_target_pairs={{0,24},{4,28},{8,16},{12,20},{16,8},{20,12},{24,0},{28,4},{1,25},{... | collective-permute-start | bytes 995336 | tf_op jit(solution)/shard_map/ppermute | solution.py:331
  17.0 16.5 %collective-permute-start.8 = (bf16[3,27,16,128]{3,2,1,0:T(8,128)(2,1)S(1)}, bf16[3,27,16,128]{3,2,1,0:T(8,128)(2,1)S(1)}, u32[]{:S(2)}, u32[]{:S(2)}) collective-permute-start(bf16[3,27,16,128]{3,2,1,0:T(8,128)(2,1)S(1)} %pad_maximum_fusion.refs_3_.refs_2_), channel_id=1, source_target_pairs={{0,16},{4,20},{8,24},{12,28},{16,0},{20,4},{24,8},{28,12},{1,17},{... | collective-permute-start | bytes 995336 | tf_op jit(solution)/shard_map/ppermute | solution.py:331
  17.2 16.3 %collective-permute-start.7 = (bf16[3,27,16,128]{3,2,1,0:T(8,128)(2,1)S(1)}, bf16[3,27,16,128]{3,2,1,0:T(8,128)(2,1)S(1)}, u32[]{:S(2)}, u32[]{:S(2)}) collective-permute-start(bf16[3,27,16,128]{3,2,1,0:T(8,128)(2,1)S(1)} %pad_maximum_fusion.refs_3_.refs_2_), channel_id=1, source_target_pairs={{0,8},{4,12},{8,0},{12,4},{16,24},{20,28},{24,16},{28,20},{1,9},{5... | collective-permute-start | bytes 995336 | tf_op jit(solution)/shard_map/ppermute | solution.py:331
  33.5 4.2 %collective-permute-start.11 = (bf16[3,27,16,128]{3,2,1,0:T(8,128)(2,1)S(1)}, bf16[3,27,16,128]{3,2,1,0:T(8,128)(2,1)S(1)}, u32[]{:S(2)}, u32[]{:S(2)}) collective-permute-start(bf16[3,27,16,128]{3,2,1,0:T(8,128)(2,1)S(1)} %pad_maximum_fusion.refs_3_.refs_2_), channel_id=1, source_target_pairs={{0,4},{4,0},{8,12},{12,8},{16,20},{20,16},{24,28},{28,24},{1,5},{5... | collective-permute-start | bytes 995336 | tf_op jit(solution)/shard_map/ppermute | solution.py:331
  34.1 3.6 %collective-permute-start.12 = (bf16[3,27,16,128]{3,2,1,0:T(8,128)(2,1)S(1)}, bf16[3,27,16,128]{3,2,1,0:T(8,128)(2,1)S(1)}, u32[]{:S(2)}, u32[]{:S(2)}) collective-permute-start(bf16[3,27,16,128]{3,2,1,0:T(8,128)(2,1)S(1)} %collective-permute-done.7.refs_5_.refs_4_), channel_id=1, source_target_pairs={{0,4},{4,0},{8,12},{12,8},{16,20},{20,16},{24,28},{28,24},{1,5},{5... | collective-permute-start | bytes 995336 | tf_op jit(solution)/shard_map/ppermute | solution.py:331
  34.1 3.6 %collective-permute-start.13 = (bf16[3,27,16,128]{3,2,1,0:T(8,128)(2,1)S(1)}, bf16[3,27,16,128]{3,2,1,0:T(8,128)(2,1)S(1)}, u32[]{:S(2)}, u32[]{:S(2)}) collective-permute-start(bf16[3,27,16,128]{3,2,1,0:T(8,128)(2,1)S(1)} %collective-permute-done.8.refs_7_.refs_6_), channel_id=1, source_target_pairs={{0,4},{4,0},{8,12},{12,8},{16,20},{20,16},{24,28},{28,24},{1,5},{5... | collective-permute-start | bytes 995336 | tf_op jit(solution)/shard_map/ppermute | solution.py:331
  34.6 3.1 %collective-permute-start.14 = (bf16[3,27,16,128]{3,2,1,0:T(8,128)(2,1)S(1)}, bf16[3,27,16,128]{3,2,1,0:T(8,128)(2,1)S(1)}, u32[]{:S(2)}, u32[]{:S(2)}) collective-permute-start(bf16[3,27,16,128]{3,2,1,0:T(8,128)(2,1)S(1)} %collective-permute-done.9.refs_9_.refs_8_), channel_id=1, source_target_pairs={{0,4},{4,0},{8,12},{12,8},{16,20},{20,16},{24,28},{28,24},{1,5},{5... | collective-permute-start | bytes 995336 | tf_op jit(solution)/shard_map/ppermute | solution.py:331
  37.6 7.6 %collective-permute-start.4 = (bf16[2,128,512]{2,1,0:T(8,128)(2,1)S(1)}, bf16[2,128,512]{2,1,0:T(8,128)(2,1)S(1)}, u32[]{:S(2)}, u32[]{:S(2)}) collective-permute-start(bf16[2,128,512]{2,1,0:T(8,128)(2,1)S(1)} %get-tuple-element.49), channel_id=1, source_target_pairs={{0,1},{1,0},{2,3},{3,2},{4,5},{5,4},{6,7},{7,6},{8,9},{9,8},{10,11... | collective-permute-start | bytes 786440 | tf_op jit(solution)/shard_map/ppermute | solution.py:331
  39.9 15.6 %collective-permute-start.15 = (f32[2,128,512]{2,1,0:T(8,128)S(1)}, f32[2,128,512]{2,1,0:T(8,128)S(1)}, u32[]{:S(2)}, u32[]{:S(2)}) collective-permute-start(f32[2,128,512]{2,1,0:T(8,128)S(1)} %conv_parts.5), channel_id=1, source_target_pairs={{0,4},{4,8},{8,12},{12,16},{16,20},{20,24},{24,28},{1,5},{5,9},{9,... | collective-permute-start | bytes 1572872 | tf_op jit(solution)/shard_map/ppermute | solution.py:378
  45.2 9.7 %collective-permute-start.5 = (bf16[2,128,512]{2,1,0:T(8,128)(2,1)S(1)}, bf16[2,128,512]{2,1,0:T(8,128)(2,1)S(1)}, u32[]{:S(2)}, u32[]{:S(2)}) collective-permute-start(bf16[2,128,512]{2,1,0:T(8,128)(2,1)S(1)} %get-tuple-element.32), channel_id=1, source_target_pairs={{0,1},{1,0},{2,3},{3,2},{4,5},{5,4},{6,7},{7,6},{8,9},{9,8},{10,11... | collective-permute-start | bytes 786440 | tf_op jit(solution)/shard_map/ppermute | solution.py:331
  47.0 7.9 %collective-permute-start.6 = (bf16[2,128,512]{2,1,0:T(8,128)(2,1)S(1)}, bf16[2,128,512]{2,1,0:T(8,128)(2,1)S(1)}, u32[]{:S(2)}, u32[]{:S(2)}) collective-permute-start(bf16[2,128,512]{2,1,0:T(8,128)(2,1)S(1)} %collective-permute-done.4.refs_1_), channel_id=1, source_target_pairs={{0,4},{4,8},{8,12},{12,16},{16,20},{20,24},{24,28},{1,5},{5,9},{9,... | collective-permute-start | bytes 786440 | tf_op jit(solution)/shard_map/ppermute | solution.py:379
  54.9 0.7 copy-start.1
  54.9 0.7 copy-start.2
  57.8 11.3 %copy-start.3 = (s32[1,2]{1,0:T(1,128)S(1)}, s32[1,2]{1,0:T(1,128)}, u32[]{:S(2)}) copy-start(s32[1,2]{1,0:T(1,128)} %bounds_ref.3) | copy-start | bytes 28
  57.8 11.3 %collective-permute-start.16 = (bf16[2,128,512]{2,1,0:T(8,128)(2,1)S(1)}, bf16[2,128,512]{2,1,0:T(8,128)(2,1)S(1)}, u32[]{:S(2)}, u32[]{:S(2)}) collective-permute-start(bf16[2,128,512]{2,1,0:T(8,128)(2,1)S(1)} %last_part.2.far_ref), channel_id=1, source_target_pairs={{4,8},{12,16},{20,24},{8,4},{16,12},{24,20},{5,9},{13,17},{21,25},... | collective-permute-start | bytes 786440 | tf_op jit(solution)/shard_map/ppermute | solution.py:389
  64.5 5.3 %collective-permute-start.17 = (bf16[2,128,512]{2,1,0:T(8,128)(2,1)S(1)}, bf16[2,128,512]{2,1,0:T(8,128)(2,1)S(1)}, u32[]{:S(2)}, u32[]{:S(2)}) collective-permute-start(bf16[2,128,512]{2,1,0:T(8,128)(2,1)S(1)} %last_part.3.near_ref), channel_id=1, source_target_pairs={{0,4},{8,12},{16,20},{24,28},{4,0},{12,8},{20,16},{28,24},{1,5},{9... | collective-permute-start | bytes 786440 | tf_op jit(solution)/shard_map/ppermute | solution.py:392

commit v6 on v5

--- a/solution.py
+++ b/solution.py
@@ -263,7 +263,7 @@
 
             @pl.when((slot >= 0) & (slot < size))
             def _():
-                out_ref[slot] = pair[i].astype(jnp.float32)
+                out_ref[slot] = pair[i]
 
     for slot in range(capacity):
 
@@ -280,7 +280,9 @@
     rows = 16
     copies = []
     for start in range(0, channels, rows):
-        frames = [window_ref[w, start : start + rows, :] for w in range(capacity)]
+        frames = [
+            window_ref[w, start : start + rows, :].astype(jnp.float32) for w in range(capacity)
+        ]
         for i in range(half):
             frame = near_in_ref[i, start : start + rows, :].astype(jnp.float32)
             for w in range(capacity):
@@ -306,7 +308,7 @@
     vectors = pl.BlockSpec(memory_space=pltpu.VMEM)
     window = pl.pallas_call(
         window_kernel,
-        out_shape=jax.ShapeDtypeStruct((capacity, channels, cells), jnp.float32),
+        out_shape=jax.ShapeDtypeStruct((capacity, channels, cells), jnp.bfloat16),
         in_specs=[scalars] + [vectors] * 3,
         out_specs=vectors,
         compiler_params=pltpu.CompilerParams(vmem_limit_bytes=VMEM_BYTES),

time: 72.4 us -> 72.4 us (level)
  no operation moved by 1% of the time
where the time goes in v6:
time: 72.4 us; the launch traced here: 71.7 us
  starting transfers between devices  26.1 us (36%)
  waiting for transfers between devices  23 us (32%)
  Pallas kernels  18.7 us (26%)
  local copies, waits for them, and re-layouts  3.58 us (5%)
    ppermute x14, waiting for transfers between devices, xor_permute(): lax.ppermute(array, axis, [(i, i ^ bits) for i in range(lax.axis_size(axi...  18.5 us
    ppermute x14, starting transfers between devices, xor_permute(): lax.ppermute(array, axis, [(i, i ^ bits) for i in range(lax.axis_size(axi...  13.6 us
    pallas_call x3, Pallas kernels, conv_parts(): pl.pallas_call(functools.partial(conv_kernel, parts, slots_of, groups), o...  11.1 us
    ppermute x1, starting transfers between devices, shards(): lax.ppermute(following, 'tm', [(i, i + 1) for i in range(tm_count - 1)])  5.36 us
    pallas_call x2, Pallas kernels, last_part(): pl.pallas_call(functools.partial(last_kernel, slot, far), out_shape=jax.S...  4.51 us
    ppermute x1, waiting for transfers between devices, shards(): far_in = lax.ppermute(far, 'tm', swapped_pairs(1))  4.5 us
    ppermute x1, starting transfers between devices, shards(): far_in = lax.ppermute(far, 'tm', swapped_pairs(1))  4.42 us
    ppermute x1, starting transfers between devices, shards(): lax.ppermute(third_tail, 'tm', [(i, i + 1) for i in range(tm_count - 1)])  2.64 us
  transfers between devices with their start and end apart: 18, of which 6 were waited for; matrix products, arithmetic and copies ran while one was open for 3% of the time, Pallas kernels for 20%

profile of v6, /device:TPU:3, one launch (start us, length us, event | category | flops | bytes accessed | tf_op | source)
XLA Modules:
  0.0 71.7 jit_solution(6369497620910904121)
XLA Ops:
  0.0 1.0 %constant_dynamic-slice_fusion.1 = (bf16[27,16,128]{2,1,0:T(8,128)(2,1)S(1)}, bf16[27,16,128]{2,1,0:T(8,128)(2,1)S(1)}, bf16[27,16,128]{2,1,0:T(8,128)(2,1)S(1)}) fusion(bf16[27,512,128]{2,1,0:T(8,128)(2,1)} %bitcast.20, s32[]{:T(128)S(6)} %select_n.22, s32[]{:T(128)S(6)} %select_n.21, s32[]{:T(128)S(6)} %select_n.20), kind=kLoop, calls=%fused_computation.3 | loop fusion | bytes 663564 | tf_op jit(solution)/shard_map/dynamic_slice | solution.py:344
  1.1 1.4 %collective-permute-start = (bf16[27,16,128]{2,1,0:T(8,128)(2,1)S(1)}, bf16[27,16,128]{2,1,0:T(8,128)(2,1)S(1)}, u32[]{:S(2)}, u32[]{:S(2)}) collective-permute-start(bf16[27,16,128]{2,1,0:T(8,128)(2,1)S(1)} %get-tuple-element.25), channel_id=1, source_target_pairs={{0,1},{1,0},{2,3},{3,2},{4,5},{5,4},{6,7},{7,6},{8,9},{9,8},{10,11... | collective-permute-start | bytes 331784 | tf_op jit(solution)/shard_map/ppermute | solution.py:333
  2.4 2.3 %collective-permute-start.1 = (bf16[27,16,128]{2,1,0:T(8,128)(2,1)S(1)}, bf16[27,16,128]{2,1,0:T(8,128)(2,1)S(1)}, u32[]{:S(2)}, u32[]{:S(2)}) collective-permute-start(bf16[27,16,128]{2,1,0:T(8,128)(2,1)S(1)} %get-tuple-element.28), channel_id=1, source_target_pairs={{0,2},{1,3},{2,0},{3,1},{4,6},{5,7},{6,4},{7,5},{8,10},{9,11},{10,... | collective-permute-start | bytes 331784 | tf_op jit(solution)/shard_map/ppermute | solution.py:333
  4.7 1.1 %copy.9 = bf16[128,4,512]{2,0,1:T(8,128)(2,1)S(1)} copy(bf16[128,4,512]{2,1,0:T(4,128)(2,1)} %param.6) | data formatting | bytes 1048576 | tf_op jit(solution)/shard_map/optimization_barrier | solution.py:361
  6.3 0.8 %collective-permute-done.1 = bf16[27,16,128]{2,1,0:T(8,128)(2,1)S(1)} collective-permute-done((bf16[27,16,128]{2,1,0:T(8,128)(2,1)S(1)}, bf16[27,16,128]{2,1,0:T(8,128)(2,1)S(1)}, u32[]{:S(2)}, u32[]{:S(2)}) %collective-permute-start.1) | collective-permute-done | bytes 110624 | tf_op jit(solution)/shard_map/ppermute | solution.py:333
  7.1 4.7 %collective-permute-done.2 = bf16[27,16,128]{2,1,0:T(8,128)(2,1)S(1)} collective-permute-done((bf16[27,16,128]{2,1,0:T(8,128)(2,1)S(1)}, bf16[27,16,128]{2,1,0:T(8,128)(2,1)S(1)}, u32[]{:S(2)}, u32[]{:S(2)}) %collective-permute-start.2) | collective-permute-done | bytes 110624 | tf_op jit(solution)/shard_map/ppermute | solution.py:333
  11.9 3.9 %collective-permute-start.3 = (bf16[4,128,512]{2,1,0:T(8,128)(2,1)S(1)}, bf16[4,128,512]{2,1,0:T(8,128)(2,1)S(1)}, u32[]{:S(2)}, u32[]{:S(2)}) collective-permute-start(bf16[4,128,512]{2,1,0:T(8,128)(2,1)S(1)} %bitcast.12), channel_id=1, source_target_pairs={{0,2},{1,3},{2,0},{3,1},{4,6},{5,7},{6,4},{7,5},{8,10},{9,11},{10,... | collective-permute-start | bytes 1572872 | tf_op jit(solution)/shard_map/ppermute | solution.py:333
  15.8 1.2 %collective-permute-start.9 = (bf16[3,27,16,128]{3,2,1,0:T(8,128)(2,1)S(1)}, bf16[3,27,16,128]{3,2,1,0:T(8,128)(2,1)S(1)}, u32[]{:S(2)}, u32[]{:S(2)}) collective-permute-start(bf16[3,27,16,128]{3,2,1,0:T(8,128)(2,1)S(1)} %pad_maximum_fusion.refs_3_.refs_2_), channel_id=1, source_target_pairs={{0,24},{4,28},{8,16},{12,20},{16,8},{20,12},{24,0},{28,4},{1,25},{... | collective-permute-start | bytes 995336 | tf_op jit(solution)/shard_map/ppermute | solution.py:333
  17.2 1.2 %collective-permute-start.7 = (bf16[3,27,16,128]{3,2,1,0:T(8,128)(2,1)S(1)}, bf16[3,27,16,128]{3,2,1,0:T(8,128)(2,1)S(1)}, u32[]{:S(2)}, u32[]{:S(2)}) collective-permute-start(bf16[3,27,16,128]{3,2,1,0:T(8,128)(2,1)S(1)} %pad_maximum_fusion.refs_3_.refs_2_), channel_id=1, source_target_pairs={{0,8},{4,12},{8,0},{12,4},{16,24},{20,28},{24,16},{28,20},{1,9},{5... | collective-permute-start | bytes 995336 | tf_op jit(solution)/shard_map/ppermute | solution.py:333
  18.4 1.2 %constant_dynamic-slice_fusion.refs_2_ = bf16[27,128,128]{2,1,0:T(8,128)(2,1)S(1)} fusion(bf16[27,512,128]{2,1,0:T(8,128)(2,1)} %bitcast.21, s32[]{:T(128)S(6)} %select_n.23), kind=kLoop, calls=%fused_computation.2 | loop fusion | bytes 1769476 | tf_op jit(solution)/shard_map/dynamic_slice | solution.py:351
  19.7 3.8 %conv_parts.3 = (f32[4,128,512]{2,1,0:T(8,128)S(1)}, f32[2,128,512]{2,1,0:T(8,128)S(1)}) custom-call(s32[12]{0:T(128)S(1)} %copy-done, bf16[4,128,512]{2,1,0:T(8,128)(2,1)S(1)} %bitcast.13, bf16[27,128,128]{2,1,0:T(8,128)(2,1)S(1)} %constant_dynamic-slice_fusion.refs_2_), custom_call_target="tpu_custom_call" | custom-call | flops 1024 | bytes 1024 | tf_op jit(solution)/shard_map/conv_parts/pallas_call | solution.py:168
  23.4 0.7 %collective-permute-done.9.refs_9_.refs_8_ = bf16[3,27,16,128]{3,2,1,0:T(8,128)(2,1)S(1)} collective-permute-done((bf16[3,27,16,128]{3,2,1,0:T(8,128)(2,1)S(1)}, bf16[3,27,16,128]{3,2,1,0:T(8,128)(2,1)S(1)}, u32[]{:S(2)}, u32[]{:S(2)}) %collective-permute-start.9) | collective-permute-done | bytes 331808 | tf_op jit(solution)/shard_map/ppermute | solution.py:333
  24.2 9.3 %collective-permute-done.8.refs_7_.refs_6_ = bf16[3,27,16,128]{3,2,1,0:T(8,128)(2,1)S(1)} collective-permute-done((bf16[3,27,16,128]{3,2,1,0:T(8,128)(2,1)S(1)}, bf16[3,27,16,128]{3,2,1,0:T(8,128)(2,1)S(1)}, u32[]{:S(2)}, u32[]{:S(2)}) %collective-permute-start.8) | collective-permute-done | bytes 331808 | tf_op jit(solution)/shard_map/ppermute | solution.py:333
  34.6 2.9 %collective-permute-done.3.refs_2_ = bf16[4,128,512]{2,1,0:T(8,128)(2,1)S(1)} collective-permute-done((bf16[4,128,512]{2,1,0:T(8,128)(2,1)S(1)}, bf16[4,128,512]{2,1,0:T(8,128)(2,1)S(1)}, u32[]{:S(2)}, u32[]{:S(2)}) %collective-permute-start.3) | collective-permute-done | bytes 524320 | tf_op jit(solution)/shard_map/ppermute | solution.py:333
  37.7 2.1 %conv_parts.5 = f32[2,128,512]{2,1,0:T(8,128)S(1)} custom-call(s32[12]{0:T(128)S(1)} %copy-done, bf16[4,128,512]{2,1,0:T(8,128)(2,1)S(1)} %collective-permute-done.10.refs_1_, bf16[4,128,512]{2,1,0:T(8,128)(2,1)S(1)} %collective-permute-done.3.refs_2_, bf16[3,27,16,128]{3,2,1,0:T(8,128)(2,1)S(1)} %pad_maximum_fusion.refs_3_.refs_2_, ...), custom_call_target="tpu_custom_call" | custom-call | flops 1024 | bytes 1024 | tf_op jit(solution)/shard_map/conv_parts/pallas_call | solution.py:168
  39.9 5.4 %collective-permute-start.15 = (f32[2,128,512]{2,1,0:T(8,128)S(1)}, f32[2,128,512]{2,1,0:T(8,128)S(1)}, u32[]{:S(2)}, u32[]{:S(2)}) collective-permute-start(f32[2,128,512]{2,1,0:T(8,128)S(1)} %conv_parts.5), channel_id=1, source_target_pairs={{0,4},{4,8},{8,12},{12,16},{16,20},{20,24},{24,28},{1,5},{5,9},{9,... | collective-permute-start | bytes 1572872 | tf_op jit(solution)/shard_map/ppermute | solution.py:380
  45.2 1.8 %collective-permute-start.5 = (bf16[2,128,512]{2,1,0:T(8,128)(2,1)S(1)}, bf16[2,128,512]{2,1,0:T(8,128)(2,1)S(1)}, u32[]{:S(2)}, u32[]{:S(2)}) collective-permute-start(bf16[2,128,512]{2,1,0:T(8,128)(2,1)S(1)} %get-tuple-element.32), channel_id=1, source_target_pairs={{0,1},{1,0},{2,3},{3,2},{4,5},{5,4},{6,7},{7,6},{8,9},{9,8},{10,11... | collective-permute-start | bytes 786440 | tf_op jit(solution)/shard_map/ppermute | solution.py:333
  47.0 2.6 %collective-permute-start.6 = (bf16[2,128,512]{2,1,0:T(8,128)(2,1)S(1)}, bf16[2,128,512]{2,1,0:T(8,128)(2,1)S(1)}, u32[]{:S(2)}, u32[]{:S(2)}) collective-permute-start(bf16[2,128,512]{2,1,0:T(8,128)(2,1)S(1)} %collective-permute-done.4.refs_1_), channel_id=1, source_target_pairs={{0,4},{4,8},{8,12},{12,16},{16,20},{20,24},{24,28},{1,5},{5,9},{9,... | collective-permute-start | bytes 786440 | tf_op jit(solution)/shard_map/ppermute | solution.py:381
  49.7 5.2 %conv_parts.4.refs_10_ = f32[4,128,512]{2,1,0:T(8,128)S(1)} custom-call(s32[12]{0:T(128)S(1)} %copy-done, bf16[4,128,512]{2,1,0:T(8,128)(2,1)S(1)} %collective-permute-done.10.refs_1_, bf16[4,128,512]{2,1,0:T(8,128)(2,1)S(1)} %collective-permute-done.3.refs_2_, bf16[3,27,16,128]{3,2,1,0:T(8,128)(2,1)S(1)} %pad_maximum_fusion.refs_3_.refs_2_, ...), custom_call_target="tpu_custom_call" | custom-call | flops 1024 | bytes 1024 | tf_op jit(solution)/shard_map/conv_parts/pallas_call | solution.py:168
  55.6 2.2 %last_part.2.far_ref = bf16[2,128,512]{2,1,0:T(8,128)(2,1)S(1)} custom-call(s32[12]{0:T(128)S(1)} %copy-done, bf16[6,384,512]{2,1,0:T(8,128)(2,1)S(1)} %shifted_frames.1.refs_1_, bf16[3,27,16,128]{3,2,1,0:T(8,128)(2,1)S(1)} %pad_maximum_fusion.refs_3_.refs_2_, bf16[3,27,16,128]{3,2,1,0:T(8,128)(2,1)S(1)} %collective-permute-done.11.refs_4_.refs_3_, ...), custom_call_target="tpu_custom_call" | custom-call | flops 1024 | bytes 1024 | tf_op jit(solution)/shard_map/last_part/pallas_call | solution.py:233
  57.8 4.4 %collective-permute-start.16 = (bf16[2,128,512]{2,1,0:T(8,128)(2,1)S(1)}, bf16[2,128,512]{2,1,0:T(8,128)(2,1)S(1)}, u32[]{:S(2)}, u32[]{:S(2)}) collective-permute-start(bf16[2,128,512]{2,1,0:T(8,128)(2,1)S(1)} %last_part.2.far_ref), channel_id=1, source_target_pairs={{4,8},{12,16},{20,24},{8,4},{16,12},{24,20},{5,9},{13,17},{21,25},... | collective-permute-start | bytes 786440 | tf_op jit(solution)/shard_map/ppermute | solution.py:391
  62.3 2.3 %last_part.3.near_ref = bf16[2,128,512]{2,1,0:T(8,128)(2,1)S(1)} custom-call(s32[12]{0:T(128)S(1)} %copy-done, bf16[6,384,512]{2,1,0:T(8,128)(2,1)S(1)} %shifted_frames.1.refs_1_, bf16[3,27,16,128]{3,2,1,0:T(8,128)(2,1)S(1)} %pad_maximum_fusion.refs_3_.refs_2_, bf16[3,27,16,128]{3,2,1,0:T(8,128)(2,1)S(1)} %collective-permute-done.11.refs_4_.refs_3_, ...), custom_call_target="tpu_custom_call" | custom-call | flops 1024 | bytes 1024 | tf_op jit(solution)/shard_map/last_part/pallas_call | solution.py:233
  64.6 4.5 %collective-permute-done.16.far_in_ref = bf16[2,128,512]{2,1,0:T(8,128)(2,1)S(1)} collective-permute-done((bf16[2,128,512]{2,1,0:T(8,128)(2,1)S(1)}, bf16[2,128,512]{2,1,0:T(8,128)(2,1)S(1)}, u32[]{:S(2)}, u32[]{:S(2)}) %collective-permute-start.16) | collective-permute-done | bytes 262176 | tf_op jit(solution)/shard_map/ppermute | solution.py:391
  69.8 1.9 %slots.1 = bf16[128,8,512]{2,1,0:T(8,128)(2,1)} custom-call(s32[1,2]{1,0:T(1,128)S(1)} %copy-done.3, bf16[8,128,512]{2,1,0:T(8,128)(2,1)S(1)} %window.1.window_ref, bf16[2,128,512]{2,1,0:T(8,128)(2,1)S(1)} %collective-permute-done.17.near_in_ref), custom_call_target="tpu_custom_call" | custom-call | tf_op jit(solution)/shard_map/slots/pallas_call | solution.py:318
  (33 shorter events, 3.4 us)
Async XLA Ops:
  0.0 19.6 %copy-start = (s32[12]{0:T(128)S(1)}, s32[12]{0:T(128)}, u32[]{:S(2)}) copy-start(s32[12]{0:T(128)} %refs_0_.9) | copy-start | bytes 148
  1.1 4.8 %collective-permute-start = (bf16[27,16,128]{2,1,0:T(8,128)(2,1)S(1)}, bf16[27,16,128]{2,1,0:T(8,128)(2,1)S(1)}, u32[]{:S(2)}, u32[]{:S(2)}) collective-permute-start(bf16[27,16,128]{2,1,0:T(8,128)(2,1)S(1)} %get-tuple-element.25), channel_id=1, source_target_pairs={{0,1},{1,0},{2,3},{3,2},{4,5},{5,4},{6,7},{7,6},{8,9},{9,8},{10,11... | collective-permute-start | bytes 331784 | tf_op jit(solution)/shard_map/ppermute | solution.py:333
  2.4 4.7 %collective-permute-start.1 = (bf16[27,16,128]{2,1,0:T(8,128)(2,1)S(1)}, bf16[27,16,128]{2,1,0:T(8,128)(2,1)S(1)}, u32[]{:S(2)}, u32[]{:S(2)}) collective-permute-start(bf16[27,16,128]{2,1,0:T(8,128)(2,1)S(1)} %get-tuple-element.28), channel_id=1, source_target_pairs={{0,2},{1,3},{2,0},{3,1},{4,6},{5,7},{6,4},{7,5},{8,10},{9,11},{10,... | collective-permute-start | bytes 331784 | tf_op jit(solution)/shard_map/ppermute | solution.py:333
  4.7 7.1 %collective-permute-start.2 = (bf16[27,16,128]{2,1,0:T(8,128)(2,1)S(1)}, bf16[27,16,128]{2,1,0:T(8,128)(2,1)S(1)}, u32[]{:S(2)}, u32[]{:S(2)}) collective-permute-start(bf16[27,16,128]{2,1,0:T(8,128)(2,1)S(1)} %get-tuple-element.29), channel_id=1, source_target_pairs={{0,3},{1,2},{2,1},{3,0},{4,7},{5,6},{6,5},{7,4},{8,11},{9,10},{10,... | collective-permute-start | bytes 331784 | tf_op jit(solution)/shard_map/ppermute | solution.py:333
  5.9 27.6 %collective-permute-start.10 = (bf16[4,128,512]{2,1,0:T(8,128)(2,1)S(1)}, bf16[4,128,512]{2,1,0:T(8,128)(2,1)S(1)}, u32[]{:S(2)}, u32[]{:S(2)}) collective-permute-start(bf16[4,128,512]{2,1,0:T(8,128)(2,1)S(1)} %bitcast.11), channel_id=1, source_target_pairs={{0,1},{1,0},{2,3},{3,2},{4,5},{5,4},{6,7},{7,6},{8,9},{9,8},{10,11... | collective-permute-start | bytes 1572872 | tf_op jit(solution)/shard_map/ppermute | solution.py:333
  11.9 25.7 %collective-permute-start.3 = (bf16[4,128,512]{2,1,0:T(8,128)(2,1)S(1)}, bf16[4,128,512]{2,1,0:T(8,128)(2,1)S(1)}, u32[]{:S(2)}, u32[]{:S(2)}) collective-permute-start(bf16[4,128,512]{2,1,0:T(8,128)(2,1)S(1)} %bitcast.12), channel_id=1, source_target_pairs={{0,2},{1,3},{2,0},{3,1},{4,6},{5,7},{6,4},{7,5},{8,10},{9,11},{10,... | collective-permute-start | bytes 1572872 | tf_op jit(solution)/shard_map/ppermute | solution.py:333
  15.8 8.4 %collective-permute-start.9 = (bf16[3,27,16,128]{3,2,1,0:T(8,128)(2,1)S(1)}, bf16[3,27,16,128]{3,2,1,0:T(8,128)(2,1)S(1)}, u32[]{:S(2)}, u32[]{:S(2)}) collective-permute-start(bf16[3,27,16,128]{3,2,1,0:T(8,128)(2,1)S(1)} %pad_maximum_fusion.refs_3_.refs_2_), channel_id=1, source_target_pairs={{0,24},{4,28},{8,16},{12,20},{16,8},{20,12},{24,0},{28,4},{1,25},{... | collective-permute-start | bytes 995336 | tf_op jit(solution)/shard_map/ppermute | solution.py:333
  17.0 16.5 %collective-permute-start.8 = (bf16[3,27,16,128]{3,2,1,0:T(8,128)(2,1)S(1)}, bf16[3,27,16,128]{3,2,1,0:T(8,128)(2,1)S(1)}, u32[]{:S(2)}, u32[]{:S(2)}) collective-permute-start(bf16[3,27,16,128]{3,2,1,0:T(8,128)(2,1)S(1)} %pad_maximum_fusion.refs_3_.refs_2_), channel_id=1, source_target_pairs={{0,16},{4,20},{8,24},{12,28},{16,0},{20,4},{24,8},{28,12},{1,17},{... | collective-permute-start | bytes 995336 | tf_op jit(solution)/shard_map/ppermute | solution.py:333
  17.2 16.3 %collective-permute-start.7 = (bf16[3,27,16,128]{3,2,1,0:T(8,128)(2,1)S(1)}, bf16[3,27,16,128]{3,2,1,0:T(8,128)(2,1)S(1)}, u32[]{:S(2)}, u32[]{:S(2)}) collective-permute-start(bf16[3,27,16,128]{3,2,1,0:T(8,128)(2,1)S(1)} %pad_maximum_fusion.refs_3_.refs_2_), channel_id=1, source_target_pairs={{0,8},{4,12},{8,0},{12,4},{16,24},{20,28},{24,16},{28,20},{1,9},{5... | collective-permute-start | bytes 995336 | tf_op jit(solution)/shard_map/ppermute | solution.py:333
  33.5 4.2 %collective-permute-start.11 = (bf16[3,27,16,128]{3,2,1,0:T(8,128)(2,1)S(1)}, bf16[3,27,16,128]{3,2,1,0:T(8,128)(2,1)S(1)}, u32[]{:S(2)}, u32[]{:S(2)}) collective-permute-start(bf16[3,27,16,128]{3,2,1,0:T(8,128)(2,1)S(1)} %pad_maximum_fusion.refs_3_.refs_2_), channel_id=1, source_target_pairs={{0,4},{4,0},{8,12},{12,8},{16,20},{20,16},{24,28},{28,24},{1,5},{5... | collective-permute-start | bytes 995336 | tf_op jit(solution)/shard_map/ppermute | solution.py:333
  34.1 3.6 %collective-permute-start.12 = (bf16[3,27,16,128]{3,2,1,0:T(8,128)(2,1)S(1)}, bf16[3,27,16,128]{3,2,1,0:T(8,128)(2,1)S(1)}, u32[]{:S(2)}, u32[]{:S(2)}) collective-permute-start(bf16[3,27,16,128]{3,2,1,0:T(8,128)(2,1)S(1)} %collective-permute-done.7.refs_5_.refs_4_), channel_id=1, source_target_pairs={{0,4},{4,0},{8,12},{12,8},{16,20},{20,16},{24,28},{28,24},{1,5},{5... | collective-permute-start | bytes 995336 | tf_op jit(solution)/shard_map/ppermute | solution.py:333
  34.1 3.6 %collective-permute-start.13 = (bf16[3,27,16,128]{3,2,1,0:T(8,128)(2,1)S(1)}, bf16[3,27,16,128]{3,2,1,0:T(8,128)(2,1)S(1)}, u32[]{:S(2)}, u32[]{:S(2)}) collective-permute-start(bf16[3,27,16,128]{3,2,1,0:T(8,128)(2,1)S(1)} %collective-permute-done.8.refs_7_.refs_6_), channel_id=1, source_target_pairs={{0,4},{4,0},{8,12},{12,8},{16,20},{20,16},{24,28},{28,24},{1,5},{5... | collective-permute-start | bytes 995336 | tf_op jit(solution)/shard_map/ppermute | solution.py:333
  34.6 3.1 %collective-permute-start.14 = (bf16[3,27,16,128]{3,2,1,0:T(8,128)(2,1)S(1)}, bf16[3,27,16,128]{3,2,1,0:T(8,128)(2,1)S(1)}, u32[]{:S(2)}, u32[]{:S(2)}) collective-permute-start(bf16[3,27,16,128]{3,2,1,0:T(8,128)(2,1)S(1)} %collective-permute-done.9.refs_9_.refs_8_), channel_id=1, source_target_pairs={{0,4},{4,0},{8,12},{12,8},{16,20},{20,16},{24,28},{28,24},{1,5},{5... | collective-permute-start | bytes 995336 | tf_op jit(solution)/shard_map/ppermute | solution.py:333
  37.6 7.6 %collective-permute-start.4 = (bf16[2,128,512]{2,1,0:T(8,128)(2,1)S(1)}, bf16[2,128,512]{2,1,0:T(8,128)(2,1)S(1)}, u32[]{:S(2)}, u32[]{:S(2)}) collective-permute-start(bf16[2,128,512]{2,1,0:T(8,128)(2,1)S(1)} %get-tuple-element.49), channel_id=1, source_target_pairs={{0,1},{1,0},{2,3},{3,2},{4,5},{5,4},{6,7},{7,6},{8,9},{9,8},{10,11... | collective-permute-start | bytes 786440 | tf_op jit(solution)/shard_map/ppermute | solution.py:333
  39.9 15.6 %collective-permute-start.15 = (f32[2,128,512]{2,1,0:T(8,128)S(1)}, f32[2,128,512]{2,1,0:T(8,128)S(1)}, u32[]{:S(2)}, u32[]{:S(2)}) collective-permute-start(f32[2,128,512]{2,1,0:T(8,128)S(1)} %conv_parts.5), channel_id=1, source_target_pairs={{0,4},{4,8},{8,12},{12,16},{16,20},{20,24},{24,28},{1,5},{5,9},{9,... | collective-permute-start | bytes 1572872 | tf_op jit(solution)/shard_map/ppermute | solution.py:380
  45.2 9.7 %collective-permute-start.5 = (bf16[2,128,512]{2,1,0:T(8,128)(2,1)S(1)}, bf16[2,128,512]{2,1,0:T(8,128)(2,1)S(1)}, u32[]{:S(2)}, u32[]{:S(2)}) collective-permute-start(bf16[2,128,512]{2,1,0:T(8,128)(2,1)S(1)} %get-tuple-element.32), channel_id=1, source_target_pairs={{0,1},{1,0},{2,3},{3,2},{4,5},{5,4},{6,7},{7,6},{8,9},{9,8},{10,11... | collective-permute-start | bytes 786440 | tf_op jit(solution)/shard_map/ppermute | solution.py:333
  47.0 7.9 %collective-permute-start.6 = (bf16[2,128,512]{2,1,0:T(8,128)(2,1)S(1)}, bf16[2,128,512]{2,1,0:T(8,128)(2,1)S(1)}, u32[]{:S(2)}, u32[]{:S(2)}) collective-permute-start(bf16[2,128,512]{2,1,0:T(8,128)(2,1)S(1)} %collective-permute-done.4.refs_1_), channel_id=1, source_target_pairs={{0,4},{4,8},{8,12},{12,16},{16,20},{20,24},{24,28},{1,5},{5,9},{9,... | collective-permute-start | bytes 786440 | tf_op jit(solution)/shard_map/ppermute | solution.py:381
  54.9 0.7 copy-start.1
  54.9 0.7 copy-start.2
  57.8 11.3 %copy-start.3 = (s32[1,2]{1,0:T(1,128)S(1)}, s32[1,2]{1,0:T(1,128)}, u32[]{:S(2)}) copy-start(s32[1,2]{1,0:T(1,128)} %bounds_ref.3) | copy-start | bytes 28
  57.8 11.3 %collective-permute-start.16 = (bf16[2,128,512]{2,1,0:T(8,128)(2,1)S(1)}, bf16[2,128,512]{2,1,0:T(8,128)(2,1)S(1)}, u32[]{:S(2)}, u32[]{:S(2)}) collective-permute-start(bf16[2,128,512]{2,1,0:T(8,128)(2,1)S(1)} %last_part.2.far_ref), channel_id=1, source_target_pairs={{4,8},{12,16},{20,24},{8,4},{16,12},{24,20},{5,9},{13,17},{21,25},... | collective-permute-start | bytes 786440 | tf_op jit(solution)/shard_map/ppermute | solution.py:391
  64.5 5.3 %collective-permute-start.17 = (bf16[2,128,512]{2,1,0:T(8,128)(2,1)S(1)}, bf16[2,128,512]{2,1,0:T(8,128)(2,1)S(1)}, u32[]{:S(2)}, u32[]{:S(2)}) collective-permute-start(bf16[2,128,512]{2,1,0:T(8,128)(2,1)S(1)} %last_part.3.near_ref), channel_id=1, source_target_pairs={{0,4},{8,12},{16,20},{24,28},{4,0},{12,8},{20,16},{28,24},{1,5},{9... | collective-permute-start | bytes 786440 | tf_op jit(solution)/shard_map/ppermute | solution.py:394
